TPU v7x, 256 devices: a whole 4x4x8 slice. The times are simulated.
256 devices in a mesh: ens: 4 (over x_hi, core), date: 8 (over z), pix: 8 (over y, x_lo).
Axes of the slice: x: 4 (x_hi: 2, x_lo: 2; x = x_hi * 2 + x_lo), y: 4, z: 8, core: 2. Of those that a mesh axis runs over, the one named last changes fastest.
Arguments:
- hindcast_runs: bfloat16 [4, 104, 4, 46, 8192], P('ens', 'date', None, None, 'pix'), may hold values from -16 to 16
- init_calendar_ordinal: int32 [104], replicated, may hold values from 0 to 367, as said below
- prediction_init_position: int32 [1], replicated, may hold values from 0 to 103
- horizon_sevenfold_bin: int32 [46], replicated, may hold values from 0 to 6, never falling along the last dimension, each value on 1 to 8 neighbouring positions
- prediction_runs: bfloat16 [11, 4, 46, 8192], P(None, 'ens', None, ('pix', 'date')), may hold values from -16 to 16
Outputs:
- smoothed_norm: float32 [104, 4, 46, 8192], P('date', 'ens', None, 'pix')
- anomalies: float32 [7, 4, 8192], P(None, 'ens', ('pix', 'date'))
Inputs may be any that keep to these rules, and one draw needn't show every extreme that they name: `init_calendar_ordinal`: strictly increasing; the first is a day of 0 to 6, consecutive start dates lie 3 or 4 days apart, the last lies 3 or 4 days before the first plus 364, and half of these 104 gaps are 4 days. `horizon_sevenfold_bin`: Non-decreasing; every bin of 0 to 6 holds 1 to 8 consecutive leads.
All inputs are finite; a program needn't handle non-finite values.
Results may differ from a plain program's by a relative error of at most 0.01.
Values may be sent and summed in bfloat16 or wider, within the bound.
No kernel may reach another device: no remote copies, remote signals or barrier semaphores. Data moves between devices by JAX's collectives and lax.ppermute only.
A program may use at most 128 MiB of HBM per device.

v0:
```python
import jax
import jax.numpy as jnp
from jax import lax
from jax.sharding import PartitionSpec as P

WEEKS = 7


def gap_weight(earlier, later, cycle_days):
    gap_days = jnp.mod(later - earlier, cycle_days)
    return jnp.maximum(8 - gap_days, 0).astype(jnp.float32)


def expand(weight):
    return weight[:, None, None, None]


def date_smooth(center, center_days, forward, backward, members_total, cycle_days):
    date_mean = 8.0 * center
    weight_sum = jnp.full(center_days.shape, 8.0, jnp.float32)
    for day_list, neighbour in forward:
        weight = gap_weight(center_days, day_list, cycle_days)
        date_mean = date_mean + expand(weight) * neighbour
        weight_sum = weight_sum + weight
    for day_list, neighbour in backward:
        weight = gap_weight(day_list, center_days, cycle_days)
        date_mean = date_mean + expand(weight) * neighbour
        weight_sum = weight_sum + weight
    return date_mean / expand(members_total * weight_sum)


def smooth_leads(date_mean):
    length = date_mean.shape[2]
    padded = jnp.pad(date_mean, ((0, 0), (0, 0), (1, 1), (0, 0)))
    total = 2.0 * date_mean + padded[:, :, :-2] + padded[:, :, 2:]
    positions = jnp.arange(length)
    row_weight = (
        4.0 - (positions == 0).astype(jnp.float32) - (positions == length - 1).astype(jnp.float32)
    )
    return total / row_weight[None, None, :, None]


def per_device(
    hindcast_runs,
    init_calendar_ordinal,
    prediction_init_position,
    horizon_sevenfold_bin,
    prediction_runs,
):
    highest = lax.Precision.HIGHEST
    members_total = hindcast_runs.shape[0] * lax.axis_size("ens")
    date_count = hindcast_runs.shape[1] * lax.axis_size("date")
    cycle_days = 7 * date_count // 2
    week_table = (
        horizon_sevenfold_bin[None, :] == jnp.arange(WEEKS, dtype=jnp.int32)[:, None]
    ).astype(jnp.float32)
    bin_count = jnp.sum(week_table, 1)
    runs_centroid = jnp.sum(prediction_runs, 0, dtype=jnp.float32) / prediction_runs.shape[0]
    owned_rows = lax.all_to_all(
        lax.all_to_all(hindcast_runs, "ens", split_axis=2, concat_axis=0, tiled=True),
        "date",
        split_axis=4,
        concat_axis=1,
        tiled=True,
    )
    member_sum = jnp.sum(owned_rows, 0, dtype=jnp.float32)
    own_rows = member_sum.shape[0]
    widened = jnp.concatenate([member_sum[own_rows - 2 :], member_sum, member_sum[:2]], 0)
    ext_days = jnp.concatenate(
        [init_calendar_ordinal[own_rows - 2 :], init_calendar_ordinal, init_calendar_ordinal[:2]], 0
    )
    forward = [
        (ext_days[2 + offset : 2 + offset + own_rows], widened[2 + offset : 2 + offset + own_rows])
        for offset in (1, 2)
    ]
    backward = [
        (ext_days[2 - offset : 2 - offset + own_rows], widened[2 - offset : 2 - offset + own_rows])
        for offset in (1, 2)
    ]
    per_cell = smooth_leads(
        date_smooth(member_sum, init_calendar_ordinal, forward, backward, members_total, cycle_days)
    )
    present_norm = lax.dynamic_index_in_dim(
        per_cell, prediction_init_position[0], 0, keepdims=False
    )
    anomalies = jnp.einsum(
        "wl,vlp->wvp", week_table, runs_centroid - present_norm, precision=highest
    )
    anomalies = anomalies / bin_count[:, None, None]
    smoothed_norm = lax.all_to_all(per_cell, "date", split_axis=0, concat_axis=3, tiled=True)
    return (smoothed_norm, anomalies)


def solution(mesh):
    return jax.shard_map(
        per_device,
        mesh=mesh,
        in_specs=(
            P("ens", "date", None, None, "pix"),
            P(),
            P(),
            P(),
            P(None, "ens", None, ("pix", "date")),
        ),
        out_specs=(P("date", "ens", None, "pix"), P(None, "ens", ("pix", "date"))),
        check_vma=False,
    )
```

profile of v0, /device:TPU:8, one launch (start us, length us, event | category | flops | bytes accessed | tf_op | source)
XLA Modules:
  0.0 398.3 jit_solution(11428826734583218224)
XLA Ops:
  0.6 4.0 %copy.34 = bf16[1,13,4,46,1024]{4,3,1,0,2:T(8,128)(2,1)S(1)} copy(bf16[1,13,4,46,1024]{4,2,3,1,0:T(4,128)(2,1)} %param.5) | data formatting | bytes 9797632 | tf_op args[0]
  4.7 63.7 %all_to_all.45 = bf16[1,13,4,46,1024]{4,3,1,0,2:T(8,128)(2,1)} all-to-all(bf16[1,13,4,46,1024]{4,3,1,0,2:T(8,128)(2,1)S(1)} %copy.34), channel_id=1, replica_groups=mesh['ens'=4,'date'=8,'pix'=8] {'ens'}, dimensions={2} | all-to-all | bytes 9797632 | tf_op jit(solution)/shard_map/all_to_all | solution.py:60
  68.4 19.2 %copy.35 = bf16[4,13,1,46,1024]{3,0,2,1,4:T(4,128)(2,1)} copy(bf16[4,13,1,46,1024]{4,3,1,0,2:T(8,128)(2,1)} %bitcast.28) | data formatting | bytes 9797632 | tf_op jit(solution)/shard_map/all_to_all | solution.py:60
  87.6 33.1 %reshape.66 = bf16[8,2,153088]{2,1,0:T(2,128)(2,1)} reshape(bf16[1024,13,1,4,46]{4,3,2,1,0:T(4,128)(2,1)} %bitcast.25) | data formatting | bytes 9797632
  120.7 0.0 copy-start.1
  120.7 8.6 %all-to-all-start.1 = ((bf16[8,2,153088]{2,1,0:T(2,128)(2,1)}), bf16[8,2,153088]{2,1,0:T(2,128)(2,1)}, u32[]{:S(2)}, u32[]{:S(2)}) async-start(bf16[8,2,153088]{2,1,0:T(2,128)(2,1)} %reshape.66), calls=%async_computation.1 | async-start | bytes 9797632 | tf_op jit(solution)/shard_map/all_to_all | solution.py:59
  129.3 0.0 copy-done.1
  129.3 0.1 fusion.37
  129.4 0.1 pad_add_fusion.1
  129.5 0.1 add_multiply_fusion
  129.6 110.9 %all-to-all-done.1 = bf16[8,2,153088]{2,1,0:T(2,128)(2,1)} async-done(((bf16[8,2,153088]{2,1,0:T(2,128)(2,1)}), bf16[8,2,153088]{2,1,0:T(2,128)(2,1)}, u32[]{:S(2)}, u32[]{:S(2)}) %all-to-all-start.1) | async-done | bytes 4898848 | tf_op jit(solution)/shard_map/all_to_all | solution.py:59
  240.5 41.4 %reshape.67 = bf16[1024,13,1,4,46]{4,3,2,1,0:T(4,128)(2,1)} reshape(bf16[8,2,153088]{2,1,0:T(2,128)(2,1)} %all-to-all-done.1) | data formatting | bytes 9797632
  281.8 21.4 %copy.36 = bf16[4,13,1,46,1024]{4,0,3,2,1:T(4,128)(2,1)} copy(bf16[4,13,1,46,1024]{3,0,2,1,4:T(4,128)(2,1)} %bitcast.26) | data formatting | bytes 9797632 | tf_op jit(solution)/shard_map/all_to_all | solution.py:59
  303.3 8.7 %convert_reduce_fusion = f32[13,46,1024]{2,1,0:T(8,128)S(1)} fusion(bf16[4,13,1,46,1024]{4,0,3,2,1:T(4,128)(2,1)} %copy.36), kind=kLoop, calls=%fused_computation | loop fusion | flops 4286464 | bytes 7348224 | tf_op jit(solution)/shard_map/reduce_sum | solution.py:66
  312.0 6.3 %copy.46 = f32[13,46,1024]{1,0,2:T(8,128)} copy(f32[13,46,1024]{2,1,0:T(8,128)S(1)} %convert_reduce_fusion) | data formatting | bytes 4898816
  318.3 5.3 %copy.39 = f32[8,13,46,128]{3,2,1,0:T(8,128)S(1)} copy(f32[8,13,46,128]{2,1,3,0:T(8,128)} %bitcast.27) | data formatting | bytes 4898816 | tf_op jit(solution)/shard_map/reduce_sum | solution.py:66
  323.6 2.2 fusion.4
  325.8 0.7 add_divide_fusion
  326.5 4.0 copy.40
  330.5 0.0 copy-start.2
  330.5 0.0 copy-start
  330.5 4.5 %all-to-all-start.2 = ((f32[104,1,46,128]{3,1,2,0:T(1,128)}), f32[104,1,46,128]{3,1,2,0:T(1,128)}, u32[]{:S(2)}, u32[]{:S(2)}) async-start(f32[104,1,46,128]{3,1,2,0:T(1,128)} %copy.40), calls=%async_computation.2 | async-start | bytes 4898816 | tf_op jit(solution)/shard_map/all_to_all | solution.py:90
  335.6 0.0 copy-done.2
  335.6 0.1 convert_reduce_fusion.2
  335.8 0.0 copy-done
  335.8 0.1 fusion.11
  335.9 0.6 copy.42
  336.5 57.7 %all-to-all-done.2 = f32[104,1,46,128]{3,1,2,0:T(1,128)} async-done(((f32[104,1,46,128]{3,1,2,0:T(1,128)}), f32[104,1,46,128]{3,1,2,0:T(1,128)}, u32[]{:S(2)}, u32[]{:S(2)}) %all-to-all-start.2) | async-done | bytes 2449440 | tf_op jit(solution)/shard_map/all_to_all | solution.py:90
  394.2 1.9 copy.45
  396.1 2.2 copy.41
  (3 shorter events, 0.0 us)
Async XLA Ops:
  120.7 8.6 %copy-start.1 = (s32[104]{0:T(128)S(1)}, s32[104]{0:T(128)}, u32[]{:S(2)}) copy-start(s32[104]{0:T(128)} %param.6) | copy-start | bytes 1252
  120.7 119.8 %all-to-all-start.1 = ((bf16[8,2,153088]{2,1,0:T(2,128)(2,1)}), bf16[8,2,153088]{2,1,0:T(2,128)(2,1)}, u32[]{:S(2)}, u32[]{:S(2)}) async-start(bf16[8,2,153088]{2,1,0:T(2,128)(2,1)} %reshape.66), calls=%async_computation.1 | async-start | bytes 9797632 | tf_op jit(solution)/shard_map/all_to_all | solution.py:59
  330.5 5.2 %copy-start.2 = (s32[46]{0:T(128)S(1)}, s32[46]{0:T(128)}, u32[]{:S(2)}) copy-start(s32[46]{0:T(128)} %param.8) | copy-start | bytes 556
  330.5 5.3 %copy-start = (bf16[11,1,46,128]{3,2,1,0:T(8,128)(2,1)S(1)}, bf16[11,1,46,128]{3,2,1,0:T(8,128)(2,1)}, u32[]{:S(2)}) copy-start(bf16[11,1,46,128]{3,2,1,0:T(8,128)(2,1)} %param.9) | copy-start | bytes 388612
  330.5 63.8 %all-to-all-start.2 = ((f32[104,1,46,128]{3,1,2,0:T(1,128)}), f32[104,1,46,128]{3,1,2,0:T(1,128)}, u32[]{:S(2)}, u32[]{:S(2)}) async-start(f32[104,1,46,128]{3,1,2,0:T(1,128)} %copy.40), calls=%async_computation.2 | async-start | bytes 4898816 | tf_op jit(solution)/shard_map/all_to_all | solution.py:90
where the time goes:
time: 401 us; the launch traced here: 398 us
  waiting for transfers between devices  169 us (42%)
  local copies, waits for them, and re-layouts  139 us (35%)
  blocking collectives  63.7 us (16%)
  starting transfers between devices  13.1 us (3%)
  other arithmetic  11.9 us (3%)
    all_to_all x1, waiting for transfers between devices, per_device(): lax.all_to_all(lax.all_to_all(hindcast_runs, 'ens', split_axis=2, concat_...  111 us
    unnamed x12, local copies, waits for them, and re-layouts  87.3 us
    all_to_all x1, blocking collectives, per_device(): lax.all_to_all(hindcast_runs, 'ens', split_axis=2, concat_axis=0, tiled=T...  63.7 us
    all_to_all x1, waiting for transfers between devices, per_device(): lax.all_to_all(per_cell, 'date', split_axis=0, concat_axis=3, tiled=True)  57.7 us
    all_to_all x1, local copies, waits for them, and re-layouts, per_device(): lax.all_to_all(lax.all_to_all(hindcast_runs, 'ens', split_axis=2, concat_...  21.4 us
    all_to_all x1, local copies, waits for them, and re-layouts, per_device(): lax.all_to_all(hindcast_runs, 'ens', split_axis=2, concat_axis=0, tiled=T...  19.2 us
    reduce_sum x1, other arithmetic, per_device(): member_sum = jnp.sum(owned_rows, 0, dtype=jnp.float32)  8.7 us
    all_to_all x1, starting transfers between devices, per_device(): lax.all_to_all(lax.all_to_all(hindcast_runs, 'ens', split_axis=2, concat_...  8.6 us
  transfers between devices with their start and end apart: 2, of which 2 were waited for; matrix products, arithmetic and copies ran while one was open for 0% of the time, Pallas kernels for 0%

commit v1 on v0

v1 whole, which is shorter than its diff:
```python
import jax
import jax.numpy as jnp
from jax import lax
from jax.sharding import PartitionSpec as P

WEEKS = 7
SCALE = 512.0


def core_swap(block):
    return lax.ppermute(block, "ens", [(0, 1), (1, 0), (2, 3), (3, 2)])


def chip_swap(block):
    return lax.ppermute(block, "ens", [(0, 2), (1, 3), (2, 0), (3, 1)])


def date_shift(block, step):
    count = lax.axis_size("date")
    return lax.ppermute(block, "date", [(i, (i + step) % count) for i in range(count)])


def date_weights(days, cycle_days):
    columns = []
    for k in (-2, -1, 0, 1, 2):
        if k == 0:
            columns.append(jnp.full(days.shape, 8.0, jnp.float32))
            continue
        other = jnp.roll(days, -k)
        gap = jnp.mod(other - days if k > 0 else days - other, cycle_days)
        columns.append(jnp.maximum(8 - gap, 0).astype(jnp.float32))
    table = jnp.stack(columns, 1)
    return table / jnp.sum(table, 1, keepdims=True)


def smooth_leads(field, axis):
    length = field.shape[axis]
    shape = [1] * field.ndim
    shape[axis] = length
    positions = jnp.arange(length).reshape(shape)
    pads = [(0, 0)] * field.ndim
    pads[axis] = (1, 1)
    padded = jnp.pad(field, pads)
    before = lax.slice_in_dim(padded, 0, length, axis=axis)
    after = lax.slice_in_dim(padded, 2, length + 2, axis=axis)
    inverse = jnp.where((positions == 0) | (positions == length - 1), 1.0 / 3.0, 0.25)
    return (2.0 * field + before + after) * inverse.astype(jnp.float32)


def per_device(
    hindcast_runs,
    init_calendar_ordinal,
    prediction_init_position,
    horizon_sevenfold_bin,
    prediction_runs,
):
    runs = hindcast_runs[0]
    rows, kinds, leads, cells = runs.shape
    dates = rows * lax.axis_size("date")
    members = lax.axis_size("ens")
    cycle_days = 7 * dates // 2
    ens = lax.axis_index("ens")
    date = lax.axis_index("date")
    core = ens % 2
    half = ens // 2

    def of_kind(block, kind):
        return lax.dynamic_index_in_dim(block, kind, 1, keepdims=False)

    edge = [(0, 2), (rows - 2, rows)]
    inner = [(2, rows - 2)]

    def part(kind, spans):
        pieces = [of_kind(runs[a:b], kind) for a, b in spans]
        return pieces[0] if len(pieces) == 1 else jnp.concatenate(pieces, 0)

    def member_sum(spans):
        for_sibling = core_swap(part(2 * (1 - half) + 1 - core, spans))
        partial = part(2 * (1 - half) + core, spans).astype(jnp.float32) + for_sibling.astype(
            jnp.float32
        )
        arrived = chip_swap((partial * SCALE).astype(jnp.float16))
        from_sibling = core_swap(part(2 * half + 1 - core, spans))
        own = part(ens, spans).astype(jnp.float32) + from_sibling.astype(jnp.float32)
        return own + arrived.astype(jnp.float32) * (1.0 / SCALE)

    edges = member_sum(edge)
    middle = member_sum(inner)
    packed = (edges * SCALE).astype(jnp.float16)
    below = date_shift(packed[2:], 1).astype(jnp.float32) * (1.0 / SCALE)
    above = date_shift(packed[:2], -1).astype(jnp.float32) * (1.0 / SCALE)
    widened = jnp.concatenate([below, edges[:2], middle, edges[2:], above], 0)

    weights = date_weights(init_calendar_ordinal, cycle_days)
    own_weights = lax.dynamic_slice_in_dim(weights, date * rows, rows, 0) * (1.0 / members)
    mean = own_weights[:, 0, None, None] * widened[:rows]
    for k in range(1, 5):
        mean = mean + own_weights[:, k, None, None] * widened[k : k + rows]
    smoothed_norm = smooth_leads(mean, 1)[:, None]

    position = prediction_init_position[0]
    row_weights = lax.dynamic_index_in_dim(weights, position, 0, keepdims=False) * (1.0 / members)
    own_dates = date * rows + jnp.arange(rows)
    offsets = jnp.mod(own_dates - position + 2, dates)
    shares = jnp.sum(
        jnp.where(offsets[:, None] == jnp.arange(5)[None, :], row_weights[None, :], 0.0), 1
    )
    week_table = (
        horizon_sevenfold_bin[None, :] == jnp.arange(WEEKS, dtype=jnp.int32)[:, None]
    ).astype(jnp.float32)
    week_mean = week_table / jnp.sum(week_table, 1, keepdims=True)
    climate = jnp.sum(runs.astype(jnp.float32) * shares[:, None, None, None], 0)
    climate = smooth_leads(climate, 1)
    highest = lax.Precision.HIGHEST
    weekly = jnp.einsum("wl,vlp->vwp", week_mean, climate, precision=highest)
    slots = lax.axis_size("date")
    weekly = weekly.reshape(kinds, WEEKS, slots, cells // slots).transpose(0, 2, 1, 3)
    weekly = weekly.reshape(kinds * slots, WEEKS, cells // slots)
    weekly = lax.psum_scatter(weekly, ("ens", "date"), scatter_dimension=0)
    centroid = jnp.sum(prediction_runs[:, 0].astype(jnp.float32), 0) * (
        1.0 / prediction_runs.shape[0]
    )
    anomalies = jnp.einsum("wl,lp->wp", week_mean, centroid, precision=highest) - weekly
    return smoothed_norm, anomalies[:, None]


def solution(mesh):
    return jax.shard_map(
        per_device,
        mesh=mesh,
        in_specs=(
            P("ens", "date", None, None, "pix"),
            P(),
            P(),
            P(),
            P(None, "ens", None, ("pix", "date")),
        ),
        out_specs=(P("date", "ens", None, "pix"), P(None, "ens", ("pix", "date"))),
        check_vma=False,
    )
```

time: 401 us -> 327 us (0.82)
  local copies, waits for them, and re-layouts: 139 us -> 25.4 us
  waiting for transfers between devices: 169 us -> 259 us
  blocking collectives: 63.7 us -> 0 us
  between operations: 1.37 us -> 15 us
  starting transfers between devices: 13.1 us -> 7.07 us
  other arithmetic: 11.9 us -> 17.8 us
    unnamed x0 -> x2, waiting for transfers between devices: none -> 240 us
    all_to_all x2 -> x0, waiting for transfers between devices: 169 us -> none  [the longest x1 111 us: per_device(): lax.all_to_all(lax.all_to_all(hindcast_runs, 'ens', split_axis=2, concat_...]
    unnamed x12 -> x22, local copies, waits for them, and re-layouts: 87.3 us -> 5.55 us
    all_to_all x1 -> x0, blocking collectives: 63.7 us -> none  [per_device(): lax.all_to_all(hindcast_runs, 'ens', split_axis=2, concat_axis=0, tiled=T...]
    all_to_all x3 -> x0, local copies, waits for them, and re-layouts: 42.9 us -> none  [the longest x1 21.4 us: per_device(): lax.all_to_all(lax.all_to_all(hindcast_runs, 'ens', split_axis=2, concat_...]
    ppermute x0 -> x8, waiting for transfers between devices: none -> 18.8 us  [the longest x2 12.5 us: chip_swap(): return lax.ppermute(block, 'ens', [(0, 2), (1, 3), (2, 0), (3, 1)])]
    all_to_all x2 -> x0, starting transfers between devices: 13.1 us -> none  [the longest x1 8.6 us: per_device(): lax.all_to_all(lax.all_to_all(hindcast_runs, 'ens', split_axis=2, concat_...]
    dynamic_slice x0 -> x2, local copies, waits for them, and re-layouts: none -> 11.2 us  [of_kind(): return lax.dynamic_index_in_dim(block, kind, 1, keepdims=False)]
  transfers between devices with their start and end apart: 2 -> 9, of which waited for: 2 -> 4; matrix products, arithmetic and copies ran while one was open for 0% -> 9% of each run, Pallas kernels for 0% -> 0%
where the time goes in v1:
time: 327 us
  waiting for transfers between devices  259 us (79%)
  local copies, waits for them, and re-layouts  25.4 us (8%)
  other arithmetic  17.8 us (5%)
  between operations  15 us (5%)
  starting transfers between devices  7.07 us (2%)
    unnamed x2, waiting for transfers between devices  240 us
    ppermute x2, waiting for transfers between devices, chip_swap(): return lax.ppermute(block, 'ens', [(0, 2), (1, 3), (2, 0), (3, 1)])  12.5 us
    dynamic_slice x2, local copies, waits for them, and re-layouts, of_kind(): return lax.dynamic_index_in_dim(block, kind, 1, keepdims=False)  11.2 us
  transfers between devices with their start and end apart: 9, of which 4 were waited for; matrix products, arithmetic and copies ran while one was open for 9% of the time, Pallas kernels for 0%

profile of v1, /device:TPU:8, one launch (start us, length us, event | category | flops | bytes accessed | tf_op | source)
XLA Modules:
  0.0 326.8 jit_solution(12621868161428565047)
XLA Ops:
  7.3 1.9 slice-done
  9.2 8.0 %constant_dynamic-slice_fusion.3 = (bf16[1,9,1,46,1024]{4,2,3,1,0:T(2,128)(2,1)}, bf16[1,9,1,46,1024]{4,2,3,1,0:T(2,128)(2,1)}, bf16[1,9,1,46,1024]{4,2,3,1,0:T(2,128)(2,1)S(1)}, bf16[1,9,1,46,1024]{4,2,3,1,0:T(2,128)(2,1)S(1)}) fusion(bf16[1,9,4,46,1024]{4,2,3,1,0:T(4,128)(2,1)S(1)} %slice-done, s32[]{:T(128)S(6)} %select_n.89, s32[]{:T(128)S(6)} %select_n.93, ...), kind=kLoop, calls=%fused_computation.63 | loop fusion | bytes 6782992 | tf_op jit(solution)/shard_map/jit(dynamic_index_in_dim)/dynamic_slice | solution.py:68
  17.2 1.2 copy.65
  18.5 1.2 copy.66
  19.7 0.5 collective-permute-start.4
  20.2 1.9 fusion.40
  22.1 3.1 constant_dynamic-slice_fusion.10
  25.3 0.1 copy.71
  25.4 0.8 pad_maximum_fusion.6
  26.3 0.8 pad_maximum_fusion.7
  27.1 0.5 collective-permute-start.1
  27.6 0.1 fusion.43
  27.7 0.1 fusion.44
  27.8 0.6 fusion.45
  28.4 0.1 fusion.46
  29.1 1.3 add_add_fusion
  30.5 0.2 multiply_reduce_fusion
  30.7 0.1 select_reduce_fusion
  30.8 5.3 %fusion = f32[4,46,1024]{2,0,1:T(4,128)S(1)} fusion(bf16[1,13,4,46,1024]{4,2,3,1,0:T(4,128)(2,1)} %param.5, f32[13]{0:T(128)S(1)} %select_reduce_fusion), kind=kLoop, calls=%fused_computation.1 | loop fusion | flops 7159808 | bytes 5652532 | tf_op jit(solution)/shard_map/reduce_sum | solution.py:112
  36.1 0.2 add_multiply_fusion.1
  36.3 0.1 convert_reduce_fusion.1
  36.4 1.0 convolution_bitcast_fusion
  37.5 0.7 copy.28
  38.3 0.7 copy.69
  39.0 0.8 copy.70
  39.8 0.1 copy.74
  39.9 0.6 dynamic-slice.12
  40.5 0.1 dynamic-slice_multiply_fusion
  40.6 2.0 multiply_convert_fusion.1
  42.6 3.0 collective-permute-start.2
  45.7 0.9 convert_reduce_fusion
  46.6 240.1 %all-reduce.5.cloned.1.call-done = f32[32,7,128]{2,1,0:T(8,128)} async-done(((f32[32,7,128]{2,1,0:T(8,128)}), f32[32,7,128]{2,1,0:T(8,128)}) %all-reduce.5.cloned.1.call-update) | async-done | bytes 114704
  286.7 1.5 fusion.10
  288.3 0.6 copy.29
  288.9 1.4 multiply_convert_fusion
  290.2 1.8 fusion.8
  292.0 0.9 collective-permute-start.6
  292.9 0.1 fusion.42
  293.0 0.1 collective-permute-start.7
  293.1 2.0 collective-permute-start.3
  295.1 0.1 fusion.41
  295.1 3.6 %collective-permute-done.7 = f16[2,46,1024]{2,1,0:T(8,128)(2,1)S(1)} collective-permute-done((f16[2,46,1024]{2,1,0:T(8,128)(2,1)S(1)}, f16[2,46,1024]{2,1,0:T(8,128)(2,1)S(1)}, u32[]{:S(2)}, u32[]{:S(2)}) %collective-permute-start.7) | collective-permute-done | bytes 188448 | tf_op jit(solution)/shard_map/ppermute | solution.py:20
  298.8 2.7 collective-permute-done.3
  301.5 12.5 %collective-permute-done.6 = f16[9,46,1024]{2,1,0:T(8,128)(2,1)S(1)} collective-permute-done((f16[9,46,1024]{2,1,0:T(8,128)(2,1)S(1)}, f16[9,46,1024]{2,1,0:T(8,128)(2,1)S(1)}, u32[]{:S(2)}, u32[]{:S(2)}) %collective-permute-start.6) | collective-permute-done | bytes 847904 | tf_op jit(solution)/shard_map/ppermute | solution.py:15
  314.0 0.7 fusion.9
  314.7 1.4 fusion.3
  316.1 0.7 add_multiply_fusion
  316.8 3.1 broadcast_in_dim.40
  (34 shorter events, 0.5 us)
Async XLA Ops:
  7.2 279.6 %all-reduce.5.cloned.1.call-start = ((), (), s32[]{:S(2)}) async-start(), calls=%async_computation | async-start | bytes 262144
  7.2 2.0 slice-start
  18.5 271.7 %collective-permute-start.5 = (bf16[9,46,1024]{2,1,0:T(8,128)(2,1)}, bf16[9,46,1024]{2,1,0:T(8,128)(2,1)}, u32[]{:S(2)}, u32[]{:S(2)}) collective-permute-start(bf16[9,46,1024]{2,1,0:T(8,128)(2,1)} %bitcast.64), channel_id=1, source_target_pairs={{0,64},{64,0},{128,192},{192,128},{1,65},{65,1},{129,193},{193,129... | collective-permute-start | bytes 2543624 | tf_op jit(solution)/shard_map/ppermute | solution.py:11
  19.7 281.8 %collective-permute-start.4 = (bf16[9,46,1024]{2,1,0:T(8,128)(2,1)}, bf16[9,46,1024]{2,1,0:T(8,128)(2,1)S(1)}, u32[]{:S(2)}, u32[]{:S(2)}) collective-permute-start(bf16[9,46,1024]{2,1,0:T(8,128)(2,1)} %bitcast.65), channel_id=1, source_target_pairs={{0,64},{64,0},{128,192},{192,128},{1,65},{65,1},{129,193},{193,129... | collective-permute-start | bytes 2543624 | tf_op jit(solution)/shard_map/ppermute | solution.py:11
  25.2 2.4 copy-start.2
  26.2 262.7 %collective-permute-start = (bf16[4,46,1024]{2,1,0:T(8,128)(2,1)}, bf16[4,46,1024]{2,1,0:T(8,128)(2,1)}, u32[]{:S(2)}, u32[]{:S(2)}) collective-permute-start(bf16[4,46,1024]{2,1,0:T(8,128)(2,1)} %pad_maximum_fusion.6), channel_id=1, source_target_pairs={{0,64},{64,0},{128,192},{192,128},{1,65},{65,1},{129,193},{193,129... | collective-permute-start | bytes 1130504 | tf_op jit(solution)/shard_map/ppermute | solution.py:11
  27.1 13.5 %collective-permute-start.1 = (bf16[4,46,1024]{2,1,0:T(8,128)(2,1)}, bf16[4,46,1024]{2,1,0:T(8,128)(2,1)}, u32[]{:S(2)}, u32[]{:S(2)}) collective-permute-start(bf16[4,46,1024]{2,1,0:T(8,128)(2,1)} %pad_maximum_fusion.7), channel_id=1, source_target_pairs={{0,64},{64,0},{128,192},{192,128},{1,65},{65,1},{129,193},{193,129... | collective-permute-start | bytes 1130504 | tf_op jit(solution)/shard_map/ppermute | solution.py:11
  30.8 5.6 %copy-start.3 = (s32[46]{0:T(128)S(1)}, s32[46]{0:T(128)}, u32[]{:S(2)}) copy-start(s32[46]{0:T(128)} %param.8) | copy-start | bytes 556
  36.1 3.9 %copy-start.4 = (u32[256]{0:T(256)S(1)}, u32[256]{0:T(256)}, u32[]{:S(2)}) copy-start(u32[256]{0:T(256)} %constant.152) | copy-start | bytes 3076
  39.8 250.5 %copy-start.1 = (bf16[1,9,1,46,1024]{4,2,3,1,0:T(2,128)(2,1)S(1)}, bf16[1,9,1,46,1024]{4,2,3,1,0:T(2,128)(2,1)}, u32[]{:S(2)}) copy-start(bf16[1,9,1,46,1024]{4,2,3,1,0:T(2,128)(2,1)} %get-tuple-element.20) | copy-start | bytes 2543620
  42.6 246.2 %collective-permute-start.2 = (f16[4,46,1024]{2,1,0:T(8,128)(2,1)}, f16[4,46,1024]{2,1,0:T(8,128)(2,1)}, u32[]{:S(2)}, u32[]{:S(2)}) collective-permute-start(f16[4,46,1024]{2,1,0:T(8,128)(2,1)} %multiply_convert_fusion.1), channel_id=1, source_target_pairs={{0,128},{64,192},{128,0},{192,64},{1,129},{65,193},{129,1},{193,65... | collective-permute-start | bytes 1130504 | tf_op jit(solution)/shard_map/ppermute | solution.py:15
  292.0 22.0 %copy-start = (bf16[1,9,1,46,1024]{4,2,3,1,0:T(2,128)(2,1)S(1)}, bf16[1,9,1,46,1024]{4,2,3,1,0:T(2,128)(2,1)}, u32[]{:S(2)}) copy-start(bf16[1,9,1,46,1024]{4,2,3,1,0:T(2,128)(2,1)} %get-tuple-element.19) | copy-start | bytes 2543620
  292.0 22.0 %collective-permute-start.6 = (f16[9,46,1024]{2,1,0:T(8,128)(2,1)S(1)}, f16[9,46,1024]{2,1,0:T(8,128)(2,1)S(1)}, u32[]{:S(2)}, u32[]{:S(2)}) collective-permute-start(f16[9,46,1024]{2,1,0:T(8,128)(2,1)S(1)} %fusion.8), channel_id=1, source_target_pairs={{0,128},{64,192},{128,0},{192,64},{1,129},{65,193},{129,1},{193,65... | collective-permute-start | bytes 2543624 | tf_op jit(solution)/shard_map/ppermute | solution.py:15
  293.0 5.7 %collective-permute-start.7 = (f16[2,46,1024]{2,1,0:T(8,128)(2,1)S(1)}, f16[2,46,1024]{2,1,0:T(8,128)(2,1)S(1)}, u32[]{:S(2)}, u32[]{:S(2)}) collective-permute-start(f16[2,46,1024]{2,1,0:T(8,128)(2,1)S(1)} %get-tuple-element.34), channel_id=1, source_target_pairs={{0,56},{8,0},{16,8},{24,16},{32,24},{40,32},{48,40},{56,48},{1,57}... | collective-permute-start | bytes 565256 | tf_op jit(solution)/shard_map/ppermute | solution.py:20
  293.1 8.4 %collective-permute-start.3 = (f16[2,46,1024]{2,1,0:T(8,128)(2,1)S(1)}, f16[2,46,1024]{2,1,0:T(8,128)(2,1)S(1)}, u32[]{:S(2)}, u32[]{:S(2)}) collective-permute-start(f16[2,46,1024]{2,1,0:T(8,128)(2,1)S(1)} %get-tuple-element.33), channel_id=1, source_target_pairs={{0,8},{8,16},{16,24},{24,32},{32,40},{40,48},{48,56},{56,0},{1,9},... | collective-permute-start | bytes 565256 | tf_op jit(solution)/shard_map/ppermute | solution.py:20
Sparse Core Ops, SparseCore 0:
  38.4 248.2 all-reduce.4

commit v2 on v1

v2 whole, which is shorter than its diff:
```python
import functools

import jax
import jax.numpy as jnp
from jax import lax
from jax.experimental import pallas as pl
from jax.experimental.pallas import tpu as pltpu
from jax.sharding import PartitionSpec as P

WEEKS = 7
LANES = 128
TILE = 8
SCALE = 512.0
MIB = 1024 * 1024


def core_swap(block):
    return lax.ppermute(block, "ens", [(0, 1), (1, 0), (2, 3), (3, 2)])


def chip_swap(block):
    return lax.ppermute(block, "ens", [(0, 2), (1, 3), (2, 0), (3, 1)])


def date_shift(block, step):
    count = lax.axis_size("date")
    return lax.ppermute(block, "date", [(i, (i + step) % count) for i in range(count)])


def split_kernel(kinds, leads, roles, ens_ref, runs_ref, *rest):
    outs, wide = rest[:-1], rest[-1]
    ens = ens_ref[0]
    core, half = ens % 2, ens // 2
    wide[...] = runs_ref[...].astype(jnp.float32)
    for (other_half, other_core), out in zip(roles, outs):
        kind = 2 * (1 - half if other_half else half) + (1 - core if other_core else core)
        for lead in range(0, leads, 2):
            picked = wide[pl.ds(lead * TILE * kinds + kind, 2 * TILE, stride=kinds), :]
            out[lead * TILE : (lead + 2) * TILE, :] = picked.astype(jnp.bfloat16)


def split_kinds(flat, ens, kinds, leads, roles, count, row_of):
    block = leads * TILE
    shape = jax.ShapeDtypeStruct((count * block, LANES), jnp.bfloat16)
    outs = pl.pallas_call(
        functools.partial(split_kernel, kinds, leads, roles),
        grid_spec=pltpu.PrefetchScalarGridSpec(
            num_scalar_prefetch=1,
            grid=(count,),
            in_specs=[pl.BlockSpec((block * kinds, LANES), lambda i, _: (row_of(i), 0))],
            out_specs=[pl.BlockSpec((block, LANES), lambda i, _: (i, 0))] * len(roles),
            scratch_shapes=[pltpu.VMEM((block * kinds, LANES), jnp.float32)],
        ),
        out_shape=[shape] * len(roles),
        cost_estimate=pl.CostEstimate(
            flops=0, transcendentals=0, bytes_accessed=count * block * LANES * 2 * (kinds + len(roles))
        ),
        compiler_params=pltpu.CompilerParams(vmem_limit_bytes=56 * MIB),
    )(ens, flat)
    return list(outs)


def smooth_kernel(leads, places, rows, aliased, weight_ref, *refs):
    sums = refs[: -3 - aliased]
    out_hbm, done, sem = refs[-3:]

    def tile(date, lead):
        which, place = places[date]
        start = (place * leads + lead) * TILE
        return sums[which][start : start + TILE, :]

    copies = []
    for slot, row in enumerate(rows):
        weight = [weight_ref[row, k] for k in range(5)]

        def mean(lead):
            value = weight[0] * tile(row - 2, lead)
            for k in range(1, 5):
                value = value + weight[k] * tile(row - 2 + k, lead)
            return value

        before, here = None, mean(0)
        for lead in range(leads):
            after = mean(lead + 1) if lead + 1 < leads else None
            value = here + here
            for beside in (before, after):
                if beside is not None:
                    value = value + beside
            edge = before is None or after is None
            done[slot, lead * TILE : (lead + 1) * TILE, :] = value * (1.0 / 3.0 if edge else 0.25)
            before, here = here, after
        copy = pltpu.make_async_copy(done.at[slot], out_hbm.at[row], sem.at[slot])
        copy.start()
        copies.append(copy)
    for copy in copies:
        copy.wait()


def smooth_rows(weights, sums, places, rows, leads, total_rows, into=None):
    vmem = pl.BlockSpec(memory_space=pltpu.VMEM)
    smem = pl.BlockSpec(memory_space=pltpu.SMEM)
    hbm = pl.BlockSpec(memory_space=pl.ANY)
    aliased = 0 if into is None else 1
    operands = [weights, *sums] + ([into] if aliased else [])
    return pl.pallas_call(
        functools.partial(smooth_kernel, leads, places, rows, aliased),
        in_specs=[smem] + [vmem] * len(sums) + [hbm] * aliased,
        out_specs=hbm,
        out_shape=jax.ShapeDtypeStruct((total_rows, leads * TILE, LANES), jnp.float32),
        scratch_shapes=[
            pltpu.VMEM((len(rows), leads * TILE, LANES), jnp.float32),
            pltpu.SemaphoreType.DMA((len(rows),)),
        ],
        input_output_aliases={len(operands) - 1: 0} if aliased else {},
        compiler_params=pltpu.CompilerParams(vmem_limit_bytes=32 * MIB),
    )(*operands)


def weekly_one_kernel(leads, rows_of, share_ref, table_ref, *refs):
    pairs, out, total = refs[:-2], refs[-2], refs[-1]
    block = leads * TILE
    total[...] = jnp.zeros_like(total)
    for index, rows in enumerate(rows_of):
        first, second = pairs[2 * index], pairs[2 * index + 1]
        for place, row in enumerate(rows):

            @pl.when(share_ref[row] != 0.0)
            def _(first=first, second=second, place=place, row=row):
                span = slice(place * block, (place + 1) * block)
                both = first[span, :].astype(jnp.float32) + second[span, :].astype(jnp.float32)
                total[...] += share_ref[row] * both

    for week in range(WEEKS):
        mean = jnp.zeros((TILE, LANES), jnp.float32)
        for lead in range(leads):
            mean = mean + table_ref[week, lead] * total[lead * TILE : (lead + 1) * TILE, :]
        out[week * TILE : (week + 1) * TILE, :] = mean


def weekly_one(shares, table, leads, rows_of, pairs):
    vmem = pl.BlockSpec(memory_space=pltpu.VMEM)
    smem = pl.BlockSpec(memory_space=pltpu.SMEM)
    return pl.pallas_call(
        functools.partial(weekly_one_kernel, leads, rows_of),
        in_specs=[smem, smem] + [vmem] * len(pairs),
        out_specs=vmem,
        out_shape=jax.ShapeDtypeStruct((WEEKS * TILE, LANES), jnp.float32),
        scratch_shapes=[pltpu.VMEM((leads * TILE, LANES), jnp.float32)],
        compiler_params=pltpu.CompilerParams(vmem_limit_bytes=32 * MIB),
    )(shares, table, *pairs)


def date_weights(days, cycle_days):
    columns = []
    for k in (-2, -1, 0, 1, 2):
        if k == 0:
            columns.append(jnp.full(days.shape, 8.0, jnp.float32))
            continue
        other = jnp.roll(days, -k)
        gap = jnp.mod(other - days if k > 0 else days - other, cycle_days)
        columns.append(jnp.maximum(8 - gap, 0).astype(jnp.float32))
    table = jnp.stack(columns, 1)
    return table / jnp.sum(table, 1, keepdims=True)


def lead_smoother(length):
    positions = jnp.arange(length)
    distance = jnp.abs(positions[:, None] - positions[None, :])
    smoother = jnp.where(distance == 0, 2.0, jnp.where(distance == 1, 1.0, 0.0))
    smoother = smoother.astype(jnp.float32)
    return smoother / jnp.sum(smoother, 1, keepdims=True)


def per_device(
    hindcast_runs,
    init_calendar_ordinal,
    prediction_init_position,
    horizon_sevenfold_bin,
    prediction_runs,
):
    highest = lax.Precision.HIGHEST
    _, rows, kinds, leads, cells = hindcast_runs.shape
    slots = lax.axis_size("date")
    dates = rows * slots
    members = lax.axis_size("ens")
    cycle_days = 7 * dates // 2
    block = leads * TILE
    ens = lax.axis_index("ens").astype(jnp.int32)
    date = lax.axis_index("date").astype(jnp.int32)
    ens_operand = ens.reshape(1)

    flat = hindcast_runs.reshape(rows, kinds, leads, TILE, LANES)
    flat = flat.transpose(0, 2, 3, 1, 4).reshape(rows * leads * TILE * kinds, LANES)

    last = 2
    chunks = [
        [0, 1, rows - 2, rows - 1],
        list(range(2, rows - 2 - last)),
        list(range(rows - 2 - last, rows - 2)),
    ]
    row_maps = [
        lambda i: jnp.where(i < 2, i, i + rows - 4),
        lambda i: i + chunks[1][0],
        lambda i: i + chunks[2][0],
    ]
    roles = [(True, True), (True, False)]
    split_x = functools.partial(
        split_kinds, ens=ens_operand, kinds=kinds, leads=leads, roles=roles
    )

    def partial_sum(mine, other):
        return ((mine.astype(jnp.float32) + other.astype(jnp.float32)) * SCALE).astype(jnp.float16)

    sent, got, packed = [], [], []
    sent.append(split_x(flat, count=len(chunks[0]), row_of=row_maps[0]))
    got.append(core_swap(sent[0][0]))
    flat_1, *sent[0] = lax.optimization_barrier((flat, *sent[0]))
    sent.append(split_x(flat_1, count=len(chunks[1]), row_of=row_maps[1]))
    got.append(core_swap(sent[1][0]))
    mine, sent[1][1] = lax.optimization_barrier((sent[0][1], sent[1][1]))
    packed.append(partial_sum(mine, got[0]))
    flat_2, packed[0] = lax.optimization_barrier((flat, packed[0]))
    sent.append(split_x(flat_2, count=len(chunks[2]), row_of=row_maps[2]))
    got.append(core_swap(sent[2][0]))
    mine, sent[2][1] = lax.optimization_barrier((sent[1][1], sent[2][1]))
    packed.append(partial_sum(mine, got[1]))
    flat_3, packed[1] = lax.optimization_barrier((flat, packed[1]))
    theirs, own = split_kinds(
        flat_3, ens_operand, kinds, leads, [(False, True), (False, False)], rows, lambda i: i
    )
    own_got = core_swap(theirs)
    mine, own = lax.optimization_barrier((sent[2][1], own))
    packed.append(partial_sum(mine, got[2]))
    (
        packed[2],
        init_calendar_ordinal,
        prediction_init_position,
        horizon_sevenfold_bin,
        prediction_runs,
    ) = lax.optimization_barrier(
        (
            packed[2],
            init_calendar_ordinal,
            prediction_init_position,
            horizon_sevenfold_bin,
            prediction_runs,
        )
    )
    arrived = [chip_swap(block) for block in packed]

    def local_sum(first, count, packed):
        span = slice(first * block, (first + count) * block)
        pair = own[span].astype(jnp.float32) + own_got[span].astype(jnp.float32)
        return pair + packed.astype(jnp.float32) * (1.0 / SCALE)

    low = local_sum(0, 2, arrived[0][: 2 * block])
    high = local_sum(rows - 2, 2, arrived[0][2 * block :])
    below = date_shift(high, 1)
    above = date_shift(low, -1)
    middle = local_sum(chunks[1][0], len(chunks[1]), arrived[1])
    final = local_sum(chunks[2][0], len(chunks[2]), arrived[2])

    weights = date_weights(init_calendar_ordinal, cycle_days)
    own_weights = lax.dynamic_slice_in_dim(weights, date * rows, rows, 0) * (1.0 / members)
    places = {-2: (0, 0), -1: (0, 1), 0: (1, 0), 1: (1, 1)}
    places |= {row: (2, i) for i, row in enumerate(chunks[1])}
    places |= {rows - 2: (3, 0), rows - 1: (3, 1), rows: (4, 0), rows + 1: (4, 1)}
    ready = chunks[1][-1] - 1
    smoothed = smooth_rows(
        own_weights, [below, low, middle], places, list(range(ready)), leads, rows
    )
    places |= {row: (5, i) for i, row in enumerate(chunks[2])}
    smoothed = smooth_rows(
        own_weights,
        [below, low, middle, high, above, final],
        places,
        list(range(ready, rows)),
        leads,
        rows,
        smoothed,
    )
    smoothed_norm = smoothed.reshape(rows, 1, leads, cells)

    position = prediction_init_position[0]
    row_weights = lax.dynamic_index_in_dim(weights, position, 0, keepdims=False) * (1.0 / members)
    offsets = jnp.mod(date * rows + jnp.arange(rows) - position + 2, dates)
    shares = jnp.sum(
        jnp.where(offsets[:, None] == jnp.arange(5)[None, :], row_weights[None, :], 0.0), 1
    )
    week_table = (
        horizon_sevenfold_bin[None, :] == jnp.arange(WEEKS, dtype=jnp.int32)[:, None]
    ).astype(jnp.float32)
    week_mean = week_table / jnp.sum(week_table, 1, keepdims=True)
    climate_table = jnp.matmul(week_mean, lead_smoother(leads), precision=highest)
    pairs = []
    for (_, mine), other in zip(sent, got):
        pairs += [mine, other]
    weekly_sent = weekly_one(shares, climate_table, leads, chunks, pairs)
    weekly_own = weekly_one(shares, climate_table, leads, [list(range(rows))], [own, own_got])
    weekly = weekly_own + chip_swap(weekly_sent)
    weekly = weekly.reshape(WEEKS, slots, LANES).transpose(1, 0, 2)
    step = slots // 2
    while step:
        upper = (date // step) % 2
        give = lax.dynamic_slice_in_dim(weekly, (1 - upper) * step, step, 0)
        keep = lax.dynamic_slice_in_dim(weekly, upper * step, step, 0)
        weekly = keep + lax.ppermute(give, "date", [(i, i ^ step) for i in range(slots)])
        step //= 2
    centroid = jnp.sum(prediction_runs[:, 0].astype(jnp.float32), 0) * (
        1.0 / prediction_runs.shape[0]
    )
    anomalies = jnp.einsum("wl,lp->wp", week_mean, centroid, precision=highest) - weekly[0]
    return smoothed_norm, anomalies[:, None]


def solution(mesh):
    return jax.shard_map(
        per_device,
        mesh=mesh,
        in_specs=(
            P("ens", "date", None, None, "pix"),
            P(),
            P(),
            P(),
            P(None, "ens", None, ("pix", "date")),
        ),
        out_specs=(P("date", "ens", None, "pix"), P(None, "ens", ("pix", "date"))),
        check_vma=False,
    )
```

time: 327 us -> 79.1 us (0.24)
  waiting for transfers between devices: 259 us -> 19.6 us
  Pallas kernels: 0 us -> 25.7 us
  local copies, waits for them, and re-layouts: 25.4 us -> 2.53 us
  between operations: 15 us -> 1.47 us
  starting transfers between devices: 7.07 us -> 20.4 us
  other arithmetic: 17.8 us -> 7.71 us
    unnamed x2 -> x0, waiting for transfers between devices: 240 us -> none
    pallas_call x0 -> x8, Pallas kernels: none -> 25.7 us  [the longest x4 20 us: split_kinds(): pl.pallas_call(functools.partial(split_kernel, kinds, leads, roles), grid...]
    dynamic_slice x2, local copies, waits for them, and re-layouts: 11.2 us -> 0.01 us  [per_device(): give = lax.dynamic_slice_in_dim(weekly, (1 - upper) * step, step, 0)]
    ppermute x0 -> x3, starting transfers between devices: none -> 9.38 us  [per_device(): lax.ppermute(give, 'date', [(i, i ^ step) for i in range(slots)])]
    ppermute x2, waiting for transfers between devices: 6.29 us -> 0.01 us  [date_shift(): lax.ppermute(block, 'date', [(i, (i + step) % count) for i in range(count)])]
    ppermute x0 -> x3, waiting for transfers between devices: none -> 6.2 us  [per_device(): lax.ppermute(give, 'date', [(i, i ^ step) for i in range(slots)])]
    reduce_sum x1, other arithmetic: 5.3 us -> 0.58 us  [lead_smoother(): return smoother / jnp.sum(smoother, 1, keepdims=True)]
    unnamed x22, local copies, waits for them, and re-layouts: 5.55 us -> 1.57 us
  transfers between devices with their start and end apart: 9 -> 13, of which waited for: 4 -> 4; matrix products, arithmetic and copies ran while one was open for 9% -> 13% of each run, Pallas kernels for 0% -> 26%
where the time goes in v2:
time: 79.1 us; the launch traced here: 78.4 us
  Pallas kernels  25.7 us (32%)
  starting transfers between devices  20.4 us (26%)
  waiting for transfers between devices  19.6 us (25%)
  other arithmetic  7.71 us (10%)
  local copies, waits for them, and re-layouts  2.53 us (3%)
  between operations  1.47 us (2%)
  matrix products  1.02 us (1%)
    pallas_call x4, Pallas kernels, split_kinds(): pl.pallas_call(functools.partial(split_kernel, kinds, leads, roles), grid...  20 us
    ppermute x4, waiting for transfers between devices, chip_swap(): return lax.ppermute(block, 'ens', [(0, 2), (1, 3), (2, 0), (3, 1)])  13.3 us
    ppermute x3, starting transfers between devices, per_device(): lax.ppermute(give, 'date', [(i, i ^ step) for i in range(slots)])  9.38 us
    ppermute x4, starting transfers between devices, chip_swap(): return lax.ppermute(block, 'ens', [(0, 2), (1, 3), (2, 0), (3, 1)])  7.23 us
    ppermute x3, waiting for transfers between devices, per_device(): lax.ppermute(give, 'date', [(i, i ^ step) for i in range(slots)])  6.2 us
    pallas_call x2, Pallas kernels, smooth_rows(): pl.pallas_call(functools.partial(smooth_kernel, leads, places, rows, alia...  3.93 us
    ppermute x2, starting transfers between devices, date_shift(): lax.ppermute(block, 'date', [(i, (i + step) % count) for i in range(count)])  3.31 us
    convert_element_type x3, other arithmetic, partial_sum(): ((mine.astype(jnp.float32) + other.astype(jnp.float32)) * SCALE).astype(j...  2.74 us
  transfers between devices with their start and end apart: 13, of which 4 were waited for; matrix products, arithmetic and copies ran while one was open for 13% of the time, Pallas kernels for 26%

profile of v2, /device:TPU:8, one launch (start us, length us, event | category | flops | bytes accessed | tf_op | source)
XLA Modules:
  0.0 78.4 jit_solution(13462717865112419054)
XLA Ops:
  0.6 3.6 %shard_map.68 = (bf16[1472,128]{1,0:T(8,128)(2,1)}, bf16[1472,128]{1,0:T(8,128)(2,1)}) custom-call(s32[1]{0:T(128)} %bitcast.3.ens_ref, bf16[19136,128]{1,0:T(8,128)(2,1)} %bitcast.33), custom_call_target="tpu_custom_call" | custom-call | bytes 2260992 | tf_op jit(solution)/shard_map/pallas_call | solution.py:45
  4.2 0.0 collective-permute-start
  4.2 5.5 %shard_map.69 = (bf16[2576,128]{1,0:T(8,128)(2,1)}, bf16[2576,128]{1,0:T(8,128)(2,1)}) custom-call(s32[1]{0:T(128)} %bitcast.3.ens_ref, bf16[19136,128]{1,0:T(8,128)(2,1)} %bitcast.34), custom_call_target="tpu_custom_call" | custom-call | bytes 3956736 | tf_op jit(solution)/shard_map/pallas_call | solution.py:45
  9.7 0.5 collective-permute-start.1
  10.9 0.6 fusion.1
  11.5 0.9 %multiply_convert_fusion.1 = f16[1472,128]{1,0:T(8,128)(2,1)} fusion(bf16[1472,128]{1,0:T(8,128)(2,1)S(1)} %collective-permute-done.refs_1_, bf16[1472,128]{1,0:T(8,128)(2,1)S(1)} %copy-done.2), kind=kLoop, calls=%fused_computation.2 | loop fusion | flops 942080 | bytes 1130496 | tf_op jit(solution)/shard_map/convert_element_type | solution.py:212
  12.4 2.0 %shard_map.70 = (bf16[736,128]{1,0:T(8,128)(2,1)}, bf16[736,128]{1,0:T(8,128)(2,1)}) custom-call(s32[1]{0:T(128)} %bitcast.3.ens_ref, bf16[19136,128]{1,0:T(8,128)(2,1)} %bitcast.35), custom_call_target="tpu_custom_call" | custom-call | bytes 1130496 | tf_op jit(solution)/shard_map/pallas_call | solution.py:45
  14.3 0.0 collective-permute-start.2
  14.4 3.0 %collective-permute-start.4 = (f16[1472,128]{1,0:T(8,128)(2,1)}, f16[1472,128]{1,0:T(8,128)(2,1)}, u32[]{:S(2)}, u32[]{:S(2)}) collective-permute-start(f16[1472,128]{1,0:T(8,128)(2,1)} %multiply_convert_fusion.1), channel_id=1, source_target_pairs={{0,128},{64,192},{128,0},{192,64},{1,129},{65,193},{129,1},{193,65... | collective-permute-start | bytes 1130504 | tf_op jit(solution)/shard_map/ppermute | solution.py:22
  17.4 0.0 collective-permute-done.1.refs_3_
  17.4 1.1 %multiply_convert_fusion = f16[2576,128]{1,0:T(8,128)(2,1)} fusion(bf16[2576,128]{1,0:T(8,128)(2,1)S(1)} %collective-permute-done.1.refs_3_, bf16[2576,128]{1,0:T(8,128)(2,1)S(1)} %copy-done.1), kind=kLoop, calls=%fused_computation.1 | loop fusion | flops 1648640 | bytes 1978368 | tf_op jit(solution)/shard_map/convert_element_type | solution.py:212
  18.5 9.0 %shard_map.71 = (bf16[4784,128]{1,0:T(8,128)(2,1)}, bf16[4784,128]{1,0:T(8,128)(2,1)}) custom-call(s32[1]{0:T(128)} %bitcast.3.ens_ref, bf16[19136,128]{1,0:T(8,128)(2,1)} %bitcast.36), custom_call_target="tpu_custom_call" | custom-call | bytes 7348224 | tf_op jit(solution)/shard_map/pallas_call | solution.py:45
  27.5 0.0 collective-permute-done.2.refs_5_
  27.5 0.7 multiply_convert_fusion.2
  28.3 0.1 fusion.54
  28.4 0.1 fusion.52
  28.4 0.1 fusion.51
  28.5 0.5 collective-permute-start.6
  29.0 0.0 collective-permute-start.3
  29.0 0.6 fusion.53
  29.6 1.4 %add_add_fusion = (f32[104]{0:T(128)S(1)}, f32[104]{0:T(128)S(1)}, f32[104]{0:T(128)S(1)}, f32[104]{0:T(128)S(1)}, f32[104]{0:T(128)S(1)}) fusion(s32[104]{0:T(128)S(1)} %copy-done.8, s32[2]{0:T(128)S(1)} %get-tuple-element.71, s32[102]{0:T(128)S(1)} %get-tuple-element.73, s32[1]{0:T(128)} %get-tuple-element.75, s32[103]{0:T(128)S(1)} %get-tuple-element.77, ...), kind=kLoop, calls=%fused_computation.75 | loop fusion | flops 4992 | bytes 4160 | tf_op jit(solution)/shard_map/reduce_sum | solution.py:163
  31.0 0.1 copy.33
  31.2 0.1 broadcast_divide_fusion
  31.3 0.1 convert_reduce_fusion.1
  31.4 0.1 select_reduce_fusion.share_ref
  31.5 0.8 %fusion.4.table_ref = f32[7,46]{1,0:T(8,128)S(1)} fusion(f32[46]{0:T(128)} %fusion.1, f32[7]{0:T(128)S(1)} %convert_reduce_fusion.1, s32[46]{0:T(128)S(1)} %copy-done.9), kind=kOutput, calls=%fused_computation.16 | convolution fusion | flops 193522 | bytes 1684 | tf_op jit(solution)/shard_map/dot_general | solution.py:294
  32.3 0.9 %copy-done.5 = bf16[736,128]{1,0:T(8,128)(2,1)S(1)} copy-done((bf16[736,128]{1,0:T(8,128)(2,1)S(1)}, bf16[736,128]{1,0:T(8,128)(2,1)}, u32[]{:S(2)}) %copy-start.5) | copy-done | bytes 188440
  33.2 0.9 %shard_map.75 = f32[56,128]{1,0:T(8,128)S(1)} custom-call(f32[13]{0:T(128)S(1)} %select_reduce_fusion.share_ref, f32[7,46]{1,0:T(8,128)S(1)} %fusion.4.table_ref, bf16[1472,128]{1,0:T(8,128)(2,1)S(1)} %copy-done.2, bf16[1472,128]{1,0:T(8,128)(2,1)S(1)} %collective-permute-done.refs_1_, bf16[2576,128]{1,0:T(8,128)(2,1)S(1)} %copy-done.1, ...), custom_call_target="tpu_custom_call" | custom-call | tf_op jit(solution)/shard_map/pallas_call | solution.py:143
  34.1 3.1 %collective-permute-start.9 = (f32[56,128]{1,0:T(8,128)S(1)}, f32[56,128]{1,0:T(8,128)S(1)}, u32[]{:S(2)}, u32[]{:S(2)}) collective-permute-start(f32[56,128]{1,0:T(8,128)S(1)} %shard_map.75), channel_id=1, source_target_pairs={{0,128},{64,192},{128,0},{192,64},{1,129},{65,193},{129,1},{193,65... | collective-permute-start | bytes 86024 | tf_op jit(solution)/shard_map/ppermute | solution.py:22
  37.3 0.0 collective-permute-done.3.refs_1_
  37.3 0.9 %shard_map.74 = f32[56,128]{1,0:T(8,128)S(1)} custom-call(f32[13]{0:T(128)S(1)} %select_reduce_fusion.share_ref, f32[7,46]{1,0:T(8,128)S(1)} %fusion.4.table_ref, bf16[4784,128]{1,0:T(8,128)(2,1)S(1)} %copy-done, bf16[4784,128]{1,0:T(8,128)(2,1)S(1)} %collective-permute-done.3.refs_1_), custom_call_target="tpu_custom_call" | custom-call | tf_op jit(solution)/shard_map/pallas_call | solution.py:143
  38.1 9.6 %collective-permute-done.9 = f32[56,128]{1,0:T(8,128)S(1)} collective-permute-done((f32[56,128]{1,0:T(8,128)S(1)}, f32[56,128]{1,0:T(8,128)S(1)}, u32[]{:S(2)}, u32[]{:S(2)}) %collective-permute-start.9) | collective-permute-done | bytes 28704 | tf_op jit(solution)/shard_map/ppermute | solution.py:22
  47.8 7.3 %collective-permute-start.10 = (f32[4,7,128]{2,1,0:T(8,128)S(1)}, f32[4,7,128]{2,1,0:T(8,128)S(1)}, u32[]{:S(2)}, u32[]{:S(2)}) collective-permute-start(f32[4,7,128]{2,1,0:T(8,128)S(1)} %bitcast.38), channel_id=1, source_target_pairs={{0,32},{8,40},{16,48},{24,56},{32,0},{40,8},{48,16},{56,24},{1,33}... | collective-permute-start | bytes 43016 | tf_op jit(solution)/shard_map/ppermute | solution.py:307
  55.1 0.6 collective-permute-start.8
  55.7 1.1 %collective-permute-done.10 = f32[4,7,128]{2,1,0:T(8,128)S(1)} collective-permute-done((f32[4,7,128]{2,1,0:T(8,128)S(1)}, f32[4,7,128]{2,1,0:T(8,128)S(1)}, u32[]{:S(2)}, u32[]{:S(2)}) %collective-permute-start.10) | collective-permute-done | bytes 14368 | tf_op jit(solution)/shard_map/ppermute | solution.py:307
  56.8 2.0 %collective-permute-start.11 = (f32[2,7,128]{2,1,0:T(8,128)S(1)}, f32[2,7,128]{2,1,0:T(8,128)S(1)}, u32[]{:S(2)}, u32[]{:S(2)}) collective-permute-start(f32[2,7,128]{2,1,0:T(8,128)S(1)} %constant_dynamic-slice_fusion.1), channel_id=1, source_target_pairs={{0,16},{8,24},{16,0},{24,8},{32,48},{40,56},{48,32},{56,40},{1,17}... | collective-permute-start | bytes 21512 | tf_op jit(solution)/shard_map/ppermute | solution.py:307
  58.8 0.0 collective-permute-done.4
  58.8 3.7 %collective-permute-done.8 = f16[736,128]{1,0:T(8,128)(2,1)S(1)} collective-permute-done((f16[736,128]{1,0:T(8,128)(2,1)S(1)}, f16[736,128]{1,0:T(8,128)(2,1)S(1)}, u32[]{:S(2)}, u32[]{:S(2)}) %collective-permute-start.8) | collective-permute-done | bytes 188448 | tf_op jit(solution)/shard_map/ppermute | solution.py:22
  62.5 1.3 %multiply_add_fusion.2 = (f32[736,128]{1,0:T(8,128)S(1)}, f32[736,128]{1,0:T(8,128)S(1)}, f32[736,128]{1,0:T(8,128)S(1)}) fusion(f16[1472,128]{1,0:T(8,128)(2,1)} %collective-permute-done.4, bf16[4784,128]{1,0:T(8,128)(2,1)S(1)} %collective-permute-done.3.refs_1_, bf16[4784,128]{1,0:T(8,128)(2,1)S(1)} %copy-done, f16[736,128]{1,0:T(8,128)(2,1)S(1)} %collective-permute-done.8), kind=kLoop, calls=%fused_computation.4 | loop fusion | flops 1695744 | bytes 2826240 | tf_op jit(solution)/shard_map/add | solution.py:254
  63.8 1.1 %collective-permute-start.5 = (f32[736,128]{1,0:T(8,128)S(1)}, f32[736,128]{1,0:T(8,128)S(1)}, u32[]{:S(2)}, u32[]{:S(2)}) collective-permute-start(f32[736,128]{1,0:T(8,128)S(1)} %get-tuple-element.66.refs_3_), channel_id=1, source_target_pairs={{0,8},{8,16},{16,24},{24,32},{32,40},{40,48},{48,56},{56,0},{1,9},... | collective-permute-start | bytes 1130504 | tf_op jit(solution)/shard_map/ppermute | solution.py:27
  64.9 2.2 %collective-permute-start.7 = (f32[736,128]{1,0:T(8,128)S(1)}, f32[736,128]{1,0:T(8,128)S(1)}, u32[]{:S(2)}, u32[]{:S(2)}) collective-permute-start(f32[736,128]{1,0:T(8,128)S(1)} %get-tuple-element.65.refs_1_), channel_id=1, source_target_pairs={{0,56},{8,0},{16,8},{24,16},{32,24},{40,32},{48,40},{56,48},{1,57}... | collective-permute-start | bytes 1130504 | tf_op jit(solution)/shard_map/ppermute | solution.py:27
  67.1 0.1 collective-permute-start.12
  67.2 1.3 %multiply_add_fusion.refs_2_ = f32[2576,128]{1,0:T(8,128)S(1)} fusion(f16[2576,128]{1,0:T(8,128)(2,1)} %collective-permute-done.6, bf16[4784,128]{1,0:T(8,128)(2,1)S(1)} %collective-permute-done.3.refs_1_, bf16[4784,128]{1,0:T(8,128)(2,1)S(1)} %copy-done), kind=kLoop, calls=%fused_computation | loop fusion | flops 1978368 | bytes 3297280 | tf_op jit(solution)/shard_map/add | solution.py:254
  68.6 5.1 %collective-permute-done.12 = f32[1,7,128]{2,1,0:T(8,128)S(1)} collective-permute-done((f32[1,7,128]{2,1,0:T(8,128)S(1)}, f32[1,7,128]{2,1,0:T(8,128)S(1)}, u32[]{:S(2)}, u32[]{:S(2)}) %collective-permute-start.12) | collective-permute-done | bytes 3616 | tf_op jit(solution)/shard_map/ppermute | solution.py:307
  73.7 0.2 fusion.16
  73.9 0.6 copy.37
  74.5 2.0 %shard_map.72.refs_6_ = f32[13,368,128]{2,1,0:T(8,128)} custom-call(f32[13,5]{1,0:T(8,128)S(1)} %dynamic-slice_multiply_fusion.weight_ref, f32[736,128]{1,0:T(8,128)S(1)} %collective-permute-done.5.refs_0_, f32[736,128]{1,0:T(8,128)S(1)} %get-tuple-element.65.refs_1_, f32[2576,128]{1,0:T(8,128)S(1)} %multiply_add_fusion.refs_2_), custom_call_target="tpu_custom_call" | custom-call | tf_op jit(solution)/shard_map/pallas_call | solution.py:105
  76.5 1.9 %shard_map.73 = f32[13,368,128]{2,1,0:T(8,128)} custom-call(f32[13,5]{1,0:T(8,128)S(1)} %dynamic-slice_multiply_fusion.weight_ref, f32[736,128]{1,0:T(8,128)S(1)} %collective-permute-done.5.refs_0_, f32[736,128]{1,0:T(8,128)S(1)} %get-tuple-element.65.refs_1_, f32[2576,128]{1,0:T(8,128)S(1)} %multiply_add_fusion.refs_2_, ...), custom_call_target="tpu_custom_call", output_to_operand_aliasing={{}: (7, {})} | custom-call | tf_op jit(solution)/shard_map/pallas_call | solution.py:105
  (37 shorter events, 0.2 us)
Async XLA Ops:
  4.2 7.2 %collective-permute-start = (bf16[1472,128]{1,0:T(8,128)(2,1)}, bf16[1472,128]{1,0:T(8,128)(2,1)S(1)}, u32[]{:S(2)}, u32[]{:S(2)}) collective-permute-start(bf16[1472,128]{1,0:T(8,128)(2,1)} %get-tuple-element.27), channel_id=1, source_target_pairs={{0,64},{64,0},{128,192},{192,128},{1,65},{65,1},{129,193},{193,129... | collective-permute-start | bytes 1130504 | tf_op jit(solution)/shard_map/ppermute | solution.py:18
  4.2 7.2 %copy-start.2 = (bf16[1472,128]{1,0:T(8,128)(2,1)S(1)}, bf16[1472,128]{1,0:T(8,128)(2,1)}, u32[]{:S(2)}) copy-start(bf16[1472,128]{1,0:T(8,128)(2,1)} %get-tuple-element.33.refs_0_) | copy-start | bytes 1130500
  9.7 7.7 %collective-permute-start.1 = (bf16[2576,128]{1,0:T(8,128)(2,1)}, bf16[2576,128]{1,0:T(8,128)(2,1)S(1)}, u32[]{:S(2)}, u32[]{:S(2)}) collective-permute-start(bf16[2576,128]{1,0:T(8,128)(2,1)} %get-tuple-element.38), channel_id=1, source_target_pairs={{0,64},{64,0},{128,192},{192,128},{1,65},{65,1},{129,193},{193,129... | collective-permute-start | bytes 1978376 | tf_op jit(solution)/shard_map/ppermute | solution.py:18
  12.4 5.0 %copy-start.1 = (bf16[2576,128]{1,0:T(8,128)(2,1)S(1)}, bf16[2576,128]{1,0:T(8,128)(2,1)}, u32[]{:S(2)}) copy-start(bf16[2576,128]{1,0:T(8,128)(2,1)} %get-tuple-element.37.refs_2_) | copy-start | bytes 1978372
  14.3 13.2 %collective-permute-start.2 = (bf16[736,128]{1,0:T(8,128)(2,1)}, bf16[736,128]{1,0:T(8,128)(2,1)S(1)}, u32[]{:S(2)}, u32[]{:S(2)}) collective-permute-start(bf16[736,128]{1,0:T(8,128)(2,1)} %get-tuple-element.42), channel_id=1, source_target_pairs={{0,64},{64,0},{128,192},{192,128},{1,65},{65,1},{129,193},{193,129... | collective-permute-start | bytes 565256 | tf_op jit(solution)/shard_map/ppermute | solution.py:18
  14.4 44.5 %collective-permute-start.4 = (f16[1472,128]{1,0:T(8,128)(2,1)}, f16[1472,128]{1,0:T(8,128)(2,1)}, u32[]{:S(2)}, u32[]{:S(2)}) collective-permute-start(f16[1472,128]{1,0:T(8,128)(2,1)} %multiply_convert_fusion.1), channel_id=1, source_target_pairs={{0,128},{64,192},{128,0},{192,64},{1,129},{65,193},{129,1},{193,65... | collective-permute-start | bytes 1130504 | tf_op jit(solution)/shard_map/ppermute | solution.py:22
  18.5 9.0 %copy-start.3 = (bf16[736,128]{1,0:T(8,128)(2,1)S(1)}, bf16[736,128]{1,0:T(8,128)(2,1)}, u32[]{:S(2)}) copy-start(bf16[736,128]{1,0:T(8,128)(2,1)} %get-tuple-element.41.refs_4_) | copy-start | bytes 565252
  18.5 9.8 %copy-start.8 = (s32[104]{0:T(128)S(1)}, s32[104]{0:T(128)}, u32[]{:S(2)}) copy-start(s32[104]{0:T(128)} %param.6) | copy-start | bytes 1252
  18.5 12.8 %copy-start.9 = (s32[46]{0:T(128)S(1)}, s32[46]{0:T(128)}, u32[]{:S(2)}) copy-start(s32[46]{0:T(128)} %param.8) | copy-start | bytes 556
  27.5 1.5 %copy-start.4 = (bf16[736,128]{1,0:T(8,128)(2,1)}, bf16[736,128]{1,0:T(8,128)(2,1)S(1)}, u32[]{:S(2)}) copy-start(bf16[736,128]{1,0:T(8,128)(2,1)S(1)} %collective-permute-done.2.refs_5_) | copy-start | bytes 565252
  28.5 38.7 %collective-permute-start.6 = (f16[2576,128]{1,0:T(8,128)(2,1)}, f16[2576,128]{1,0:T(8,128)(2,1)}, u32[]{:S(2)}, u32[]{:S(2)}) collective-permute-start(f16[2576,128]{1,0:T(8,128)(2,1)} %multiply_convert_fusion), channel_id=1, source_target_pairs={{0,128},{64,192},{128,0},{192,64},{1,129},{65,193},{129,1},{193,65... | collective-permute-start | bytes 1978376 | tf_op jit(solution)/shard_map/ppermute | solution.py:22
  29.0 8.2 %collective-permute-start.3 = (bf16[4784,128]{1,0:T(8,128)(2,1)}, bf16[4784,128]{1,0:T(8,128)(2,1)S(1)}, u32[]{:S(2)}, u32[]{:S(2)}) collective-permute-start(bf16[4784,128]{1,0:T(8,128)(2,1)} %get-tuple-element.45), channel_id=1, source_target_pairs={{0,64},{64,0},{128,192},{192,128},{1,65},{65,1},{129,193},{193,129... | collective-permute-start | bytes 3674120 | tf_op jit(solution)/shard_map/ppermute | solution.py:18
  31.5 5.7 %copy-start.7 = (bf16[11,1,46,128]{3,2,1,0:T(8,128)(2,1)S(1)}, bf16[11,1,46,128]{3,2,1,0:T(8,128)(2,1)}, u32[]{:S(2)}) copy-start(bf16[11,1,46,128]{3,2,1,0:T(8,128)(2,1)} %param.9) | copy-start | bytes 388612
  32.3 0.9 %copy-start.5 = (bf16[736,128]{1,0:T(8,128)(2,1)S(1)}, bf16[736,128]{1,0:T(8,128)(2,1)}, u32[]{:S(2)}) copy-start(bf16[736,128]{1,0:T(8,128)(2,1)} %copy-done.4) | copy-start | bytes 565252
  33.2 4.0 %copy-start = (bf16[4784,128]{1,0:T(8,128)(2,1)S(1)}, bf16[4784,128]{1,0:T(8,128)(2,1)}, u32[]{:S(2)}) copy-start(bf16[4784,128]{1,0:T(8,128)(2,1)} %get-tuple-element.44.refs_0_) | copy-start | bytes 3674116
  34.1 13.7 %collective-permute-start.9 = (f32[56,128]{1,0:T(8,128)S(1)}, f32[56,128]{1,0:T(8,128)S(1)}, u32[]{:S(2)}, u32[]{:S(2)}) collective-permute-start(f32[56,128]{1,0:T(8,128)S(1)} %shard_map.75), channel_id=1, source_target_pairs={{0,128},{64,192},{128,0},{192,64},{1,129},{65,193},{129,1},{193,65... | collective-permute-start | bytes 86024 | tf_op jit(solution)/shard_map/ppermute | solution.py:22
  37.2 17.8 %copy-start.6 = (f16[736,128]{1,0:T(8,128)(2,1)S(1)}, f16[736,128]{1,0:T(8,128)(2,1)}, u32[]{:S(2)}) copy-start(f16[736,128]{1,0:T(8,128)(2,1)} %multiply_convert_fusion.2) | copy-start | bytes 565252
  47.8 9.0 %collective-permute-start.10 = (f32[4,7,128]{2,1,0:T(8,128)S(1)}, f32[4,7,128]{2,1,0:T(8,128)S(1)}, u32[]{:S(2)}, u32[]{:S(2)}) collective-permute-start(f32[4,7,128]{2,1,0:T(8,128)S(1)} %bitcast.38), channel_id=1, source_target_pairs={{0,32},{8,40},{16,48},{24,56},{32,0},{40,8},{48,16},{56,24},{1,33}... | collective-permute-start | bytes 43016 | tf_op jit(solution)/shard_map/ppermute | solution.py:307
  55.1 7.4 %collective-permute-start.8 = (f16[736,128]{1,0:T(8,128)(2,1)S(1)}, f16[736,128]{1,0:T(8,128)(2,1)S(1)}, u32[]{:S(2)}, u32[]{:S(2)}) collective-permute-start(f16[736,128]{1,0:T(8,128)(2,1)S(1)} %copy-done.6), channel_id=1, source_target_pairs={{0,128},{64,192},{128,0},{192,64},{1,129},{65,193},{129,1},{193,65... | collective-permute-start | bytes 565256 | tf_op jit(solution)/shard_map/ppermute | solution.py:22
  56.8 10.3 %collective-permute-start.11 = (f32[2,7,128]{2,1,0:T(8,128)S(1)}, f32[2,7,128]{2,1,0:T(8,128)S(1)}, u32[]{:S(2)}, u32[]{:S(2)}) collective-permute-start(f32[2,7,128]{2,1,0:T(8,128)S(1)} %constant_dynamic-slice_fusion.1), channel_id=1, source_target_pairs={{0,16},{8,24},{16,0},{24,8},{32,48},{40,56},{48,32},{56,40},{1,17}... | collective-permute-start | bytes 21512 | tf_op jit(solution)/shard_map/ppermute | solution.py:307
  63.8 10.7 %collective-permute-start.5 = (f32[736,128]{1,0:T(8,128)S(1)}, f32[736,128]{1,0:T(8,128)S(1)}, u32[]{:S(2)}, u32[]{:S(2)}) collective-permute-start(f32[736,128]{1,0:T(8,128)S(1)} %get-tuple-element.66.refs_3_), channel_id=1, source_target_pairs={{0,8},{8,16},{16,24},{24,32},{32,40},{40,48},{48,56},{56,0},{1,9},... | collective-permute-start | bytes 1130504 | tf_op jit(solution)/shard_map/ppermute | solution.py:27
  64.9 11.6 %collective-permute-start.7 = (f32[736,128]{1,0:T(8,128)S(1)}, f32[736,128]{1,0:T(8,128)S(1)}, u32[]{:S(2)}, u32[]{:S(2)}) collective-permute-start(f32[736,128]{1,0:T(8,128)S(1)} %get-tuple-element.65.refs_1_), channel_id=1, source_target_pairs={{0,56},{8,0},{16,8},{24,16},{32,24},{40,32},{48,40},{56,48},{1,57}... | collective-permute-start | bytes 1130504 | tf_op jit(solution)/shard_map/ppermute | solution.py:27
  67.1 6.5 %collective-permute-start.12 = (f32[1,7,128]{2,1,0:T(8,128)S(1)}, f32[1,7,128]{2,1,0:T(8,128)S(1)}, u32[]{:S(2)}, u32[]{:S(2)}) collective-permute-start(f32[1,7,128]{2,1,0:T(8,128)S(1)} %constant_dynamic-slice_fusion), channel_id=1, source_target_pairs={{0,8},{8,0},{16,24},{24,16},{32,40},{40,32},{48,56},{56,48},{1,9},... | collective-permute-start | bytes 10760 | tf_op jit(solution)/shard_map/ppermute | solution.py:307

commit v3 on v2

v3 whole, which is shorter than its diff:
```python
import functools

import jax
import jax.numpy as jnp
from jax import lax
from jax.experimental import pallas as pl
from jax.experimental.pallas import tpu as pltpu
from jax.sharding import PartitionSpec as P

WEEKS = 7
LANES = 128
TILE = 8
SCALE = 512.0
MIB = 1024 * 1024
SMALL = pl.CostEstimate(flops=1, transcendentals=0, bytes_accessed=1)


def core_swap(block):
    return lax.ppermute(block, "ens", [(0, 1), (1, 0), (2, 3), (3, 2)])


def chip_swap(block):
    return lax.ppermute(block, "ens", [(0, 2), (1, 3), (2, 0), (3, 1)])


def date_shift(block, step):
    count = lax.axis_size("date")
    return lax.ppermute(block, "date", [(i, (i + step) % count) for i in range(count)])


def split_kernel(kinds, leads, rows, roles, groups, ens_ref, runs_ref, *rest):
    outs, (held, wide, sem) = rest[:-3], rest[-3:]
    block = leads * TILE
    copies = []
    for slot, row in enumerate(rows):
        copy = pltpu.make_async_copy(
            runs_ref.at[pl.ds(row * block * kinds, block * kinds)], held.at[slot], sem.at[slot]
        )
        copy.start()
        copies.append(copy)
    ens = ens_ref[0]
    core, half = ens % 2, ens // 2
    chosen = [
        2 * (1 - half if other_half else half) + (1 - core if other_core else core)
        for other_half, other_core in roles
    ]
    for slot in range(len(rows)):
        group = [i for i, members in enumerate(groups) if rows[slot] in members][0]
        start = groups[group].index(rows[slot]) * block
        copies[slot].wait()
        spread = wide.at[slot % 2]
        spread[...] = held[slot].astype(jnp.float32)
        for role, kind in enumerate(chosen):
            out = outs[group * len(roles) + role]
            for lead in range(0, leads, 2):
                picked = spread[pl.ds(lead * TILE * kinds + kind, 2 * TILE, stride=kinds), :]
                out[start + lead * TILE : start + (lead + 2) * TILE, :] = picked.astype(
                    jnp.bfloat16
                )


def split_kinds(flat, ens, kinds, leads, roles, groups):
    block = leads * TILE
    rows = [row for group in groups for row in group]
    shapes = [
        pltpu.VMEM((len(group) * block, LANES), jnp.bfloat16)
        for group in groups
        for _ in roles
    ]
    outs = pl.pallas_call(
        functools.partial(split_kernel, kinds, leads, rows, roles, groups),
        in_specs=[
            pl.BlockSpec(memory_space=pltpu.SMEM),
            pl.BlockSpec(memory_space=pltpu.HBM),
        ],
        out_specs=[pl.BlockSpec(memory_space=pltpu.VMEM)] * len(shapes),
        scratch_shapes=[
            pltpu.VMEM((len(rows), block * kinds, LANES), jnp.bfloat16),
            pltpu.VMEM((2, block * kinds, LANES), jnp.float32),
            pltpu.SemaphoreType.DMA((len(rows),)),
        ],
        out_shape=shapes,
        cost_estimate=pl.CostEstimate(
            flops=0,
            transcendentals=0,
            bytes_accessed=len(rows) * block * LANES * 2 * (kinds + len(roles)),
        ),
        compiler_params=pltpu.CompilerParams(vmem_limit_bytes=16 * MIB),
    )(ens, pltpu.with_memory_space_constraint(flat, pltpu.HBM))
    return [list(outs[i : i + len(roles)]) for i in range(0, len(shapes), len(roles))]


def smooth_kernel(leads, places, rows, count, extra, weight_ref, *refs):
    sums = refs[:count]
    outs, (done, sem) = refs[-2 - (2 if extra else 1) : -2], refs[-2:]

    def tile(date, lead):
        which, place = places[date]
        start = (place * leads + lead) * TILE
        return sums[which][start : start + TILE, :]

    copies = []
    for slot, row in enumerate(rows):
        weight = [weight_ref[row, k] for k in range(5)]

        def mean(lead):
            value = weight[0] * tile(row - 2, lead)
            for k in range(1, 5):
                value = value + weight[k] * tile(row - 2 + k, lead)
            return value

        before, here = None, mean(0)
        for lead in range(leads):
            after = mean(lead + 1) if lead + 1 < leads else None
            value = here + here
            for beside in (before, after):
                if beside is not None:
                    value = value + beside
            edge = before is None or after is None
            done[slot, lead * TILE : (lead + 1) * TILE, :] = value * (1.0 / 3.0 if edge else 0.25)
            before, here = here, after
        copy = pltpu.make_async_copy(done.at[slot], outs[0].at[row], sem.at[slot])
        copy.start()
        copies.append(copy)
    if extra:
        forecast, kept, given = refs[count : count + 3]
        outs[1][:, 0, :] = forecast[...] - (kept[...] + given[...])
    for copy in copies:
        copy.wait()


def smooth_rows(weights, sums, places, rows, leads, total_rows, extra=(), into=None):
    vmem = pl.BlockSpec(memory_space=pltpu.VMEM)
    smem = pl.BlockSpec(memory_space=pltpu.SMEM)
    hbm = pl.BlockSpec(memory_space=pltpu.HBM)
    operands = [weights, *sums, *extra] + ([] if into is None else [into])
    shapes = [jax.ShapeDtypeStruct((total_rows, leads * TILE, LANES), jnp.float32)]
    if extra:
        shapes.append(jax.ShapeDtypeStruct((WEEKS, 1, LANES), jnp.float32))
    return pl.pallas_call(
        functools.partial(smooth_kernel, leads, places, rows, len(sums), len(extra)),
        in_specs=[smem] + [vmem] * (len(sums) + len(extra)) + ([] if into is None else [hbm]),
        out_specs=[hbm] + ([vmem] if extra else []),
        out_shape=shapes,
        scratch_shapes=[
            pltpu.VMEM((len(rows), leads * TILE, LANES), jnp.float32),
            pltpu.SemaphoreType.DMA((len(rows),)),
        ],
        input_output_aliases={} if into is None else {len(operands) - 1: 0},
        cost_estimate=SMALL,
        compiler_params=pltpu.CompilerParams(vmem_limit_bytes=16 * MIB),
    )(*operands)


def weekly_one_kernel(leads, rows_of, share_ref, table_ref, *refs):
    pairs, out, total = refs[:-2], refs[-2], refs[-1]
    block = leads * TILE
    total[...] = jnp.zeros_like(total)
    for index, rows in enumerate(rows_of):
        first, second = pairs[2 * index], pairs[2 * index + 1]
        for place, row in enumerate(rows):

            @pl.when(share_ref[row] != 0.0)
            def _(first=first, second=second, place=place, row=row):
                span = slice(place * block, (place + 1) * block)
                both = first[span, :].astype(jnp.float32) + second[span, :].astype(jnp.float32)
                total[...] += share_ref[row] * both

    for week in range(WEEKS):
        mean = jnp.zeros((TILE, LANES), jnp.float32)
        for lead in range(leads):
            mean = mean + table_ref[week, lead] * total[lead * TILE : (lead + 1) * TILE, :]
        out[week * TILE : (week + 1) * TILE, :] = mean


def weekly_one(shares, table, leads, rows_of, pairs):
    vmem = pl.BlockSpec(memory_space=pltpu.VMEM)
    smem = pl.BlockSpec(memory_space=pltpu.SMEM)
    return pl.pallas_call(
        functools.partial(weekly_one_kernel, leads, rows_of),
        in_specs=[smem, smem] + [vmem] * len(pairs),
        out_specs=vmem,
        out_shape=jax.ShapeDtypeStruct((WEEKS * TILE, LANES), jnp.float32),
        scratch_shapes=[pltpu.VMEM((leads * TILE, LANES), jnp.float32)],
        cost_estimate=SMALL,
        compiler_params=pltpu.CompilerParams(vmem_limit_bytes=16 * MIB),
    )(shares, table, *pairs)


def date_weights(days, cycle_days):
    columns = []
    for k in (-2, -1, 0, 1, 2):
        if k == 0:
            columns.append(jnp.full(days.shape, 8.0, jnp.float32))
            continue
        other = jnp.roll(days, -k)
        gap = jnp.mod(other - days if k > 0 else days - other, cycle_days)
        columns.append(jnp.maximum(8 - gap, 0).astype(jnp.float32))
    table = jnp.stack(columns, 1)
    return table / jnp.sum(table, 1, keepdims=True)


def lead_smoother(length):
    positions = jnp.arange(length)
    distance = jnp.abs(positions[:, None] - positions[None, :])
    smoother = jnp.where(distance == 0, 2.0, jnp.where(distance == 1, 1.0, 0.0))
    smoother = smoother.astype(jnp.float32)
    return smoother / jnp.sum(smoother, 1, keepdims=True)


def per_device(
    hindcast_runs,
    init_calendar_ordinal,
    prediction_init_position,
    horizon_sevenfold_bin,
    prediction_runs,
):
    highest = lax.Precision.HIGHEST
    _, rows, kinds, leads, cells = hindcast_runs.shape
    slots = lax.axis_size("date")
    dates = rows * slots
    members = lax.axis_size("ens")
    cycle_days = 7 * dates // 2
    block = leads * TILE
    ens = lax.axis_index("ens").astype(jnp.int32)
    date = lax.axis_index("date").astype(jnp.int32)
    ens_operand = ens.reshape(1)

    flat = hindcast_runs.reshape(rows, kinds, leads, TILE, LANES)
    flat = flat.transpose(0, 2, 3, 1, 4).reshape(rows * leads * TILE * kinds, LANES)

    last = 2
    chunks = [
        [0, 1, rows - 2, rows - 1],
        list(range(2, rows - 2 - last)),
        list(range(rows - 2 - last, rows - 2)),
    ]
    split = functools.partial(split_kinds, kinds=kinds, leads=leads)
    for_x = [(True, True), (True, False)]
    for_own = [(False, True), (False, False)]

    def pair_sum(mine, other):
        return ((mine.astype(jnp.float32) + other.astype(jnp.float32)) * SCALE).astype(jnp.float16)

    [sent_0] = split(flat, ens_operand, roles=for_x, groups=chunks[:1])
    got = [core_swap(sent_0[0])]
    flat, *sent_0 = lax.optimization_barrier((flat, *sent_0))
    sent = [sent_0] + split(flat, ens_operand, roles=for_x, groups=chunks[1:])
    got += [core_swap(sent[1][0]), core_swap(sent[2][0])]
    mine, *sent[1] = lax.optimization_barrier((sent[0][1], *sent[1]))
    packed = [pair_sum(mine, got[0])]
    flat, packed[0] = lax.optimization_barrier((flat, packed[0]))
    [[theirs, own]] = split(flat, ens_operand, roles=for_own, groups=[list(range(rows))])
    own_got = core_swap(theirs)
    mine, own = lax.optimization_barrier((sent[1][1], own))
    packed.append(pair_sum(mine, got[1]))
    mine, packed[1] = lax.optimization_barrier((sent[2][1], packed[1]))
    packed.append(pair_sum(mine, got[2]))
    small = (
        init_calendar_ordinal,
        prediction_init_position,
        horizon_sevenfold_bin,
        prediction_runs,
    )
    packed[2], *small = lax.optimization_barrier((packed[2], *small))
    init_calendar_ordinal, prediction_init_position, horizon_sevenfold_bin, prediction_runs = small
    arrived = [chip_swap(block) for block in packed]

    def local_sum(first, count, packed):
        span = slice(first * block, (first + count) * block)
        pair = own[span].astype(jnp.float32) + own_got[span].astype(jnp.float32)
        return pair + packed.astype(jnp.float32) * (1.0 / SCALE)

    low = local_sum(0, 2, arrived[0][: 2 * block])
    high = local_sum(rows - 2, 2, arrived[0][2 * block :])
    below = date_shift(high, 1)
    above = date_shift(low, -1)
    middle = local_sum(chunks[1][0], len(chunks[1]), arrived[1])
    final = local_sum(chunks[2][0], len(chunks[2]), arrived[2])

    weights = date_weights(init_calendar_ordinal, cycle_days)
    own_weights = lax.dynamic_slice_in_dim(weights, date * rows, rows, 0) * (1.0 / members)

    position = prediction_init_position[0]
    row_weights = lax.dynamic_index_in_dim(weights, position, 0, keepdims=False) * (1.0 / members)
    offsets = jnp.mod(date * rows + jnp.arange(rows) - position + 2, dates)
    shares = jnp.sum(
        jnp.where(offsets[:, None] == jnp.arange(5)[None, :], row_weights[None, :], 0.0), 1
    )
    week_table = (
        horizon_sevenfold_bin[None, :] == jnp.arange(WEEKS, dtype=jnp.int32)[:, None]
    ).astype(jnp.float32)
    week_mean = week_table / jnp.sum(week_table, 1, keepdims=True)
    climate_table = jnp.matmul(week_mean, lead_smoother(leads), precision=highest)
    pairs = []
    for (_, mine), other in zip(sent, got):
        pairs += [mine, other]
    weekly = jnp.stack(
        [
            weekly_one(shares, climate_table, leads, chunks, pairs),
            weekly_one(shares, climate_table, leads, [list(range(rows))], [own, own_got]),
        ]
    )
    weekly = weekly.reshape(2, WEEKS, slots, LANES).transpose(2, 0, 1, 3)
    weekly, low, high = lax.optimization_barrier((weekly, low, high))
    weekly = lax.all_to_all(weekly, "date", split_axis=0, concat_axis=0, tiled=True)
    weekly = jnp.sum(weekly, 0, keepdims=True)
    weekly_given = chip_swap(weekly[0, 0])
    centroid = jnp.sum(prediction_runs[:, 0].astype(jnp.float32), 0) * (
        1.0 / prediction_runs.shape[0]
    )
    forecast = jnp.einsum("wl,lp->wp", week_mean, centroid, precision=highest)

    places = {-2: (0, 0), -1: (0, 1), 0: (1, 0), 1: (1, 1)}
    places |= {row: (2, i) for i, row in enumerate(chunks[1])}
    places |= {rows - 2: (3, 0), rows - 1: (3, 1), rows: (4, 0), rows + 1: (4, 1)}
    places |= {row: (5, i) for i, row in enumerate(chunks[2])}
    ready = chunks[1][-1] - 1
    [smoothed] = smooth_rows(
        own_weights, [below, low, middle], places, list(range(ready)), leads, rows
    )
    smoothed, anomalies = smooth_rows(
        own_weights,
        [below, low, middle, high, above, final],
        places,
        list(range(ready, rows)),
        leads,
        rows,
        (forecast, weekly[0, 1], weekly_given),
        smoothed,
    )
    return smoothed.reshape(rows, 1, leads, cells), anomalies


def solution(mesh):
    return jax.shard_map(
        per_device,
        mesh=mesh,
        in_specs=(
            P("ens", "date", None, None, "pix"),
            P(),
            P(),
            P(),
            P(None, "ens", None, ("pix", "date")),
        ),
        out_specs=(P("date", "ens", None, "pix"), P(None, "ens", ("pix", "date"))),
        check_vma=False,
    )
```

time: 79.1 us -> 63.9 us (0.81)
  Pallas kernels: 25.7 us -> 15 us
  waiting for transfers between devices: 19.6 us -> 9.09 us
  other arithmetic: 7.71 us -> 13 us
  local copies, waits for them, and re-layouts: 2.53 us -> 3.65 us
    ppermute x4, waiting for transfers between devices: 13.3 us -> 0.01 us  [chip_swap(): return lax.ppermute(block, 'ens', [(0, 2), (1, 3), (2, 0), (3, 1)])]
    pallas_call x6 -> x5, Pallas kernels: 24 us -> 12.7 us  [the longest x3 7.94 us: split_kinds(): pl.pallas_call(functools.partial(split_kernel, kinds, leads, rows, roles,...]
    ppermute x3 -> x0, starting transfers between devices: 9.38 us -> none  [per_device(): lax.ppermute(give, 'date', [(i, i ^ step) for i in range(slots)])]
    all_to_all x0 -> x1, starting transfers between devices: none -> 8.76 us  [per_device(): lax.all_to_all(weekly, 'date', split_axis=0, concat_axis=0, tiled=True)]
    ppermute x3 -> x0, waiting for transfers between devices: 6.2 us -> none  [per_device(): lax.ppermute(give, 'date', [(i, i ^ step) for i in range(slots)])]
    ppermute x2, waiting for transfers between devices: 0.01 us -> 4.61 us  [date_shift(): lax.ppermute(block, 'date', [(i, (i + step) % count) for i in range(count)])]
    all_to_all x0 -> x1, waiting for transfers between devices: none -> 4.46 us  [per_device(): lax.all_to_all(weekly, 'date', split_axis=0, concat_axis=0, tiled=True)]
    convert_element_type x3, other arithmetic: 2.74 us -> 4.81 us  [pair_sum(): ((mine.astype(jnp.float32) + other.astype(jnp.float32)) * SCALE).astype(j...]
  transfers between devices with their start and end apart: 13 -> 11, of which waited for: 4 -> 2; matrix products, arithmetic and copies ran while one was open for 13% -> 24% of each run, Pallas kernels for 26% -> 17%
where the time goes in v3:
time: 63.9 us; the launch traced here: 63.5 us
  starting transfers between devices  20.2 us (32%)
  Pallas kernels  15 us (23%)
  other arithmetic  13 us (20%)
  waiting for transfers between devices  9.09 us (14%)
  local copies, waits for them, and re-layouts  3.65 us (6%)
  between operations  1.52 us (2%)
  matrix products  1.09 us (2%)
    all_to_all x1, starting transfers between devices, per_device(): lax.all_to_all(weekly, 'date', split_axis=0, concat_axis=0, tiled=True)  8.76 us
    pallas_call x3, Pallas kernels, split_kinds(): pl.pallas_call(functools.partial(split_kernel, kinds, leads, rows, roles,...  7.94 us
    ppermute x4, starting transfers between devices, chip_swap(): return lax.ppermute(block, 'ens', [(0, 2), (1, 3), (2, 0), (3, 1)])  7.31 us
    convert_element_type x3, other arithmetic, pair_sum(): ((mine.astype(jnp.float32) + other.astype(jnp.float32)) * SCALE).astype(j...  4.81 us
    pallas_call x2, Pallas kernels, smooth_rows(): pl.pallas_call(functools.partial(smooth_kernel, leads, places, rows, len(...  4.79 us
    ppermute x2, waiting for transfers between devices, date_shift(): lax.ppermute(block, 'date', [(i, (i + step) % count) for i in range(count)])  4.61 us
    all_to_all x1, waiting for transfers between devices, per_device(): lax.all_to_all(weekly, 'date', split_axis=0, concat_axis=0, tiled=True)  4.46 us
    add x2, other arithmetic, local_sum(): return pair + packed.astype(jnp.float32) * (1.0 / SCALE)  3.46 us
  transfers between devices with their start and end apart: 11, of which 2 were waited for; matrix products, arithmetic and copies ran while one was open for 24% of the time, Pallas kernels for 17%

profile of v3, /device:TPU:8, one launch (start us, length us, event | category | flops | bytes accessed | tf_op | source)
XLA Modules:
  0.0 63.5 jit_solution(4440590094931039160)
XLA Ops:
  0.6 1.5 %shard_map.68 = (bf16[1472,128]{1,0:T(8,128)(2,1)S(1)}, bf16[1472,128]{1,0:T(8,128)(2,1)S(1)}) custom-call(s32[1]{0:T(128)} %bitcast.ens_ref, bf16[19136,128]{1,0:T(8,128)(2,1)} %bitcast.31), custom_call_target="tpu_custom_call" | custom-call | bytes 2260992 | tf_op jit(solution)/shard_map/pallas_call | solution.py:70
  2.1 0.1 collective-permute-start
  2.2 2.9 %shard_map.69 = (bf16[2576,128]{1,0:T(8,128)(2,1)}, bf16[2576,128]{1,0:T(8,128)(2,1)S(1)}, bf16[736,128]{1,0:T(8,128)(2,1)}, bf16[736,128]{1,0:T(8,128)(2,1)S(1)}) custom-call(s32[1]{0:T(128)} %bitcast.ens_ref, bf16[19136,128]{1,0:T(8,128)(2,1)} %bitcast.32), custom_call_target="tpu_custom_call" | custom-call | bytes 5087232 | tf_op jit(solution)/shard_map/pallas_call | solution.py:70
  5.1 0.7 %copy-done.4 = bf16[736,128]{1,0:T(8,128)(2,1)} copy-done((bf16[736,128]{1,0:T(8,128)(2,1)}, bf16[736,128]{1,0:T(8,128)(2,1)S(1)}, u32[]{:S(2)}) %copy-start.4) | copy-done | bytes 188440
  5.8 0.5 collective-permute-start.1
  6.3 0.0 collective-permute-start.2
  7.0 0.7 %fusion.3 = f32[46]{0:T(128)} fusion(), kind=kLoop, calls=%fused_computation.14 | loop fusion | flops 14766 | bytes 184 | tf_op jit(solution)/shard_map/reduce_sum | solution.py:208
  7.7 0.0 collective-permute-done.refs_1_
  7.7 0.9 %multiply_convert_fusion.1 = f16[1472,128]{1,0:T(8,128)(2,1)} fusion(bf16[1472,128]{1,0:T(8,128)(2,1)S(1)} %collective-permute-done.refs_1_, bf16[1472,128]{1,0:T(8,128)(2,1)S(1)} %get-tuple-element.38.refs_0_), kind=kLoop, calls=%fused_computation.2 | loop fusion | flops 942080 | bytes 1130496 | tf_op jit(solution)/shard_map/convert_element_type | solution.py:243
  8.6 3.0 %collective-permute-start.4 = (f16[1472,128]{1,0:T(8,128)(2,1)}, f16[1472,128]{1,0:T(8,128)(2,1)}, u32[]{:S(2)}, u32[]{:S(2)}) collective-permute-start(f16[1472,128]{1,0:T(8,128)(2,1)} %multiply_convert_fusion.1), channel_id=1, source_target_pairs={{0,128},{64,192},{128,0},{192,64},{1,129},{65,193},{129,1},{193,65... | collective-permute-start | bytes 1130504 | tf_op jit(solution)/shard_map/ppermute | solution.py:23
  11.6 3.6 %shard_map.70 = (bf16[4784,128]{1,0:T(8,128)(2,1)}, bf16[4784,128]{1,0:T(8,128)(2,1)S(1)}) custom-call(s32[1]{0:T(128)} %bitcast.ens_ref, bf16[19136,128]{1,0:T(8,128)(2,1)} %bitcast.33), custom_call_target="tpu_custom_call" | custom-call | bytes 7348224 | tf_op jit(solution)/shard_map/pallas_call | solution.py:70
  15.2 0.0 copy-start.8
  15.3 0.0 copy-start.9
  15.3 0.3 collective-permute-start.3
  15.6 0.0 collective-permute-done.1.refs_3_
  15.6 2.2 %multiply_convert_fusion = f16[2576,128]{1,0:T(8,128)(2,1)} fusion(bf16[2576,128]{1,0:T(8,128)(2,1)} %collective-permute-done.1.refs_3_, bf16[2576,128]{1,0:T(8,128)(2,1)S(1)} %get-tuple-element.41.refs_2_), kind=kLoop, calls=%fused_computation.1 | loop fusion | flops 1648640 | bytes 1978368 | tf_op jit(solution)/shard_map/convert_element_type | solution.py:243
  17.8 0.0 collective-permute-done.2.refs_5_
  17.8 1.7 %multiply_convert_fusion.2 = f16[736,128]{1,0:T(8,128)(2,1)} fusion(bf16[736,128]{1,0:T(8,128)(2,1)} %collective-permute-done.2.refs_5_, bf16[736,128]{1,0:T(8,128)(2,1)S(1)} %copy-done.5), kind=kLoop, calls=%fused_computation.6 | loop fusion | flops 471040 | bytes 565248 | tf_op jit(solution)/shard_map/convert_element_type | solution.py:243
  19.5 0.1 fusion.48
  19.5 0.6 fusion.47
  20.1 0.1 fusion.46
  20.2 0.1 fusion.45
  20.3 1.4 %add_add_fusion = (f32[104]{0:T(128)S(1)}, f32[104]{0:T(128)S(1)}, f32[104]{0:T(128)S(1)}, f32[104]{0:T(128)S(1)}, f32[104]{0:T(128)S(1)}) fusion(s32[104]{0:T(128)S(1)} %copy-done.8, s32[2]{0:T(128)S(1)} %get-tuple-element.81, s32[102]{0:T(128)S(1)} %get-tuple-element.83, s32[1]{0:T(128)} %get-tuple-element.85, s32[103]{0:T(128)S(1)} %get-tuple-element.87, ...), kind=kLoop, calls=%fused_computation.65 | loop fusion | flops 4992 | bytes 4160 | tf_op jit(solution)/shard_map/reduce_sum | solution.py:200
  21.7 0.1 copy.37
  21.8 0.6 collective-permute-start.8
  22.4 0.1 broadcast_divide_fusion
  22.5 0.1 convert_reduce_fusion.1
  22.6 0.9 %convert_reduce_fusion = f32[46,128]{1,0:T(8,128)S(1)} fusion(bf16[11,1,46,128]{3,2,1,0:T(8,128)(2,1)} %param.9), kind=kLoop, calls=%fused_computation.7 | loop fusion | flops 123648 | bytes 153088 | tf_op jit(solution)/shard_map/reduce_sum | solution.py:309
  23.5 0.9 %fusion.6.table_ref = f32[7,46]{1,0:T(8,128)S(1)} fusion(f32[46]{0:T(128)} %fusion.3, f32[7]{0:T(128)S(1)} %convert_reduce_fusion.1, s32[46]{0:T(128)S(1)} %copy-done.9), kind=kOutput, calls=%fused_computation.18 | convolution fusion | flops 193522 | bytes 1684 | tf_op jit(solution)/shard_map/dot_general | solution.py:294
  24.4 0.1 select_reduce_fusion.share_ref
  24.5 0.2 fusion.refs_6_
  24.7 1.0 %copy-done.1 = bf16[1472,128]{1,0:T(8,128)(2,1)S(1)} copy-done((bf16[1472,128]{1,0:T(8,128)(2,1)S(1)}, bf16[1472,128]{1,0:T(8,128)(2,1)}, u32[]{:S(2)}) %copy-start.1) | copy-done | bytes 376856
  25.7 0.9 %copy-done.6 = bf16[736,128]{1,0:T(8,128)(2,1)S(1)} copy-done((bf16[736,128]{1,0:T(8,128)(2,1)S(1)}, bf16[736,128]{1,0:T(8,128)(2,1)}, u32[]{:S(2)}) %copy-start.6) | copy-done | bytes 188440
  26.7 1.4 %shard_map.71 = f32[56,128]{1,0:T(8,128)S(1)} custom-call(f32[13]{0:T(128)S(1)} %select_reduce_fusion.share_ref, f32[7,46]{1,0:T(8,128)S(1)} %fusion.6.table_ref, bf16[1472,128]{1,0:T(8,128)(2,1)S(1)} %get-tuple-element.38.refs_0_, bf16[1472,128]{1,0:T(8,128)(2,1)S(1)} %copy-done.1, bf16[2576,128]{1,0:T(8,128)(2,1)S(1)} %get-tuple-element.41.refs_2_, ...), custom_call_target="tpu_custom_call" | custom-call | flops 1 | bytes 1 | tf_op jit(solution)/shard_map/pallas_call | solution.py:179
  28.1 3.1 %collective-permute-start.6 = (f16[2576,128]{1,0:T(8,128)(2,1)}, f16[2576,128]{1,0:T(8,128)(2,1)}, u32[]{:S(2)}, u32[]{:S(2)}) collective-permute-start(f16[2576,128]{1,0:T(8,128)(2,1)} %multiply_convert_fusion), channel_id=1, source_target_pairs={{0,128},{64,192},{128,0},{192,64},{1,129},{65,193},{129,1},{193,65... | collective-permute-start | bytes 1978376 | tf_op jit(solution)/shard_map/ppermute | solution.py:23
  31.2 0.9 %shard_map.72 = f32[56,128]{1,0:T(8,128)S(1)} custom-call(f32[13]{0:T(128)S(1)} %select_reduce_fusion.share_ref, f32[7,46]{1,0:T(8,128)S(1)} %fusion.6.table_ref, bf16[4784,128]{1,0:T(8,128)(2,1)S(1)} %get-tuple-element.45.refs_0_, bf16[4784,128]{1,0:T(8,128)(2,1)S(1)} %collective-permute-done.3.refs_1_), custom_call_target="tpu_custom_call" | custom-call | flops 1 | bytes 1 | tf_op jit(solution)/shard_map/pallas_call | solution.py:179
  32.1 0.7 %maximum_bitcast_fusion = f32[8,2,7,128]{3,1,2,0:T(2,128)} fusion(f32[1,7,8,128]{3,0,1,2:T(1,128)S(1)} %copy.39, f32[1,7,8,128]{3,0,1,2:T(1,128)S(1)} %copy.38), kind=kLoop, calls=%fused_computation.8 | loop fusion | flops 14336 | bytes 114688 | tf_op jit(solution)/shard_map/transpose | solution.py:304
  32.8 2.1 %multiply_add_fusion.2 = (f32[736,128]{1,0:T(8,128)S(1)}, f32[736,128]{1,0:T(8,128)}, f32[736,128]{1,0:T(8,128)}) fusion(f16[1472,128]{1,0:T(8,128)(2,1)} %collective-permute-done.4, bf16[4784,128]{1,0:T(8,128)(2,1)S(1)} %collective-permute-done.3.refs_1_, bf16[4784,128]{1,0:T(8,128)(2,1)S(1)} %get-tuple-element.45.refs_0_, ...), kind=kLoop, calls=%fused_computation.4 | loop fusion | flops 1695744 | bytes 2826240 | tf_op jit(solution)/shard_map/add | solution.py:272
  34.9 8.8 %all-to-all-start = ((f32[8,2,7,128]{3,1,2,0:T(2,128)}), f32[8,2,7,128]{3,1,2,0:T(2,128)S(1)}, u32[]{:S(2)}, u32[]{:S(2)}) async-start(f32[8,2,7,128]{3,1,2,0:T(2,128)} %maximum_bitcast_fusion), calls=%async_computation | async-start | bytes 114688 | tf_op jit(solution)/shard_map/all_to_all | solution.py:306
  43.7 0.7 %dynamic-slice_multiply_fusion.weight_ref = f32[13,5]{1,0:T(8,128)S(1)} fusion(f32[104,5]{1,0:T(8,128)} %copy-done.7, s32[]{:T(128)S(6)} %select_n.56), kind=kLoop, calls=%fused_computation.27 | loop fusion | flops 65 | bytes 524 | tf_op jit(solution)/shard_map/mul | solution.py:282
  44.4 3.2 %collective-permute-start.7 = (f32[736,128]{1,0:T(8,128)S(1)}, f32[736,128]{1,0:T(8,128)}, u32[]{:S(2)}, u32[]{:S(2)}) collective-permute-start(f32[736,128]{1,0:T(8,128)S(1)} %get-tuple-element.50.refs_1_), channel_id=1, source_target_pairs={{0,56},{8,0},{16,8},{24,16},{32,24},{40,32},{48,40},{56,48},{1,57}... | collective-permute-start | bytes 1130504 | tf_op jit(solution)/shard_map/ppermute | solution.py:28
  47.6 0.0 collective-permute-start.5
  47.6 4.5 %all-to-all-done = f32[8,2,7,128]{3,1,2,0:T(2,128)S(1)} async-done(((f32[8,2,7,128]{3,1,2,0:T(2,128)}), f32[8,2,7,128]{3,1,2,0:T(2,128)S(1)}, u32[]{:S(2)}, u32[]{:S(2)}) %all-to-all-start) | async-done | bytes 57376 | tf_op jit(solution)/shard_map/all_to_all | solution.py:306
  52.1 0.6 collective-permute-start.9
  52.7 1.3 %multiply_add_fusion.refs_2_ = f32[2576,128]{1,0:T(8,128)S(1)} fusion(f16[2576,128]{1,0:T(8,128)(2,1)} %collective-permute-done.6, bf16[4784,128]{1,0:T(8,128)(2,1)S(1)} %collective-permute-done.3.refs_1_, bf16[4784,128]{1,0:T(8,128)(2,1)S(1)} %get-tuple-element.45.refs_0_), kind=kLoop, calls=%fused_computation | loop fusion | flops 1978368 | bytes 3297280 | tf_op jit(solution)/shard_map/add | solution.py:272
  54.1 4.6 %collective-permute-done.5.refs_0_ = f32[736,128]{1,0:T(8,128)S(1)} collective-permute-done((f32[736,128]{1,0:T(8,128)}, f32[736,128]{1,0:T(8,128)S(1)}, u32[]{:S(2)}, u32[]{:S(2)}) %collective-permute-start.5) | collective-permute-done | bytes 376864 | tf_op jit(solution)/shard_map/ppermute | solution.py:28
  58.7 2.0 %shard_map.73.refs_9_ = f32[13,368,128]{2,1,0:T(8,128)} custom-call(f32[13,5]{1,0:T(8,128)S(1)} %dynamic-slice_multiply_fusion.weight_ref, f32[736,128]{1,0:T(8,128)S(1)} %collective-permute-done.5.refs_0_, f32[736,128]{1,0:T(8,128)S(1)} %get-tuple-element.50.refs_1_, f32[2576,128]{1,0:T(8,128)S(1)} %multiply_add_fusion.refs_2_), custom_call_target="tpu_custom_call" | custom-call | flops 1 | bytes 1 | tf_op jit(solution)/shard_map/pallas_call | solution.py:140
  60.7 2.8 %shard_map.74 = (f32[13,368,128]{2,1,0:T(8,128)}, f32[7,1,128]{2,1,0:T(1,128)}) custom-call(f32[13,5]{1,0:T(8,128)S(1)} %dynamic-slice_multiply_fusion.weight_ref, f32[736,128]{1,0:T(8,128)S(1)} %collective-permute-done.5.refs_0_, f32[736,128]{1,0:T(8,128)S(1)} %get-tuple-element.50.refs_1_, ...), custom_call_target="tpu_custom_call", output_to_operand_aliasing={{0}: (10, {})} | custom-call | flops 1 | bytes 1 | tf_op jit(solution)/shard_map/pallas_call | solution.py:140
  (30 shorter events, 0.2 us)
Async XLA Ops:
  2.1 5.6 %collective-permute-start = (bf16[1472,128]{1,0:T(8,128)(2,1)S(1)}, bf16[1472,128]{1,0:T(8,128)(2,1)S(1)}, u32[]{:S(2)}, u32[]{:S(2)}) collective-permute-start(bf16[1472,128]{1,0:T(8,128)(2,1)S(1)} %get-tuple-element.30), channel_id=1, source_target_pairs={{0,64},{64,0},{128,192},{192,128},{1,65},{65,1},{129,193},{193,129... | collective-permute-start | bytes 1130504 | tf_op jit(solution)/shard_map/ppermute | solution.py:19
  5.1 0.7 %copy-start.4 = (bf16[736,128]{1,0:T(8,128)(2,1)}, bf16[736,128]{1,0:T(8,128)(2,1)S(1)}, u32[]{:S(2)}) copy-start(bf16[736,128]{1,0:T(8,128)(2,1)S(1)} %get-tuple-element.42.refs_4_) | copy-start | bytes 565252
  5.8 9.8 %collective-permute-start.1 = (bf16[2576,128]{1,0:T(8,128)(2,1)}, bf16[2576,128]{1,0:T(8,128)(2,1)}, u32[]{:S(2)}, u32[]{:S(2)}) collective-permute-start(bf16[2576,128]{1,0:T(8,128)(2,1)} %get-tuple-element.35), channel_id=1, source_target_pairs={{0,64},{64,0},{128,192},{192,128},{1,65},{65,1},{129,193},{193,129... | collective-permute-start | bytes 1978376 | tf_op jit(solution)/shard_map/ppermute | solution.py:19
  6.3 11.5 %collective-permute-start.2 = (bf16[736,128]{1,0:T(8,128)(2,1)}, bf16[736,128]{1,0:T(8,128)(2,1)}, u32[]{:S(2)}, u32[]{:S(2)}) collective-permute-start(bf16[736,128]{1,0:T(8,128)(2,1)} %get-tuple-element.43), channel_id=1, source_target_pairs={{0,64},{64,0},{128,192},{192,128},{1,65},{65,1},{129,193},{193,129... | collective-permute-start | bytes 565256 | tf_op jit(solution)/shard_map/ppermute | solution.py:19
  7.7 0.9 %copy-start = (bf16[1472,128]{1,0:T(8,128)(2,1)}, bf16[1472,128]{1,0:T(8,128)(2,1)S(1)}, u32[]{:S(2)}) copy-start(bf16[1472,128]{1,0:T(8,128)(2,1)S(1)} %collective-permute-done.refs_1_) | copy-start | bytes 1130500
  8.6 24.2 %collective-permute-start.4 = (f16[1472,128]{1,0:T(8,128)(2,1)}, f16[1472,128]{1,0:T(8,128)(2,1)}, u32[]{:S(2)}, u32[]{:S(2)}) collective-permute-start(f16[1472,128]{1,0:T(8,128)(2,1)} %multiply_convert_fusion.1), channel_id=1, source_target_pairs={{0,128},{64,192},{128,0},{192,64},{1,129},{65,193},{129,1},{193,65... | collective-permute-start | bytes 1130504 | tf_op jit(solution)/shard_map/ppermute | solution.py:23
  15.2 2.5 %copy-start.5 = (bf16[736,128]{1,0:T(8,128)(2,1)S(1)}, bf16[736,128]{1,0:T(8,128)(2,1)}, u32[]{:S(2)}) copy-start(bf16[736,128]{1,0:T(8,128)(2,1)} %copy-done.4) | copy-start | bytes 565252
  15.2 4.2 %copy-start.8 = (s32[104]{0:T(128)S(1)}, s32[104]{0:T(128)}, u32[]{:S(2)}) copy-start(s32[104]{0:T(128)} %param.6) | copy-start | bytes 1252
  15.3 7.2 %copy-start.9 = (s32[46]{0:T(128)S(1)}, s32[46]{0:T(128)}, u32[]{:S(2)}) copy-start(s32[46]{0:T(128)} %param.8) | copy-start | bytes 556
  15.3 15.9 %collective-permute-start.3 = (bf16[4784,128]{1,0:T(8,128)(2,1)}, bf16[4784,128]{1,0:T(8,128)(2,1)S(1)}, u32[]{:S(2)}, u32[]{:S(2)}) collective-permute-start(bf16[4784,128]{1,0:T(8,128)(2,1)} %get-tuple-element.46), channel_id=1, source_target_pairs={{0,64},{64,0},{128,192},{192,128},{1,65},{65,1},{129,193},{193,129... | collective-permute-start | bytes 3674120 | tf_op jit(solution)/shard_map/ppermute | solution.py:19
  21.8 11.0 %collective-permute-start.8 = (f16[736,128]{1,0:T(8,128)(2,1)}, f16[736,128]{1,0:T(8,128)(2,1)S(1)}, u32[]{:S(2)}, u32[]{:S(2)}) collective-permute-start(f16[736,128]{1,0:T(8,128)(2,1)} %multiply_convert_fusion.2), channel_id=1, source_target_pairs={{0,128},{64,192},{128,0},{192,64},{1,129},{65,193},{129,1},{193,65... | collective-permute-start | bytes 565256 | tf_op jit(solution)/shard_map/ppermute | solution.py:23
  22.4 2.1 %copy-start.7 = (f32[104,5]{1,0:T(8,128)}, f32[104,5]{1,0:T(8,128)S(1)}, u32[]{:S(2)}) copy-start(f32[104,5]{1,0:T(8,128)S(1)} %broadcast_divide_fusion) | copy-start | bytes 6244
  24.7 1.0 %copy-start.1 = (bf16[1472,128]{1,0:T(8,128)(2,1)S(1)}, bf16[1472,128]{1,0:T(8,128)(2,1)}, u32[]{:S(2)}) copy-start(bf16[1472,128]{1,0:T(8,128)(2,1)} %copy-done) | copy-start | bytes 1130500
  25.7 0.9 %copy-start.6 = (bf16[736,128]{1,0:T(8,128)(2,1)S(1)}, bf16[736,128]{1,0:T(8,128)(2,1)}, u32[]{:S(2)}) copy-start(bf16[736,128]{1,0:T(8,128)(2,1)} %copy-done.4) | copy-start | bytes 565252
  28.1 24.6 %collective-permute-start.6 = (f16[2576,128]{1,0:T(8,128)(2,1)}, f16[2576,128]{1,0:T(8,128)(2,1)}, u32[]{:S(2)}, u32[]{:S(2)}) collective-permute-start(f16[2576,128]{1,0:T(8,128)(2,1)} %multiply_convert_fusion), channel_id=1, source_target_pairs={{0,128},{64,192},{128,0},{192,64},{1,129},{65,193},{129,1},{193,65... | collective-permute-start | bytes 1978376 | tf_op jit(solution)/shard_map/ppermute | solution.py:23
  34.9 17.2 %all-to-all-start = ((f32[8,2,7,128]{3,1,2,0:T(2,128)}), f32[8,2,7,128]{3,1,2,0:T(2,128)S(1)}, u32[]{:S(2)}, u32[]{:S(2)}) async-start(f32[8,2,7,128]{3,1,2,0:T(2,128)} %maximum_bitcast_fusion), calls=%async_computation | async-start | bytes 114688 | tf_op jit(solution)/shard_map/all_to_all | solution.py:306
  44.4 16.3 %collective-permute-start.7 = (f32[736,128]{1,0:T(8,128)S(1)}, f32[736,128]{1,0:T(8,128)}, u32[]{:S(2)}, u32[]{:S(2)}) collective-permute-start(f32[736,128]{1,0:T(8,128)S(1)} %get-tuple-element.50.refs_1_), channel_id=1, source_target_pairs={{0,56},{8,0},{16,8},{24,16},{32,24},{40,32},{48,40},{56,48},{1,57}... | collective-permute-start | bytes 1130504 | tf_op jit(solution)/shard_map/ppermute | solution.py:28
  47.6 11.1 %collective-permute-start.5 = (f32[736,128]{1,0:T(8,128)}, f32[736,128]{1,0:T(8,128)S(1)}, u32[]{:S(2)}, u32[]{:S(2)}) collective-permute-start(f32[736,128]{1,0:T(8,128)} %get-tuple-element.52.refs_3_), channel_id=1, source_target_pairs={{0,8},{8,16},{16,24},{24,32},{32,40},{40,48},{48,56},{56,0},{1,9},... | collective-permute-start | bytes 1130504 | tf_op jit(solution)/shard_map/ppermute | solution.py:28
  52.1 8.6 %collective-permute-start.9 = (f32[7,128]{1,0:T(8,128)S(1)}, f32[7,128]{1,0:T(8,128)S(1)}, u32[]{:S(2)}, u32[]{:S(2)}) collective-permute-start(f32[7,128]{1,0:T(8,128)S(1)} %get-tuple-element.78), channel_id=1, source_target_pairs={{0,128},{64,192},{128,0},{192,64},{1,129},{65,193},{129,1},{193,65... | collective-permute-start | bytes 10760 | tf_op jit(solution)/shard_map/ppermute | solution.py:23
  54.1 6.6 %copy-start.2 = (f32[736,128]{1,0:T(8,128)S(1)}, f32[736,128]{1,0:T(8,128)}, u32[]{:S(2)}) copy-start(f32[736,128]{1,0:T(8,128)} %get-tuple-element.52.refs_3_) | copy-start | bytes 1130500
  54.1 6.6 %copy-start.3 = (f32[736,128]{1,0:T(8,128)S(1)}, f32[736,128]{1,0:T(8,128)}, u32[]{:S(2)}) copy-start(f32[736,128]{1,0:T(8,128)} %get-tuple-element.77.refs_5_) | copy-start | bytes 1130500

commit v4 on v0

v4 whole, which is shorter than its diff:
```python
import functools

import jax
import jax.numpy as jnp
from jax import lax
from jax.experimental import pallas as pl
from jax.experimental.pallas import tpu as pltpu
from jax.sharding import PartitionSpec as P

WEEKS = 7
LANES = 128
TILE = 8
SCALE = 512.0
MIB = 1024 * 1024
SMEM = pl.BlockSpec(memory_space=pltpu.SMEM)
VMEM = pl.BlockSpec(memory_space=pltpu.VMEM)
HBM = pl.BlockSpec(memory_space=pltpu.HBM)


def estimate(num_bytes):
    return pl.CostEstimate(flops=1, transcendentals=0, bytes_accessed=num_bytes)


def core_swap(block):
    return lax.ppermute(block, "ens", [(0, 1), (1, 0), (2, 3), (3, 2)])


def chip_swap(block):
    return lax.ppermute(block, "ens", [(0, 2), (1, 3), (2, 0), (3, 1)])


def date_shift(block, step):
    count = lax.axis_size("date")
    return lax.ppermute(block, "date", [(i, (i + step) % count) for i in range(count)])


def split_kernel(kinds, leads, rows, wanted, ens_ref, runs_ref, *rest):
    outs, (held, wide, sem) = rest[:-3], rest[-3:]
    block = leads * TILE
    copies = []
    for slot, row in enumerate(rows):
        copy = pltpu.make_async_copy(
            runs_ref.at[pl.ds(row * block * kinds, block * kinds)], held.at[slot], sem.at[slot]
        )
        copy.start()
        copies.append(copy)
    ens = ens_ref[0]
    core, half = ens % 2, ens // 2
    for slot, row in enumerate(rows):
        copies[slot].wait()
        spread = wide.at[slot % 2]
        spread[...] = held[slot].astype(jnp.float32)
        for out, (members, other_half, other_core) in zip(outs, wanted):
            if row not in members:
                continue
            kind = 2 * (1 - half if other_half else half) + (1 - core if other_core else core)
            start = members.index(row) * block
            for lead in range(0, leads, 2):
                picked = spread[pl.ds(lead * TILE * kinds + kind, 2 * TILE, stride=kinds), :]
                out[start + lead * TILE : start + (lead + 2) * TILE, :] = picked.astype(
                    jnp.bfloat16
                )


def split_kinds(flat, ens, kinds, leads, rows, wanted):
    block = leads * TILE
    shapes = [pltpu.VMEM((len(members) * block, LANES), jnp.bfloat16) for members, _, _ in wanted]
    outs = pl.pallas_call(
        functools.partial(split_kernel, kinds, leads, rows, wanted),
        in_specs=[SMEM, HBM],
        out_specs=[VMEM] * len(shapes),
        scratch_shapes=[
            pltpu.VMEM((len(rows), block * kinds, LANES), jnp.bfloat16),
            pltpu.VMEM((2, block * kinds, LANES), jnp.float32),
            pltpu.SemaphoreType.DMA((len(rows),)),
        ],
        out_shape=shapes,
        cost_estimate=estimate(len(rows) * block * LANES * 2 * kinds),
        compiler_params=pltpu.CompilerParams(vmem_limit_bytes=10 * MIB),
    )(ens, pltpu.with_memory_space_constraint(flat, pltpu.HBM))
    return list(outs)


def wrapped(index, count):
    index = jnp.where(index < 0, index + count, index)
    return jnp.where(index >= count, index - count, index)


def neighbour_weights(days_ref, date, cycle_days):
    count = days_ref.shape[0]
    weights = []
    for k in range(-2, 3):
        other = days_ref[wrapped(date + k, count)]
        gap = other - days_ref[date] if k >= 0 else days_ref[date] - other
        gap = jnp.where(gap < 0, gap + cycle_days, gap)
        weights.append(jnp.maximum(8 - gap, 0).astype(jnp.float32))
    total = weights[0] + weights[1] + weights[2] + weights[3] + weights[4]
    return weights, 1.0 / jnp.full((TILE, LANES), total, jnp.float32)


def smoothed_leads(leads, value):
    before, here = None, value(0)
    for lead in range(leads):
        after = value(lead + 1) if lead + 1 < leads else None
        total = here + here
        for beside in (before, after):
            if beside is not None:
                total = total + beside
        yield lead, total * (1.0 / 3.0 if before is None or after is None else 0.25)
        before, here = here, after


def smooth_kernel(leads, places, rows, members, cycle_days, date_ref, days_ref, *refs):
    sums, (forecast, kept, given, out_hbm, anomalies, done, sem) = refs[:-7], refs[-7:]

    def tile(row, lead):
        which, place = places[row]
        start = (place * leads + lead) * TILE
        return sums[which][start : start + TILE, :]

    copies = []
    for row in range(rows):
        weights, inverse = neighbour_weights(days_ref, date_ref[0] * rows + row, cycle_days)
        inverse = inverse * (1.0 / members)

        def mean(lead):
            value = weights[0] * tile(row - 2, lead)
            for k in range(1, 5):
                value = value + weights[k] * tile(row - 2 + k, lead)
            return value * inverse

        for lead, value in smoothed_leads(leads, mean):
            done[row, lead * TILE : (lead + 1) * TILE, :] = value
        copy = pltpu.make_async_copy(done.at[row], out_hbm.at[row], sem.at[row])
        copy.start()
        copies.append(copy)
    anomalies[:, 0, :] = forecast[...] - (kept[WEEKS:, :] + given[...])
    for copy in copies:
        copy.wait()


def smooth_rows(date, days, sums, extra, places, rows, leads, members, cycle_days):
    return pl.pallas_call(
        functools.partial(smooth_kernel, leads, places, rows, members, cycle_days),
        in_specs=[SMEM, SMEM] + [VMEM] * (len(sums) + len(extra)),
        out_specs=[HBM, VMEM],
        out_shape=[
            jax.ShapeDtypeStruct((rows, leads * TILE, LANES), jnp.float32),
            jax.ShapeDtypeStruct((WEEKS, 1, LANES), jnp.float32),
        ],
        scratch_shapes=[
            pltpu.VMEM((rows, leads * TILE, LANES), jnp.float32),
            pltpu.SemaphoreType.DMA((rows,)),
        ],
        cost_estimate=estimate(1),
        compiler_params=pltpu.CompilerParams(vmem_limit_bytes=10 * MIB),
    )(date, days, *sums, *extra)


def weekly_kernel(
    kinds, leads, rows, members, cycle_days, ens_ref, date_ref, days_ref, position_ref, bins_ref, *refs
):
    forecast_ref, runs_ref, *outs, climate, held, sem, weekly, means, counts = refs
    block = leads * TILE * kinds
    group = TILE * kinds
    position = position_ref[0]
    dates = days_ref.shape[0]
    weights, inverse = neighbour_weights(days_ref, position, cycle_days)
    inverse = inverse * (1.0 / members)
    for week in range(WEEKS):
        counts[week] = 0
    for lead in range(leads):
        counts[bins_ref[lead]] += 1

    row_of = [wrapped(position + k - 2, dates) - date_ref[0] * rows for k in range(5)]
    here = [(row >= 0) & (row < rows) for row in row_of]

    def copy_of(k):
        start = pl.multiple_of(row_of[k] * block, 16)
        return pltpu.make_async_copy(runs_ref.at[pl.ds(start, block)], held.at[k], sem.at[k])

    for k in range(5):

        @pl.when(here[k])
        def _():
            copy_of(k).start()

    total = forecast_ref[0].astype(jnp.float32)
    for run in range(1, forecast_ref.shape[0]):
        total = total + forecast_ref[run].astype(jnp.float32)
    climate[:leads, :] = total
    means[...] = jnp.zeros_like(means)
    for lead in range(leads):
        means[pl.ds(bins_ref[lead], 1), :] += climate[lead : lead + 1, :]
    for week in range(WEEKS):
        count = jnp.full((1, LANES), (counts[week] * forecast_ref.shape[0]).astype(jnp.float32))
        outs[1][week : week + 1, :] = means[week : week + 1, :] / count

    climate[...] = jnp.zeros_like(climate)
    weekly[...] = jnp.zeros_like(weekly)
    for k in range(5):

        @pl.when(here[k])
        def _():
            copy_of(k).wait()
            climate[...] += weights[k] * held[k].astype(jnp.float32)

    @pl.when(here[0] | here[1] | here[2] | here[3] | here[4])
    def _():
        def part(lead):
            return climate[lead * group : (lead + 1) * group, :]

        for lead, value in smoothed_leads(leads, part):
            span = pl.ds(pl.multiple_of(bins_ref[lead] * group, group), group)
            weekly[span, :] += value

    core, half = ens_ref[0] % 2, ens_ref[0] // 2
    order = [(1 - half, 1 - core), (half, 1 - core), (1 - half, core), (half, core)]
    for week in range(WEEKS):
        scale = inverse / jnp.full((TILE, LANES), counts[week].astype(jnp.float32))
        for role, (of_half, of_core) in enumerate(order):
            kind = 2 * of_half + of_core
            mean = weekly[pl.ds(week * group + kind, TILE, stride=kinds), :] * scale
            for slot in range(TILE):
                outs[0][slot, role * WEEKS + week, :] = mean[slot]


def weekly_means(ens, date, days, position, bins, forecast, flat, kinds, leads, rows, members, cycle_days):
    return pl.pallas_call(
        functools.partial(weekly_kernel, kinds, leads, rows, members, cycle_days),
        in_specs=[SMEM] * 5 + [VMEM, HBM],
        out_specs=[VMEM, VMEM],
        out_shape=[
            jax.ShapeDtypeStruct((TILE, kinds * WEEKS, LANES), jnp.float32),
            jax.ShapeDtypeStruct((WEEKS, LANES), jnp.float32),
        ],
        scratch_shapes=[
            pltpu.VMEM((leads * TILE * kinds, LANES), jnp.float32),
            pltpu.VMEM((5, leads * TILE * kinds, LANES), jnp.bfloat16),
            pltpu.SemaphoreType.DMA((5,)),
            pltpu.VMEM((WEEKS * TILE * kinds, LANES), jnp.float32),
            pltpu.VMEM((TILE, LANES), jnp.float32),
            pltpu.SMEM((WEEKS,), jnp.int32),
        ],
        cost_estimate=estimate(1),
        compiler_params=pltpu.CompilerParams(vmem_limit_bytes=10 * MIB),
    )(ens, date, days, position, bins, forecast, pltpu.with_memory_space_constraint(flat, pltpu.HBM))


def per_device(
    hindcast_runs,
    init_calendar_ordinal,
    prediction_init_position,
    horizon_sevenfold_bin,
    prediction_runs,
):
    _, rows, kinds, leads, cells = hindcast_runs.shape
    dates = rows * lax.axis_size("date")
    members = lax.axis_size("ens")
    cycle_days = 7 * dates // 2
    block = leads * TILE
    ens = lax.axis_index("ens").astype(jnp.int32).reshape(1)
    date = lax.axis_index("date").astype(jnp.int32).reshape(1)

    flat = hindcast_runs.reshape(rows, kinds, leads, TILE, LANES)
    flat = flat.transpose(0, 2, 3, 1, 4).reshape(rows * leads * TILE * kinds, LANES)

    chunks = [[0, 1, 2, rows - 2, rows - 1], list(range(3, rows - 2))]
    split = functools.partial(split_kinds, kinds=kinds, leads=leads)
    edge, inner, every = chunks[0], chunks[1], list(range(rows))

    def pair_sum(mine, other):
        return ((mine.astype(jnp.float32) + other.astype(jnp.float32)) * SCALE).astype(jnp.float16)

    theirs_0, mine_0 = split(flat, ens, rows=edge, wanted=[(edge, True, True), (edge, True, False)])
    got_0 = core_swap(theirs_0)
    flat, mine_0 = lax.optimization_barrier((flat, mine_0))
    theirs_1, mine_1, theirs, own = split(
        flat,
        ens,
        rows=inner + edge,
        wanted=[
            (inner, True, True),
            (inner, True, False),
            (every, False, True),
            (every, False, False),
        ],
    )
    got_1 = core_swap(theirs_1)
    own_got = core_swap(theirs)
    mine_0, mine_1 = lax.optimization_barrier((mine_0, mine_1))
    packed_0 = pair_sum(mine_0, got_0)
    mine_1, packed_0 = lax.optimization_barrier((mine_1, packed_0))
    packed_1 = pair_sum(mine_1, got_1)
    flat, packed_1 = lax.optimization_barrier((flat, packed_1))
    arrived_0 = chip_swap(packed_0)
    arrived_1 = chip_swap(packed_1)

    def local_sum(first, count, packed):
        span = slice(first * block, (first + count) * block)
        pair = own[span].astype(jnp.float32) + own_got[span].astype(jnp.float32)
        return pair + packed.astype(jnp.float32) * (1.0 / SCALE)

    low = local_sum(0, 2, arrived_0[: 2 * block])
    high = local_sum(rows - 2, 2, arrived_0[-2 * block :])
    below = date_shift(high, 1)
    above = date_shift(low, -1)
    third = local_sum(2, 1, arrived_0[2 * block : 3 * block])
    middle = local_sum(inner[0], len(inner), arrived_1)

    weekly, forecast = weekly_means(
        ens,
        date,
        init_calendar_ordinal,
        prediction_init_position,
        horizon_sevenfold_bin,
        prediction_runs[:, 0],
        flat,
        kinds,
        leads,
        rows,
        members,
        cycle_days,
    )
    weekly = jnp.sum(lax.all_to_all(weekly, "date", split_axis=0, concat_axis=0, tiled=True), 0)
    weekly = weekly[2 * WEEKS :] + core_swap(weekly[: 2 * WEEKS])
    given = chip_swap(weekly[:WEEKS])

    places = {-2: (0, 0), -1: (0, 1), 0: (1, 0), 1: (1, 1)}
    places |= {2: (5, 0)} | {row: (2, i) for i, row in enumerate(inner)}
    places |= {rows - 2: (3, 0), rows - 1: (3, 1), rows: (4, 0), rows + 1: (4, 1)}
    smoothed, anomalies = smooth_rows(
        date,
        init_calendar_ordinal,
        [below, low, middle, high, above, third],
        [forecast, weekly, given],
        places,
        rows,
        leads,
        members,
        cycle_days,
    )
    return smoothed.reshape(rows, 1, leads, cells), anomalies


def solution(mesh):
    return jax.shard_map(
        per_device,
        mesh=mesh,
        in_specs=(
            P("ens", "date", None, None, "pix"),
            P(),
            P(),
            P(),
            P(None, "ens", None, ("pix", "date")),
        ),
        out_specs=(P("date", "ens", None, "pix"), P(None, "ens", ("pix", "date"))),
        check_vma=False,
    )
```

time: 401 us -> 53.7 us (0.13)
  waiting for transfers between devices: 169 us -> 17.4 us
  local copies, waits for them, and re-layouts: 139 us -> 0.03 us
  blocking collectives: 63.7 us -> 0 us
  Pallas kernels: 0 us -> 12.7 us
  other arithmetic: 11.9 us -> 7.24 us
    all_to_all x2 -> x1, waiting for transfers between devices: 169 us -> 8.87 us  [per_device(): lax.all_to_all(weekly, 'date', split_axis=0, concat_axis=0, tiled=True)]
    unnamed x12 -> x6, local copies, waits for them, and re-layouts: 87.3 us -> 0.02 us
    all_to_all x1 -> x0, blocking collectives: 63.7 us -> none  [per_device(): lax.all_to_all(hindcast_runs, 'ens', split_axis=2, concat_axis=0, tiled=T...]
    all_to_all x3 -> x0, local copies, waits for them, and re-layouts: 42.9 us -> none  [the longest x1 21.4 us: per_device(): lax.all_to_all(lax.all_to_all(hindcast_runs, 'ens', split_axis=2, concat_...]
    pallas_call x0 -> x4, Pallas kernels: none -> 12.7 us  [the longest x2 6.24 us: split_kinds(): pl.pallas_call(functools.partial(split_kernel, kinds, leads, rows, wanted...]
    reduce_sum x3 -> x1, other arithmetic: 8.85 us -> 0.01 us  [per_device(): jnp.sum(lax.all_to_all(weekly, 'date', split_axis=0, concat_axis=0, tiled...]
    ppermute x0 -> x9, waiting for transfers between devices: none -> 8.55 us  [the longest x3 4.45 us: chip_swap(): return lax.ppermute(block, 'ens', [(0, 2), (1, 3), (2, 0), (3, 1)])]
    ppermute x0 -> x9, starting transfers between devices: none -> 7.08 us  [the longest x3 4.12 us: chip_swap(): return lax.ppermute(block, 'ens', [(0, 2), (1, 3), (2, 0), (3, 1)])]
  transfers between devices with their start and end apart: 2 -> 10, of which waited for: 2 -> 5; matrix products, arithmetic and copies ran while one was open for 0% -> 14% of each run, Pallas kernels for 0% -> 14%
where the time goes in v4:
time: 53.7 us; the launch traced here: 52.7 us
  waiting for transfers between devices  17.4 us (32%)
  starting transfers between devices  13.9 us (26%)
  Pallas kernels  12.7 us (24%)
  other arithmetic  7.24 us (13%)
  between operations  1.43 us (3%)
    all_to_all x1, waiting for transfers between devices, per_device(): lax.all_to_all(weekly, 'date', split_axis=0, concat_axis=0, tiled=True)  8.87 us
    all_to_all x1, starting transfers between devices, per_device(): lax.all_to_all(weekly, 'date', split_axis=0, concat_axis=0, tiled=True)  6.79 us
    pallas_call x2, Pallas kernels, split_kinds(): pl.pallas_call(functools.partial(split_kernel, kinds, leads, rows, wanted...  6.24 us
    ppermute x3, waiting for transfers between devices, chip_swap(): return lax.ppermute(block, 'ens', [(0, 2), (1, 3), (2, 0), (3, 1)])  4.45 us
    ppermute x3, starting transfers between devices, chip_swap(): return lax.ppermute(block, 'ens', [(0, 2), (1, 3), (2, 0), (3, 1)])  4.12 us
    add x3, other arithmetic, local_sum(): return pair + packed.astype(jnp.float32) * (1.0 / SCALE)  3.75 us
    convert_element_type x2, other arithmetic, pair_sum(): ((mine.astype(jnp.float32) + other.astype(jnp.float32)) * SCALE).astype(j...  3.48 us
    pallas_call x1, Pallas kernels, weekly_means(): pl.pallas_call(functools.partial(weekly_kernel, kinds, leads, rows, membe...  3.36 us
  transfers between devices with their start and end apart: 10, of which 5 were waited for; matrix products, arithmetic and copies ran while one was open for 14% of the time, Pallas kernels for 14%

profile of v4, /device:TPU:8, one launch (start us, length us, event | category | flops | bytes accessed | tf_op | source)
XLA Modules:
  0.0 52.7 jit_solution(2011721788895036882)
XLA Ops:
  0.6 2.4 %shard_map.68 = (bf16[1840,128]{1,0:T(8,128)(2,1)}, bf16[1840,128]{1,0:T(8,128)(2,1)S(1)}) custom-call(s32[1]{0:T(128)} %bitcast.1.ens_ref, bf16[19136,128]{1,0:T(8,128)(2,1)} %bitcast.10), custom_call_target="tpu_custom_call" | custom-call | flops 1 | bytes 1884160 | tf_op jit(solution)/shard_map/pallas_call | solution.py:68
  3.0 0.1 collective-permute-start.1
  3.1 3.9 %shard_map.69 = (bf16[2944,128]{1,0:T(8,128)(2,1)S(1)}, bf16[2944,128]{1,0:T(8,128)(2,1)S(1)}, bf16[4784,128]{1,0:T(8,128)(2,1)}, bf16[4784,128]{1,0:T(8,128)(2,1)S(1)}) custom-call(s32[1]{0:T(128)} %bitcast.1.ens_ref, bf16[19136,128]{1,0:T(8,128)(2,1)} %bitcast.11), custom_call_target="tpu_custom_call" | custom-call | flops 1 | bytes 4898816 | tf_op jit(solution)/shard_map/pallas_call | solution.py:68
  7.0 0.6 %collective-permute-start.4 = (bf16[2944,128]{1,0:T(8,128)(2,1)S(1)}, bf16[2944,128]{1,0:T(8,128)(2,1)}, u32[]{:S(2)}, u32[]{:S(2)}) collective-permute-start(bf16[2944,128]{1,0:T(8,128)(2,1)S(1)} %get-tuple-element.31), channel_id=1, source_target_pairs={{0,64},{64,0},{128,192},{192,128},{1,65},{65,1},{129,193},{193,129... | collective-permute-start | bytes 2261000 | tf_op jit(solution)/shard_map/ppermute | solution.py:25
  7.6 0.1 collective-permute-start
  8.3 0.0 copy-start
  8.3 0.0 copy-start.1
  8.3 0.0 copy-start.2
  8.4 0.0 collective-permute-done.1
  8.4 2.1 %multiply_convert_fusion.1 = f16[1840,128]{1,0:T(8,128)(2,1)} fusion(bf16[1840,128]{1,0:T(8,128)(2,1)} %collective-permute-done.1, bf16[1840,128]{1,0:T(8,128)(2,1)S(1)} %get-tuple-element.27), kind=kLoop, calls=%fused_computation.2 | loop fusion | flops 1177600 | bytes 1413120 | tf_op jit(solution)/shard_map/convert_element_type | solution.py:273
  10.4 3.0 %collective-permute-start.2 = (f16[1840,128]{1,0:T(8,128)(2,1)}, f16[1840,128]{1,0:T(8,128)(2,1)}, u32[]{:S(2)}, u32[]{:S(2)}) collective-permute-start(f16[1840,128]{1,0:T(8,128)(2,1)} %multiply_convert_fusion.1), channel_id=1, source_target_pairs={{0,128},{64,192},{128,0},{192,64},{1,129},{65,193},{129,1},{193,65... | collective-permute-start | bytes 1413128 | tf_op jit(solution)/shard_map/ppermute | solution.py:29
  13.5 0.0 collective-permute-done.4
  13.5 1.4 %multiply_convert_fusion = f16[2944,128]{1,0:T(8,128)(2,1)S(1)} fusion(bf16[2944,128]{1,0:T(8,128)(2,1)} %collective-permute-done.4, bf16[2944,128]{1,0:T(8,128)(2,1)S(1)} %get-tuple-element.30), kind=kLoop, calls=%fused_computation.1 | loop fusion | flops 1884160 | bytes 2260992 | tf_op jit(solution)/shard_map/convert_element_type | solution.py:273
  14.9 0.0 copy-done
  14.9 0.0 copy-done.1
  14.9 0.0 copy-done.2
  14.9 3.4 %shard_map.70 = (f32[8,28,128]{2,1,0:T(8,128)}, f32[7,128]{1,0:T(8,128)S(1)}) custom-call(s32[1]{0:T(128)} %bitcast.1.ens_ref, s32[1]{0:T(128)} %bitcast.date_ref, s32[104]{0:T(128)S(1)} %copy-done.1, s32[1]{0:T(128)S(6)} %copy.11.position_ref, s32[46]{0:T(128)S(1)} %copy-done.2, bf16[11,46,128]{2,1,0:T(8,128)(2,1)S(1)} %bitcast.9, bf16[19136,128]{1,0:T(8,128)(2,1)} %bitcast.12), custom_call_target="tpu_custom_call" | custom-call | flops 1 | bytes 1 | tf_op jit(solution)/shard_map/pallas_call | solution.py:229
  18.3 6.8 %all-to-all-start = ((f32[8,28,128]{2,1,0:T(8,128)}), f32[8,28,128]{2,1,0:T(8,128)S(1)}, u32[]{:S(2)}, u32[]{:S(2)}) async-start(f32[8,28,128]{2,1,0:T(8,128)} %get-tuple-element.35), calls=%async_computation | async-start | bytes 262144 | tf_op jit(solution)/shard_map/all_to_all | solution.py:325
  25.1 0.5 collective-permute-start.5
  25.6 8.9 %all-to-all-done = f32[8,28,128]{2,1,0:T(8,128)S(1)} async-done(((f32[8,28,128]{2,1,0:T(8,128)}), f32[8,28,128]{2,1,0:T(8,128)S(1)}, u32[]{:S(2)}, u32[]{:S(2)}) %all-to-all-start) | async-done | bytes 114720 | tf_op jit(solution)/shard_map/all_to_all | solution.py:325
  34.5 0.1 collective-permute-start.7
  34.6 1.2 %collective-permute-done.7 = f32[14,128]{1,0:T(8,128)S(1)} collective-permute-done((f32[14,128]{1,0:T(8,128)S(1)}, f32[14,128]{1,0:T(8,128)S(1)}, u32[]{:S(2)}, u32[]{:S(2)}) %collective-permute-start.7) | collective-permute-done | bytes 7200 | tf_op jit(solution)/shard_map/ppermute | solution.py:25
  35.7 0.6 %collective-permute-start.8 = (f32[7,128]{1,0:T(8,128)S(1)}, f32[7,128]{1,0:T(8,128)S(1)}, u32[]{:S(2)}, u32[]{:S(2)}) collective-permute-start(f32[7,128]{1,0:T(8,128)S(1)} %slice.65), channel_id=1, source_target_pairs={{0,128},{64,192},{128,0},{192,64},{1,129},{65,193},{129,1},{193,65... | collective-permute-start | bytes 10760 | tf_op jit(solution)/shard_map/ppermute | solution.py:29
  36.3 0.0 collective-permute-done.2
  36.3 0.0 collective-permute-done
  36.3 1.4 %multiply_add_fusion.1 = (f32[736,128]{1,0:T(8,128)S(1)}, f32[736,128]{1,0:T(8,128)S(1)}) fusion(f16[1840,128]{1,0:T(8,128)(2,1)} %collective-permute-done.2, bf16[4784,128]{1,0:T(8,128)(2,1)} %collective-permute-done, bf16[4784,128]{1,0:T(8,128)(2,1)S(1)} %get-tuple-element.22), kind=kLoop, calls=%fused_computation.3 | loop fusion | flops 1130496 | bytes 1884160 | tf_op jit(solution)/shard_map/add | solution.py:302
  37.7 0.1 collective-permute-start.6
  37.8 2.0 %collective-permute-start.3 = (f32[736,128]{1,0:T(8,128)S(1)}, f32[736,128]{1,0:T(8,128)S(1)}, u32[]{:S(2)}, u32[]{:S(2)}) collective-permute-start(f32[736,128]{1,0:T(8,128)S(1)} %get-tuple-element.43.refs_3_), channel_id=1, source_target_pairs={{0,8},{8,16},{16,24},{24,32},{32,40},{40,48},{48,56},{56,0},{1,9},... | collective-permute-start | bytes 1130504 | tf_op jit(solution)/shard_map/ppermute | solution.py:34
  39.8 1.0 %multiply_add_fusion.3.refs_5_ = f32[368,128]{1,0:T(8,128)S(1)} fusion(f16[1840,128]{1,0:T(8,128)(2,1)} %collective-permute-done.2, bf16[4784,128]{1,0:T(8,128)(2,1)} %collective-permute-done, bf16[4784,128]{1,0:T(8,128)(2,1)S(1)} %get-tuple-element.22), kind=kLoop, calls=%fused_computation.5 | loop fusion | flops 282624 | bytes 471040 | tf_op jit(solution)/shard_map/add | solution.py:302
  40.8 4.4 %collective-permute-done.5 = f16[2944,128]{1,0:T(8,128)(2,1)S(1)} collective-permute-done((f16[2944,128]{1,0:T(8,128)(2,1)S(1)}, f16[2944,128]{1,0:T(8,128)(2,1)S(1)}, u32[]{:S(2)}, u32[]{:S(2)}) %collective-permute-start.5) | collective-permute-done | bytes 753696 | tf_op jit(solution)/shard_map/ppermute | solution.py:29
  45.2 1.4 %multiply_add_fusion.refs_2_ = f32[2944,128]{1,0:T(8,128)S(1)} fusion(f16[2944,128]{1,0:T(8,128)(2,1)S(1)} %collective-permute-done.5, bf16[4784,128]{1,0:T(8,128)(2,1)} %collective-permute-done, bf16[4784,128]{1,0:T(8,128)(2,1)S(1)} %get-tuple-element.22), kind=kLoop, calls=%fused_computation | loop fusion | flops 2260992 | bytes 3768320 | tf_op jit(solution)/shard_map/add | solution.py:302
  46.6 0.0 collective-permute-done.8.refs_8_
  46.7 1.6 %collective-permute-done.6.refs_4_ = f32[736,128]{1,0:T(8,128)S(1)} collective-permute-done((f32[736,128]{1,0:T(8,128)S(1)}, f32[736,128]{1,0:T(8,128)S(1)}, u32[]{:S(2)}, u32[]{:S(2)}) %collective-permute-start.6) | collective-permute-done | bytes 376864 | tf_op jit(solution)/shard_map/ppermute | solution.py:34
  48.3 1.3 %collective-permute-done.3.refs_0_ = f32[736,128]{1,0:T(8,128)S(1)} collective-permute-done((f32[736,128]{1,0:T(8,128)S(1)}, f32[736,128]{1,0:T(8,128)S(1)}, u32[]{:S(2)}, u32[]{:S(2)}) %collective-permute-start.3) | collective-permute-done | bytes 376864 | tf_op jit(solution)/shard_map/ppermute | solution.py:34
  49.6 3.1 %shard_map.71 = (f32[13,368,128]{2,1,0:T(8,128)}, f32[7,1,128]{2,1,0:T(1,128)}) custom-call(s32[1]{0:T(128)} %bitcast.date_ref, s32[104]{0:T(128)S(1)} %copy-done.1, f32[736,128]{1,0:T(8,128)S(1)} %collective-permute-done.3.refs_0_, f32[736,128]{1,0:T(8,128)S(1)} %get-tuple-element.42.refs_1_, f32[2944,128]{1,0:T(8,128)S(1)} %multiply_add_fusion.refs_2_, ...), custom_call_target="tpu_custom_call" | custom-call | flops 1 | bytes 1 | tf_op jit(solution)/shard_map/pallas_call | solution.py:143
  (4 shorter events, 0.0 us)
Async XLA Ops:
  3.0 5.3 %collective-permute-start.1 = (bf16[1840,128]{1,0:T(8,128)(2,1)}, bf16[1840,128]{1,0:T(8,128)(2,1)}, u32[]{:S(2)}, u32[]{:S(2)}) collective-permute-start(bf16[1840,128]{1,0:T(8,128)(2,1)} %get-tuple-element.28), channel_id=1, source_target_pairs={{0,64},{64,0},{128,192},{192,128},{1,65},{65,1},{129,193},{193,129... | collective-permute-start | bytes 1413128 | tf_op jit(solution)/shard_map/ppermute | solution.py:25
  7.0 6.5 %collective-permute-start.4 = (bf16[2944,128]{1,0:T(8,128)(2,1)S(1)}, bf16[2944,128]{1,0:T(8,128)(2,1)}, u32[]{:S(2)}, u32[]{:S(2)}) collective-permute-start(bf16[2944,128]{1,0:T(8,128)(2,1)S(1)} %get-tuple-element.31), channel_id=1, source_target_pairs={{0,64},{64,0},{128,192},{192,128},{1,65},{65,1},{129,193},{193,129... | collective-permute-start | bytes 2261000 | tf_op jit(solution)/shard_map/ppermute | solution.py:25
  7.6 28.8 %collective-permute-start = (bf16[4784,128]{1,0:T(8,128)(2,1)}, bf16[4784,128]{1,0:T(8,128)(2,1)}, u32[]{:S(2)}, u32[]{:S(2)}) collective-permute-start(bf16[4784,128]{1,0:T(8,128)(2,1)} %get-tuple-element.23), channel_id=1, source_target_pairs={{0,64},{64,0},{128,192},{192,128},{1,65},{65,1},{129,193},{193,129... | collective-permute-start | bytes 3674120 | tf_op jit(solution)/shard_map/ppermute | solution.py:25
  8.3 6.6 %copy-start = (bf16[11,1,46,128]{3,2,1,0:T(8,128)(2,1)S(1)}, bf16[11,1,46,128]{3,2,1,0:T(8,128)(2,1)}, u32[]{:S(2)}) copy-start(bf16[11,1,46,128]{3,2,1,0:T(8,128)(2,1)} %param.9) | copy-start | bytes 388612
  8.3 6.6 %copy-start.1 = (s32[104]{0:T(128)S(1)}, s32[104]{0:T(128)}, u32[]{:S(2)}) copy-start(s32[104]{0:T(128)} %days_ref.3) | copy-start | bytes 1252
  8.3 6.6 %copy-start.2 = (s32[46]{0:T(128)S(1)}, s32[46]{0:T(128)}, u32[]{:S(2)}) copy-start(s32[46]{0:T(128)} %bins_ref.1) | copy-start | bytes 556
  10.4 25.9 %collective-permute-start.2 = (f16[1840,128]{1,0:T(8,128)(2,1)}, f16[1840,128]{1,0:T(8,128)(2,1)}, u32[]{:S(2)}, u32[]{:S(2)}) collective-permute-start(f16[1840,128]{1,0:T(8,128)(2,1)} %multiply_convert_fusion.1), channel_id=1, source_target_pairs={{0,128},{64,192},{128,0},{192,64},{1,129},{65,193},{129,1},{193,65... | collective-permute-start | bytes 1413128 | tf_op jit(solution)/shard_map/ppermute | solution.py:29
  18.3 16.2 %all-to-all-start = ((f32[8,28,128]{2,1,0:T(8,128)}), f32[8,28,128]{2,1,0:T(8,128)S(1)}, u32[]{:S(2)}, u32[]{:S(2)}) async-start(f32[8,28,128]{2,1,0:T(8,128)} %get-tuple-element.35), calls=%async_computation | async-start | bytes 262144 | tf_op jit(solution)/shard_map/all_to_all | solution.py:325
  25.1 20.2 %collective-permute-start.5 = (f16[2944,128]{1,0:T(8,128)(2,1)S(1)}, f16[2944,128]{1,0:T(8,128)(2,1)S(1)}, u32[]{:S(2)}, u32[]{:S(2)}) collective-permute-start(f16[2944,128]{1,0:T(8,128)(2,1)S(1)} %multiply_convert_fusion), channel_id=1, source_target_pairs={{0,128},{64,192},{128,0},{192,64},{1,129},{65,193},{129,1},{193,65... | collective-permute-start | bytes 2261000 | tf_op jit(solution)/shard_map/ppermute | solution.py:29
  34.5 1.3 %collective-permute-start.7 = (f32[14,128]{1,0:T(8,128)S(1)}, f32[14,128]{1,0:T(8,128)S(1)}, u32[]{:S(2)}, u32[]{:S(2)}) collective-permute-start(f32[14,128]{1,0:T(8,128)S(1)} %slice.64), channel_id=1, source_target_pairs={{0,64},{64,0},{128,192},{192,128},{1,65},{65,1},{129,193},{193,129... | collective-permute-start | bytes 21512 | tf_op jit(solution)/shard_map/ppermute | solution.py:25
  35.7 10.9 %collective-permute-start.8 = (f32[7,128]{1,0:T(8,128)S(1)}, f32[7,128]{1,0:T(8,128)S(1)}, u32[]{:S(2)}, u32[]{:S(2)}) collective-permute-start(f32[7,128]{1,0:T(8,128)S(1)} %slice.65), channel_id=1, source_target_pairs={{0,128},{64,192},{128,0},{192,64},{1,129},{65,193},{129,1},{193,65... | collective-permute-start | bytes 10760 | tf_op jit(solution)/shard_map/ppermute | solution.py:29
  37.7 10.6 %collective-permute-start.6 = (f32[736,128]{1,0:T(8,128)S(1)}, f32[736,128]{1,0:T(8,128)S(1)}, u32[]{:S(2)}, u32[]{:S(2)}) collective-permute-start(f32[736,128]{1,0:T(8,128)S(1)} %get-tuple-element.42.refs_1_), channel_id=1, source_target_pairs={{0,56},{8,0},{16,8},{24,16},{32,24},{40,32},{48,40},{56,48},{1,57}... | collective-permute-start | bytes 1130504 | tf_op jit(solution)/shard_map/ppermute | solution.py:34
  37.8 11.8 %collective-permute-start.3 = (f32[736,128]{1,0:T(8,128)S(1)}, f32[736,128]{1,0:T(8,128)S(1)}, u32[]{:S(2)}, u32[]{:S(2)}) collective-permute-start(f32[736,128]{1,0:T(8,128)S(1)} %get-tuple-element.43.refs_3_), channel_id=1, source_target_pairs={{0,8},{8,16},{16,24},{24,32},{32,40},{40,48},{48,56},{56,0},{1,9},... | collective-permute-start | bytes 1130504 | tf_op jit(solution)/shard_map/ppermute | solution.py:34

commit v5 on v4

v5 whole, which is shorter than its diff:
```python
import functools

import jax
import jax.numpy as jnp
from jax import lax
from jax.experimental import pallas as pl
from jax.experimental.pallas import tpu as pltpu
from jax.sharding import PartitionSpec as P

WEEKS = 7
LANES = 128
TILE = 8
SCALE = 512.0
MIB = 1024 * 1024
SMEM = pl.BlockSpec(memory_space=pltpu.SMEM)
VMEM = pl.BlockSpec(memory_space=pltpu.VMEM)
HBM = pl.BlockSpec(memory_space=pltpu.HBM)


def estimate(num_bytes):
    return pl.CostEstimate(flops=1, transcendentals=0, bytes_accessed=num_bytes)


def core_swap(block):
    return lax.ppermute(block, "ens", [(0, 1), (1, 0), (2, 3), (3, 2)])


def chip_swap(block):
    return lax.ppermute(block, "ens", [(0, 2), (1, 3), (2, 0), (3, 1)])


def date_shift(block, step):
    count = lax.axis_size("date")
    return lax.ppermute(block, "date", [(i, (i + step) % count) for i in range(count)])


def split_rows(kinds, leads, rows, wanted, ens_ref, copies, held, wide, outs):
    block = leads * TILE
    core, half = ens_ref[0] % 2, ens_ref[0] // 2
    for slot, row in enumerate(rows):
        copies[slot].wait()
        spread = wide.at[slot % 2]
        spread[...] = held[slot].astype(jnp.float32)
        for out, (members, other_half, other_core) in zip(outs, wanted):
            if row not in members:
                continue
            kind = 2 * (1 - half if other_half else half) + (1 - core if other_core else core)
            start = members.index(row) * block
            for lead in range(0, leads, 2):
                picked = spread[pl.ds(lead * TILE * kinds + kind, 2 * TILE, stride=kinds), :]
                out[start + lead * TILE : start + (lead + 2) * TILE, :] = picked.astype(
                    jnp.bfloat16
                )


def start_rows(rows, block, runs_ref, held, sem):
    copies = []
    for slot, row in enumerate(rows):
        copy = pltpu.make_async_copy(
            runs_ref.at[pl.ds(row * block, block)], held.at[slot], sem.at[slot]
        )
        copy.start()
        copies.append(copy)
    return copies


def split_kernel(kinds, leads, rows, wanted, ens_ref, runs_ref, *rest):
    outs, (held, wide, sem) = rest[:-3], rest[-3:]
    copies = start_rows(rows, leads * TILE * kinds, runs_ref, held, sem)
    split_rows(kinds, leads, rows, wanted, ens_ref, copies, held, wide, outs)


def split_scratch(rows, block):
    return [
        pltpu.VMEM((len(rows), block, LANES), jnp.bfloat16),
        pltpu.VMEM((2, block, LANES), jnp.float32),
        pltpu.SemaphoreType.DMA((len(rows),)),
    ]


def split_kinds(flat, ens, kinds, leads, rows, wanted):
    block = leads * TILE
    shapes = [pltpu.VMEM((len(members) * block, LANES), jnp.bfloat16) for members, _, _ in wanted]
    outs = pl.pallas_call(
        functools.partial(split_kernel, kinds, leads, rows, wanted),
        in_specs=[SMEM, HBM],
        out_specs=[VMEM] * len(shapes),
        scratch_shapes=split_scratch(rows, block * kinds),
        out_shape=shapes,
        cost_estimate=estimate(len(rows) * block * LANES * 2 * kinds),
        compiler_params=pltpu.CompilerParams(vmem_limit_bytes=10 * MIB),
    )(ens, pltpu.with_memory_space_constraint(flat, pltpu.HBM))
    return list(outs)


def wrapped(index, count):
    index = jnp.where(index < 0, index + count, index)
    return jnp.where(index >= count, index - count, index)


def neighbour_weights(days_ref, date, cycle_days):
    count = days_ref.shape[0]
    weights = []
    for k in range(-2, 3):
        other = days_ref[wrapped(date + k, count)]
        gap = other - days_ref[date] if k >= 0 else days_ref[date] - other
        gap = jnp.where(gap < 0, gap + cycle_days, gap)
        weights.append(jnp.maximum(8 - gap, 0).astype(jnp.float32))
    total = weights[0] + weights[1] + weights[2] + weights[3] + weights[4]
    return weights, 1.0 / jnp.full((TILE, LANES), total, jnp.float32)


def smoothed_leads(leads, value):
    before, here = None, value(0)
    for lead in range(leads):
        after = value(lead + 1) if lead + 1 < leads else None
        total = here + here
        for beside in (before, after):
            if beside is not None:
                total = total + beside
        yield lead, total * (1.0 / 3.0 if before is None or after is None else 0.25)
        before, here = here, after


def smooth_kernel(leads, places, rows, total_rows, members, cycle_days, count, date_ref, days_ref, *refs):
    sums, (out_hbm, done, sem) = refs[:count], refs[-3:]

    def tile(row, lead):
        which, place = places[row]
        start = (place * leads + lead) * TILE
        return sums[which][start : start + TILE, :]

    copies = []
    for slot, row in enumerate(rows):
        weights, inverse = neighbour_weights(days_ref, date_ref[0] * total_rows + row, cycle_days)
        inverse = inverse * (1.0 / members)

        def mean(lead):
            value = weights[0] * tile(row - 2, lead)
            for k in range(1, 5):
                value = value + weights[k] * tile(row - 2 + k, lead)
            return value * inverse

        for lead, value in smoothed_leads(leads, mean):
            done[slot, lead * TILE : (lead + 1) * TILE, :] = value
        copy = pltpu.make_async_copy(done.at[slot], out_hbm.at[row], sem.at[slot])
        copy.start()
        copies.append(copy)
    for copy in copies:
        copy.wait()


def smooth_rows(date, days, arrays, rows, total_rows, leads, members, cycle_days, cost, into=None):
    places = {row: (i, j) for i, (_, held) in enumerate(arrays) for j, row in enumerate(held)}
    sums = [array for array, _ in arrays]
    operands = [date, days, *sums] + ([] if into is None else [into])
    return pl.pallas_call(
        functools.partial(
            smooth_kernel, leads, places, rows, total_rows, members, cycle_days, len(sums)
        ),
        in_specs=[SMEM, SMEM] + [VMEM] * len(sums) + ([] if into is None else [HBM]),
        out_specs=HBM,
        out_shape=jax.ShapeDtypeStruct((total_rows, leads * TILE, LANES), jnp.float32),
        scratch_shapes=[
            pltpu.VMEM((len(rows), leads * TILE, LANES), jnp.float32),
            pltpu.SemaphoreType.DMA((len(rows),)),
        ],
        input_output_aliases={} if into is None else {len(operands) - 1: 0},
        cost_estimate=estimate(cost),
        compiler_params=pltpu.CompilerParams(vmem_limit_bytes=8 * MIB),
    )(*operands)


def anomaly_kernel(forecast, kept, given, out):
    out[:, 0, :] = forecast[...] - (kept[...] + given[...])


def weekly_anomalies(forecast, kept, given):
    return pl.pallas_call(
        anomaly_kernel,
        in_specs=[VMEM] * 3,
        out_specs=VMEM,
        out_shape=jax.ShapeDtypeStruct((WEEKS, 1, LANES), jnp.float32),
        cost_estimate=estimate(1),
        compiler_params=pltpu.CompilerParams(vmem_limit_bytes=MIB),
    )(forecast, kept, given)


def count_weeks(leads, bins_ref, counts):
    for week in range(WEEKS):
        counts[week] = 0
    for lead in range(leads):
        counts[bins_ref[lead]] += 1


def weekly_kernel(
    kinds, leads, rows, members, cycle_days, ens_ref, date_ref, days_ref, position_ref, bins_ref, *refs
):
    runs_ref, give, keep, climate, near, sem, weekly, counts = refs
    group = TILE * kinds
    block = leads * group
    position = position_ref[0]
    dates = days_ref.shape[0]
    row_of = [wrapped(position + k - 2, dates) - date_ref[0] * rows for k in range(5)]
    here = [(row >= 0) & (row < rows) for row in row_of]

    def copy_of(k):
        start = pl.multiple_of(row_of[k] * block, 16)
        return pltpu.make_async_copy(runs_ref.at[pl.ds(start, block)], near.at[k], sem.at[k])

    for k in range(5):

        @pl.when(here[k])
        def _():
            copy_of(k).start()

    weights, inverse = neighbour_weights(days_ref, position, cycle_days)
    inverse = inverse * (1.0 / members)
    count_weeks(leads, bins_ref, counts)
    weekly[...] = jnp.zeros_like(weekly)

    @pl.when(here[0] | here[1] | here[2] | here[3] | here[4])
    def _():
        climate[...] = jnp.zeros_like(climate)
        for k in range(5):

            @pl.when(here[k])
            def _():
                copy_of(k).wait()
                climate[...] += weights[k] * near[k].astype(jnp.float32)

        def part(lead):
            return climate[lead * group : (lead + 1) * group, :]

        for lead, value in smoothed_leads(leads, part):
            span = pl.ds(pl.multiple_of(bins_ref[lead] * group, group), group)
            weekly[span, :] += value

    core, half = ens_ref[0] % 2, ens_ref[0] // 2
    for week in range(WEEKS):
        scale = inverse / jnp.full((TILE, LANES), counts[week].astype(jnp.float32))
        for role, of_half in enumerate((1 - half, half)):
            for out, of_core in ((give, 1 - core), (keep, core)):
                kind = 2 * of_half + of_core
                mean = weekly[pl.ds(week * group + kind, TILE, stride=kinds), :] * scale
                for slot in range(TILE):
                    out[role * TILE + slot, week, :] = mean[slot]


def weekly_shares(ens, date, days, position, bins, flat, kinds, leads, rows, members, cycle_days):
    block = leads * TILE * kinds
    shape = pltpu.VMEM((2 * TILE, WEEKS, LANES), jnp.float32)
    return pl.pallas_call(
        functools.partial(weekly_kernel, kinds, leads, rows, members, cycle_days),
        in_specs=[SMEM] * 5 + [HBM],
        out_specs=[VMEM] * 2,
        out_shape=[shape] * 2,
        scratch_shapes=[
            pltpu.VMEM((block, LANES), jnp.float32),
            pltpu.VMEM((5, block, LANES), jnp.bfloat16),
            pltpu.SemaphoreType.DMA((5,)),
            pltpu.VMEM((WEEKS * TILE * kinds, LANES), jnp.float32),
            pltpu.SMEM((WEEKS,), jnp.int32),
        ],
        cost_estimate=estimate(1),
        compiler_params=pltpu.CompilerParams(vmem_limit_bytes=8 * MIB),
    )(ens, date, days, position, bins, pltpu.with_memory_space_constraint(flat, pltpu.HBM))


def forecast_kernel(leads, bins_ref, forecast_ref, out, total, means, counts):
    count_weeks(leads, bins_ref, counts)
    runs = forecast_ref.shape[0]
    value = forecast_ref[0].astype(jnp.float32)
    for run in range(1, runs):
        value = value + forecast_ref[run].astype(jnp.float32)
    total[...] = value
    means[...] = jnp.zeros_like(means)
    for lead in range(leads):
        means[pl.ds(bins_ref[lead], 1), :] += total[lead : lead + 1, :]
    for week in range(WEEKS):
        count = jnp.full((1, LANES), (counts[week] * runs).astype(jnp.float32))
        out[week : week + 1, :] = means[week : week + 1, :] / count


def forecast_weeks(bins, forecast, leads):
    return pl.pallas_call(
        functools.partial(forecast_kernel, leads),
        in_specs=[SMEM, VMEM],
        out_specs=VMEM,
        out_shape=jax.ShapeDtypeStruct((WEEKS, LANES), jnp.float32),
        scratch_shapes=[
            pltpu.VMEM((leads, LANES), jnp.float32),
            pltpu.VMEM((TILE, LANES), jnp.float32),
            pltpu.SMEM((WEEKS,), jnp.int32),
        ],
        cost_estimate=estimate(1),
        compiler_params=pltpu.CompilerParams(vmem_limit_bytes=4 * MIB),
    )(bins, forecast)


def date_bits():
    slot = lax.axis_index("date").astype(jnp.uint32)
    steps = [1 << bit for bit in range(lax.axis_size("date").bit_length() - 1)][::-1]
    return [number for step in steps for number in ((slot // step) & 1, ((slot // step) & 1) ^ 1)]


def weeks_over_dates(total, bits):
    slots = lax.axis_size("date")
    step = slots // 2
    for mine, other in zip(bits[::2], bits[1::2]):
        halves = total.reshape(2, step, *total.shape[1:])
        give = lax.dynamic_index_in_dim(halves, other, 0, keepdims=False)
        keep = lax.dynamic_index_in_dim(halves, mine, 0, keepdims=False)
        got = lax.ppermute(give, "date", [(i, i ^ step) for i in range(slots)])
        total = keep + got
        step //= 2
    return keep[0], got[0]


def per_device(
    hindcast_runs,
    init_calendar_ordinal,
    prediction_init_position,
    horizon_sevenfold_bin,
    prediction_runs,
):
    _, rows, kinds, leads, cells = hindcast_runs.shape
    dates = rows * lax.axis_size("date")
    members = lax.axis_size("ens")
    cycle_days = 7 * dates // 2
    block = leads * TILE
    ens = lax.axis_index("ens").astype(jnp.int32).reshape(1)
    date = lax.axis_index("date").astype(jnp.int32).reshape(1)

    numbers = date_bits()

    flat = hindcast_runs.reshape(rows, kinds, leads, TILE, LANES)
    flat = flat.transpose(0, 2, 3, 1, 4).reshape(rows * leads * TILE * kinds, LANES)
    flat, ens, date, *numbers = lax.optimization_barrier((flat, ens, date, *numbers))

    first = [0, 1, rows - 2, rows - 1]
    second = list(range(2, rows - 2))
    split = functools.partial(split_kinds, kinds=kinds, leads=leads)

    def for_x(flat, members):
        return split(flat, ens, rows=members, wanted=[(members, True, True), (members, True, False)])

    def pair_sum(mine, other):
        return ((mine.astype(jnp.float32) + other.astype(jnp.float32)) * SCALE).astype(jnp.float16)

    theirs_0, mine_0 = for_x(flat, first)
    got_0 = core_swap(theirs_0)
    flat, mine_0 = lax.optimization_barrier((flat, mine_0))
    theirs_1, mine_1 = for_x(flat, second)
    got_1 = core_swap(theirs_1)
    flat, mine_1 = lax.optimization_barrier((flat, mine_1))
    weeks_give, weeks_keep = weekly_shares(
        ens,
        date,
        init_calendar_ordinal,
        prediction_init_position,
        horizon_sevenfold_bin,
        flat,
        kinds,
        leads,
        rows,
        members,
        cycle_days,
    )
    mine_0, weeks_keep = lax.optimization_barrier((mine_0, weeks_keep))
    packed_0 = pair_sum(mine_0, got_0)
    packed_0, weeks_give = lax.optimization_barrier((packed_0, weeks_give))
    weeks_got = core_swap(weeks_give)
    arrived_0 = chip_swap(packed_0)
    flat, packed_0, mine_1 = lax.optimization_barrier((flat, packed_0, mine_1))
    packed_1 = pair_sum(mine_1, got_1)
    arrived_1 = chip_swap(packed_1)
    parts = [first, second]
    own = split(
        flat,
        ens,
        rows=first + second,
        wanted=[(part, False, other) for part in parts for other in (True, False)],
    )
    others = [core_swap(theirs) for theirs in own[::2]]

    weeks = weeks_keep + weeks_got
    weeks = weeks[TILE:] + chip_swap(weeks[:TILE])
    def local_sum(own, other, own_place, packed, place, count):
        own_span = slice(own_place * block, (own_place + count) * block)
        pair = own[own_span].astype(jnp.float32) + other[own_span].astype(jnp.float32)
        span = slice(place * block, (place + count) * block)
        return pair + packed[span].astype(jnp.float32) * (1.0 / SCALE)

    low = local_sum(own[1], others[0], 0, arrived_0, 0, 2)
    high = local_sum(own[1], others[0], 2, arrived_0, 2, 2)
    weeks, low, high = lax.optimization_barrier((weeks, low, high))
    kept, given = weeks_over_dates(weeks, numbers)
    below = date_shift(high, 1)
    above = date_shift(low, -1)
    middle = local_sum(own[3], others[1], 0, arrived_1, 0, len(second))

    forecast = forecast_weeks(horizon_sevenfold_bin, prediction_runs[:, 0], leads)

    arrays = [
        (below, [-2, -1]),
        (low, [0, 1]),
        (middle, second),
        (high, [rows - 2, rows - 1]),
        (above, [rows, rows + 1]),
    ]
    smooth = functools.partial(
        smooth_rows,
        date,
        init_calendar_ordinal,
        total_rows=rows,
        leads=leads,
        members=members,
        cycle_days=cycle_days,
    )
    smoothed = smooth(arrays[1:-1], list(range(2, rows - 2)), cost=10 * MIB)
    smoothed = smooth(arrays, [0, 1, rows - 2, rows - 1], cost=1, into=smoothed)
    return smoothed.reshape(rows, 1, leads, cells), weekly_anomalies(forecast, kept, given)


def solution(mesh):
    return jax.shard_map(
        per_device,
        mesh=mesh,
        in_specs=(
            P("ens", "date", None, None, "pix"),
            P(),
            P(),
            P(),
            P(None, "ens", None, ("pix", "date")),
        ),
        out_specs=(P("date", "ens", None, "pix"), P(None, "ens", ("pix", "date"))),
        check_vma=False,
    )
```

time: 53.7 us -> 50.7 us (0.944); the launches traced: 52.7 us -> 50.5 us
  starting transfers between devices: 13.9 us -> 20.4 us
  other arithmetic: 7.24 us -> 1.03 us
  waiting for transfers between devices: 17.4 us -> 14 us
  Pallas kernels: 12.7 us -> 13.5 us
    all_to_all x1 -> x0, waiting for transfers between devices: 8.87 us -> none  [per_device(): lax.all_to_all(weekly, 'date', split_axis=0, concat_axis=0, tiled=True)]
    ppermute x0 -> x3, starting transfers between devices: none -> 8.09 us  [weeks_over_dates(): got = lax.ppermute(give, 'date', [(i, i ^ step) for i in range(slots)])]
    all_to_all x1 -> x0, starting transfers between devices: 6.79 us -> none  [per_device(): lax.all_to_all(weekly, 'date', split_axis=0, concat_axis=0, tiled=True)]
    ppermute x0 -> x3, waiting for transfers between devices: none -> 4.87 us  [weeks_over_dates(): got = lax.ppermute(give, 'date', [(i, i ^ step) for i in range(slots)])]
    ppermute x3, waiting for transfers between devices: 4.45 us -> 7.9 us  [chip_swap(): return lax.ppermute(block, 'ens', [(0, 2), (1, 3), (2, 0), (3, 1)])]
    add x4 -> x6, other arithmetic: 3.75 us -> 0.55 us  [the longest x2 0.53 us: local_sum(): return pair + packed[span].astype(jnp.float32) * (1.0 / SCALE)]
    convert_element_type x2, other arithmetic: 3.48 us -> 0.48 us  [pair_sum(): ((mine.astype(jnp.float32) + other.astype(jnp.float32)) * SCALE).astype(j...]
    ppermute x2, waiting for transfers between devices: 2.93 us -> 0.01 us  [date_shift(): lax.ppermute(block, 'date', [(i, (i + step) % count) for i in range(count)])]
  transfers between devices with their start and end apart: 10 -> 13, of which waited for: 5 -> 5; matrix products, arithmetic and copies ran while one was open for 14% -> 2% of each run, Pallas kernels for 14% -> 21%
where the time goes in v5:
time: 50.7 us; the launch traced here: 50.5 us
  starting transfers between devices  20.4 us (40%)
  waiting for transfers between devices  14 us (28%)
  Pallas kernels  13.5 us (27%)
  between operations  1.49 us (3%)
  other arithmetic  1.03 us (2%)
    ppermute x3, starting transfers between devices, weeks_over_dates(): got = lax.ppermute(give, 'date', [(i, i ^ step) for i in range(slots)])  8.09 us
    ppermute x3, waiting for transfers between devices, chip_swap(): return lax.ppermute(block, 'ens', [(0, 2), (1, 3), (2, 0), (3, 1)])  7.9 us
    ppermute x3, starting transfers between devices, chip_swap(): return lax.ppermute(block, 'ens', [(0, 2), (1, 3), (2, 0), (3, 1)])  6.75 us
    pallas_call x3, Pallas kernels, split_kinds(): pl.pallas_call(functools.partial(split_kernel, kinds, leads, rows, wanted...  6.12 us
    ppermute x3, waiting for transfers between devices, weeks_over_dates(): got = lax.ppermute(give, 'date', [(i, i ^ step) for i in range(slots)])  4.87 us
    ppermute x2, starting transfers between devices, date_shift(): lax.ppermute(block, 'date', [(i, (i + step) % count) for i in range(count)])  4.2 us
    pallas_call x2, Pallas kernels, smooth_rows(): pl.pallas_call(functools.partial(smooth_kernel, leads, places, rows, tota...  3.78 us
    pallas_call x1, Pallas kernels, weekly_shares(): pl.pallas_call(functools.partial(weekly_kernel, kinds, leads, rows, membe...  2.16 us
  transfers between devices with their start and end apart: 13, of which 5 were waited for; matrix products, arithmetic and copies ran while one was open for 2% of the time, Pallas kernels for 21%

profile of v5, /device:TPU:8, one launch (start us, length us, event | category | flops | bytes accessed | tf_op | source)
XLA Modules:
  0.0 50.5 jit_solution(17983897953644248974)
XLA Ops:
  0.6 1.5 %shard_map.68 = (bf16[1472,128]{1,0:T(8,128)(2,1)S(1)}, bf16[1472,128]{1,0:T(8,128)(2,1)S(1)}) custom-call(s32[1]{0:T(128)} %bitcast.3.ens_ref, bf16[19136,128]{1,0:T(8,128)(2,1)} %bitcast.24), custom_call_target="tpu_custom_call" | custom-call | flops 1 | bytes 1507328 | tf_op jit(solution)/shard_map/pallas_call | solution.py:84
  2.1 0.1 collective-permute-start
  2.2 0.0 copy-start.1
  2.2 0.0 copy-start.2
  2.2 2.1 %shard_map.69 = (bf16[3312,128]{1,0:T(8,128)(2,1)S(1)}, bf16[3312,128]{1,0:T(8,128)(2,1)S(1)}) custom-call(s32[1]{0:T(128)} %bitcast.3.ens_ref, bf16[19136,128]{1,0:T(8,128)(2,1)} %bitcast.25), custom_call_target="tpu_custom_call" | custom-call | flops 1 | bytes 3391488 | tf_op jit(solution)/shard_map/pallas_call | solution.py:84
  4.3 0.6 %collective-permute-start.7 = (bf16[3312,128]{1,0:T(8,128)(2,1)S(1)}, bf16[3312,128]{1,0:T(8,128)(2,1)S(1)}, u32[]{:S(2)}, u32[]{:S(2)}) collective-permute-start(bf16[3312,128]{1,0:T(8,128)(2,1)S(1)} %get-tuple-element.58), channel_id=1, source_target_pairs={{0,64},{64,0},{128,192},{192,128},{1,65},{65,1},{129,193},{193,129... | collective-permute-start | bytes 2543624 | tf_op jit(solution)/shard_map/ppermute | solution.py:25
  5.6 0.0 copy-done.1
  5.6 0.0 copy-done.2
  5.6 2.2 %shard_map.70 = (f32[16,7,128]{2,1,0:T(8,128)S(1)}, f32[16,7,128]{2,1,0:T(8,128)S(1)}) custom-call(s32[1]{0:T(128)} %bitcast.3.ens_ref, s32[1]{0:T(128)} %bitcast.4.date_ref, s32[104]{0:T(128)S(1)} %copy-done.1, s32[1]{0:T(128)S(6)} %copy.13.position_ref, s32[46]{0:T(128)S(1)} %copy-done.2, bf16[19136,128]{1,0:T(8,128)(2,1)} %bitcast.26), custom_call_target="tpu_custom_call" | custom-call | flops 1 | bytes 1 | tf_op jit(solution)/shard_map/pallas_call | solution.py:253
  7.8 0.0 collective-permute-done
  7.8 0.2 multiply_convert_fusion.1
  7.9 0.1 collective-permute-start.1
  8.0 1.2 %collective-permute-done.1 = f32[16,7,128]{2,1,0:T(8,128)S(1)} collective-permute-done((f32[16,7,128]{2,1,0:T(8,128)S(1)}, f32[16,7,128]{2,1,0:T(8,128)S(1)}, u32[]{:S(2)}, u32[]{:S(2)}) %collective-permute-start.1) | collective-permute-done | bytes 57376 | tf_op jit(solution)/shard_map/ppermute | solution.py:25
  9.3 3.1 %collective-permute-start.2 = (f32[8,7,128]{2,1,0:T(8,128)S(1)}, f32[8,7,128]{2,1,0:T(8,128)S(1)}, u32[]{:S(2)}, u32[]{:S(2)}) collective-permute-start(f32[8,7,128]{2,1,0:T(8,128)S(1)} %slice.33), channel_id=1, source_target_pairs={{0,128},{64,192},{128,0},{192,64},{1,129},{65,193},{129,1},{193,65... | collective-permute-start | bytes 86024 | tf_op jit(solution)/shard_map/ppermute | solution.py:29
  12.4 0.5 collective-permute-start.4
  12.9 2.6 %shard_map.71 = (bf16[1472,128]{1,0:T(8,128)(2,1)S(1)}, bf16[1472,128]{1,0:T(8,128)(2,1)S(1)}, bf16[3312,128]{1,0:T(8,128)(2,1)S(1)}, bf16[3312,128]{1,0:T(8,128)(2,1)S(1)}) custom-call(s32[1]{0:T(128)} %bitcast.3.ens_ref, bf16[19136,128]{1,0:T(8,128)(2,1)} %bitcast.27), custom_call_target="tpu_custom_call" | custom-call | flops 1 | bytes 4898816 | tf_op jit(solution)/shard_map/pallas_call | solution.py:84
  15.5 0.1 collective-permute-start.3
  15.6 0.5 collective-permute-start.6
  16.1 0.0 collective-permute-done.2
  16.1 0.0 copy-start
  16.1 0.0 collective-permute-done.7
  16.1 0.3 multiply_convert_fusion
  16.5 3.1 %collective-permute-start.8 = (f16[3312,128]{1,0:T(8,128)(2,1)S(1)}, f16[3312,128]{1,0:T(8,128)(2,1)S(1)}, u32[]{:S(2)}, u32[]{:S(2)}) collective-permute-start(f16[3312,128]{1,0:T(8,128)(2,1)S(1)} %multiply_convert_fusion), channel_id=1, source_target_pairs={{0,128},{64,192},{128,0},{192,64},{1,129},{65,193},{129,1},{193,65... | collective-permute-start | bytes 2543624 | tf_op jit(solution)/shard_map/ppermute | solution.py:29
  19.6 6.0 %collective-permute-done.4 = f16[1472,128]{1,0:T(8,128)(2,1)S(1)} collective-permute-done((f16[1472,128]{1,0:T(8,128)(2,1)S(1)}, f16[1472,128]{1,0:T(8,128)(2,1)S(1)}, u32[]{:S(2)}, u32[]{:S(2)}) %collective-permute-start.4) | collective-permute-done | bytes 376864 | tf_op jit(solution)/shard_map/ppermute | solution.py:29
  25.6 0.0 collective-permute-done.3
  25.6 0.2 multiply_add_fusion.1
  25.8 6.0 %collective-permute-start.10 = (f32[4,7,128]{2,1,0:T(8,128)S(1)}, f32[4,7,128]{2,1,0:T(8,128)S(1)}, u32[]{:S(2)}, u32[]{:S(2)}) collective-permute-start(f32[4,7,128]{2,1,0:T(8,128)S(1)} %dynamic-slice_bitcast_fusion), channel_id=1, source_target_pairs={{0,32},{8,40},{16,48},{24,56},{32,0},{40,8},{48,16},{56,24},{1,33}... | collective-permute-start | bytes 43016 | tf_op jit(solution)/shard_map/ppermute | solution.py:314
  31.8 1.7 %collective-permute-done.10 = f32[4,7,128]{2,1,0:T(8,128)S(1)} collective-permute-done((f32[4,7,128]{2,1,0:T(8,128)S(1)}, f32[4,7,128]{2,1,0:T(8,128)S(1)}, u32[]{:S(2)}, u32[]{:S(2)}) %collective-permute-start.10) | collective-permute-done | bytes 14368 | tf_op jit(solution)/shard_map/ppermute | solution.py:314
  33.5 2.0 %collective-permute-start.11 = (f32[2,7,128]{2,1,0:T(8,128)S(1)}, f32[2,7,128]{2,1,0:T(8,128)S(1)}, u32[]{:S(2)}, u32[]{:S(2)}) collective-permute-start(f32[2,7,128]{2,1,0:T(8,128)S(1)} %dynamic-slice_bitcast_fusion.1), channel_id=1, source_target_pairs={{0,16},{8,24},{16,0},{24,8},{32,48},{40,56},{48,32},{56,40},{1,17}... | collective-permute-start | bytes 21512 | tf_op jit(solution)/shard_map/ppermute | solution.py:314
  35.5 0.0 copy-done
  35.5 0.9 %shard_map.74.forecast = f32[7,128]{1,0:T(8,128)S(1)} custom-call(s32[46]{0:T(128)S(1)} %copy-done.2, bf16[11,46,128]{2,1,0:T(8,128)(2,1)S(1)} %bitcast.22), custom_call_target="tpu_custom_call" | custom-call | flops 1 | bytes 1 | tf_op jit(solution)/shard_map/pallas_call | solution.py:286
  36.4 2.1 %collective-permute-start.5 = (f32[736,128]{1,0:T(8,128)S(1)}, f32[736,128]{1,0:T(8,128)S(1)}, u32[]{:S(2)}, u32[]{:S(2)}) collective-permute-start(f32[736,128]{1,0:T(8,128)S(1)} %get-tuple-element.53.refs_2_.refs_3_), channel_id=1, source_target_pairs={{0,8},{8,16},{16,24},{24,32},{32,40},{40,48},{48,56},{56,0},{1,9},... | collective-permute-start | bytes 1130504 | tf_op jit(solution)/shard_map/ppermute | solution.py:34
  38.5 2.1 %collective-permute-start.9 = (f32[736,128]{1,0:T(8,128)S(1)}, f32[736,128]{1,0:T(8,128)S(1)}, u32[]{:S(2)}, u32[]{:S(2)}) collective-permute-start(f32[736,128]{1,0:T(8,128)S(1)} %get-tuple-element.54.refs_0_.refs_1_), channel_id=1, source_target_pairs={{0,56},{8,0},{16,8},{24,16},{32,24},{40,32},{48,40},{56,48},{1,57}... | collective-permute-start | bytes 1130504 | tf_op jit(solution)/shard_map/ppermute | solution.py:34
  40.6 0.0 collective-permute-done.11
  40.6 0.1 collective-permute-start.12
  40.7 0.0 collective-permute-done.6
  40.7 1.9 %collective-permute-done.8 = f16[3312,128]{1,0:T(8,128)(2,1)S(1)} collective-permute-done((f16[3312,128]{1,0:T(8,128)(2,1)S(1)}, f16[3312,128]{1,0:T(8,128)(2,1)S(1)}, u32[]{:S(2)}, u32[]{:S(2)}) %collective-permute-start.8) | collective-permute-done | bytes 847904 | tf_op jit(solution)/shard_map/ppermute | solution.py:29
  42.6 0.3 multiply_add_fusion.refs_1_.refs_2_
  43.0 3.1 %collective-permute-done.12 = f32[1,7,128]{2,1,0:T(8,128)S(1)} collective-permute-done((f32[1,7,128]{2,1,0:T(8,128)S(1)}, f32[1,7,128]{2,1,0:T(8,128)S(1)}, u32[]{:S(2)}, u32[]{:S(2)}) %collective-permute-start.12) | collective-permute-done | bytes 3616 | tf_op jit(solution)/shard_map/ppermute | solution.py:314
  46.1 0.6 %shard_map.75 = f32[7,1,128]{2,1,0:T(1,128)} custom-call(f32[7,128]{1,0:T(8,128)S(1)} %shard_map.74.forecast, f32[7,128]{1,0:T(8,128)S(1)} %get-tuple-element.73.kept, f32[7,128]{1,0:T(8,128)S(1)} %bitcast.23), custom_call_target="tpu_custom_call" | custom-call | flops 1 | bytes 1 | tf_op jit(solution)/shard_map/pallas_call | solution.py:179
  46.7 2.1 %shard_map.72.refs_5_ = f32[13,368,128]{2,1,0:T(8,128)} custom-call(s32[1]{0:T(128)} %bitcast.4.date_ref, s32[104]{0:T(128)S(1)} %copy-done.1, f32[736,128]{1,0:T(8,128)S(1)} %get-tuple-element.54.refs_0_.refs_1_, f32[3312,128]{1,0:T(8,128)S(1)} %multiply_add_fusion.refs_1_.refs_2_, f32[736,128]{1,0:T(8,128)S(1)} %get-tuple-element.53.refs_2_.refs_3_), custom_call_target="tpu_custom_call" | custom-call | flops 1 | bytes 10485760 | tf_op jit(solution)/shard_map/pallas_call | solution.py:157
  48.8 0.0 collective-permute-done.5.refs_0_
  48.8 0.0 collective-permute-done.9.refs_4_
  48.8 1.7 %shard_map.73 = f32[13,368,128]{2,1,0:T(8,128)} custom-call(s32[1]{0:T(128)} %bitcast.4.date_ref, s32[104]{0:T(128)S(1)} %copy-done.1, f32[736,128]{1,0:T(8,128)S(1)} %collective-permute-done.5.refs_0_, f32[736,128]{1,0:T(8,128)S(1)} %get-tuple-element.54.refs_0_.refs_1_, ...), custom_call_target="tpu_custom_call", output_to_operand_aliasing={{}: (7, {})} | custom-call | flops 1 | bytes 1 | tf_op jit(solution)/shard_map/pallas_call | solution.py:157
  (8 shorter events, 0.0 us)
Async XLA Ops:
  2.1 5.6 %collective-permute-start = (bf16[1472,128]{1,0:T(8,128)(2,1)S(1)}, bf16[1472,128]{1,0:T(8,128)(2,1)S(1)}, u32[]{:S(2)}, u32[]{:S(2)}) collective-permute-start(bf16[1472,128]{1,0:T(8,128)(2,1)S(1)} %get-tuple-element.45), channel_id=1, source_target_pairs={{0,64},{64,0},{128,192},{192,128},{1,65},{65,1},{129,193},{193,129... | collective-permute-start | bytes 1130504 | tf_op jit(solution)/shard_map/ppermute | solution.py:25
  2.2 3.4 %copy-start.1 = (s32[104]{0:T(128)S(1)}, s32[104]{0:T(128)}, u32[]{:S(2)}) copy-start(s32[104]{0:T(128)} %days_ref.5) | copy-start | bytes 1252
  2.2 3.3 %copy-start.2 = (s32[46]{0:T(128)S(1)}, s32[46]{0:T(128)}, u32[]{:S(2)}) copy-start(s32[46]{0:T(128)} %bins_ref.3) | copy-start | bytes 556
  4.3 11.8 %collective-permute-start.7 = (bf16[3312,128]{1,0:T(8,128)(2,1)S(1)}, bf16[3312,128]{1,0:T(8,128)(2,1)S(1)}, u32[]{:S(2)}, u32[]{:S(2)}) collective-permute-start(bf16[3312,128]{1,0:T(8,128)(2,1)S(1)} %get-tuple-element.58), channel_id=1, source_target_pairs={{0,64},{64,0},{128,192},{192,128},{1,65},{65,1},{129,193},{193,129... | collective-permute-start | bytes 2543624 | tf_op jit(solution)/shard_map/ppermute | solution.py:25
  7.9 1.3 %collective-permute-start.1 = (f32[16,7,128]{2,1,0:T(8,128)S(1)}, f32[16,7,128]{2,1,0:T(8,128)S(1)}, u32[]{:S(2)}, u32[]{:S(2)}) collective-permute-start(f32[16,7,128]{2,1,0:T(8,128)S(1)} %get-tuple-element.47), channel_id=1, source_target_pairs={{0,64},{64,0},{128,192},{192,128},{1,65},{65,1},{129,193},{193,129... | collective-permute-start | bytes 172040 | tf_op jit(solution)/shard_map/ppermute | solution.py:25
  9.3 6.8 %collective-permute-start.2 = (f32[8,7,128]{2,1,0:T(8,128)S(1)}, f32[8,7,128]{2,1,0:T(8,128)S(1)}, u32[]{:S(2)}, u32[]{:S(2)}) collective-permute-start(f32[8,7,128]{2,1,0:T(8,128)S(1)} %slice.33), channel_id=1, source_target_pairs={{0,128},{64,192},{128,0},{192,64},{1,129},{65,193},{129,1},{193,65... | collective-permute-start | bytes 86024 | tf_op jit(solution)/shard_map/ppermute | solution.py:29
  12.4 13.2 %collective-permute-start.4 = (f16[1472,128]{1,0:T(8,128)(2,1)S(1)}, f16[1472,128]{1,0:T(8,128)(2,1)S(1)}, u32[]{:S(2)}, u32[]{:S(2)}) collective-permute-start(f16[1472,128]{1,0:T(8,128)(2,1)S(1)} %multiply_convert_fusion.1), channel_id=1, source_target_pairs={{0,128},{64,192},{128,0},{192,64},{1,129},{65,193},{129,1},{193,65... | collective-permute-start | bytes 1130504 | tf_op jit(solution)/shard_map/ppermute | solution.py:29
  15.5 10.1 %collective-permute-start.3 = (bf16[1472,128]{1,0:T(8,128)(2,1)S(1)}, bf16[1472,128]{1,0:T(8,128)(2,1)S(1)}, u32[]{:S(2)}, u32[]{:S(2)}) collective-permute-start(bf16[1472,128]{1,0:T(8,128)(2,1)S(1)} %get-tuple-element.52), channel_id=1, source_target_pairs={{0,64},{64,0},{128,192},{192,128},{1,65},{65,1},{129,193},{193,129... | collective-permute-start | bytes 1130504 | tf_op jit(solution)/shard_map/ppermute | solution.py:25
  15.6 25.1 %collective-permute-start.6 = (bf16[3312,128]{1,0:T(8,128)(2,1)S(1)}, bf16[3312,128]{1,0:T(8,128)(2,1)S(1)}, u32[]{:S(2)}, u32[]{:S(2)}) collective-permute-start(bf16[3312,128]{1,0:T(8,128)(2,1)S(1)} %get-tuple-element.56), channel_id=1, source_target_pairs={{0,64},{64,0},{128,192},{192,128},{1,65},{65,1},{129,193},{193,129... | collective-permute-start | bytes 2543624 | tf_op jit(solution)/shard_map/ppermute | solution.py:25
  16.1 19.5 %copy-start = (bf16[11,1,46,128]{3,2,1,0:T(8,128)(2,1)S(1)}, bf16[11,1,46,128]{3,2,1,0:T(8,128)(2,1)}, u32[]{:S(2)}) copy-start(bf16[11,1,46,128]{3,2,1,0:T(8,128)(2,1)} %param.9) | copy-start | bytes 388612
  16.5 26.2 %collective-permute-start.8 = (f16[3312,128]{1,0:T(8,128)(2,1)S(1)}, f16[3312,128]{1,0:T(8,128)(2,1)S(1)}, u32[]{:S(2)}, u32[]{:S(2)}) collective-permute-start(f16[3312,128]{1,0:T(8,128)(2,1)S(1)} %multiply_convert_fusion), channel_id=1, source_target_pairs={{0,128},{64,192},{128,0},{192,64},{1,129},{65,193},{129,1},{193,65... | collective-permute-start | bytes 2543624 | tf_op jit(solution)/shard_map/ppermute | solution.py:29
  25.8 7.7 %collective-permute-start.10 = (f32[4,7,128]{2,1,0:T(8,128)S(1)}, f32[4,7,128]{2,1,0:T(8,128)S(1)}, u32[]{:S(2)}, u32[]{:S(2)}) collective-permute-start(f32[4,7,128]{2,1,0:T(8,128)S(1)} %dynamic-slice_bitcast_fusion), channel_id=1, source_target_pairs={{0,32},{8,40},{16,48},{24,56},{32,0},{40,8},{48,16},{56,24},{1,33}... | collective-permute-start | bytes 43016 | tf_op jit(solution)/shard_map/ppermute | solution.py:314
  33.5 7.1 %collective-permute-start.11 = (f32[2,7,128]{2,1,0:T(8,128)S(1)}, f32[2,7,128]{2,1,0:T(8,128)S(1)}, u32[]{:S(2)}, u32[]{:S(2)}) collective-permute-start(f32[2,7,128]{2,1,0:T(8,128)S(1)} %dynamic-slice_bitcast_fusion.1), channel_id=1, source_target_pairs={{0,16},{8,24},{16,0},{24,8},{32,48},{40,56},{48,32},{56,40},{1,17}... | collective-permute-start | bytes 21512 | tf_op jit(solution)/shard_map/ppermute | solution.py:314
  36.4 12.4 %collective-permute-start.5 = (f32[736,128]{1,0:T(8,128)S(1)}, f32[736,128]{1,0:T(8,128)S(1)}, u32[]{:S(2)}, u32[]{:S(2)}) collective-permute-start(f32[736,128]{1,0:T(8,128)S(1)} %get-tuple-element.53.refs_2_.refs_3_), channel_id=1, source_target_pairs={{0,8},{8,16},{16,24},{24,32},{32,40},{40,48},{48,56},{56,0},{1,9},... | collective-permute-start | bytes 1130504 | tf_op jit(solution)/shard_map/ppermute | solution.py:34
  38.5 10.4 %collective-permute-start.9 = (f32[736,128]{1,0:T(8,128)S(1)}, f32[736,128]{1,0:T(8,128)S(1)}, u32[]{:S(2)}, u32[]{:S(2)}) collective-permute-start(f32[736,128]{1,0:T(8,128)S(1)} %get-tuple-element.54.refs_0_.refs_1_), channel_id=1, source_target_pairs={{0,56},{8,0},{16,8},{24,16},{32,24},{40,32},{48,40},{56,48},{1,57}... | collective-permute-start | bytes 1130504 | tf_op jit(solution)/shard_map/ppermute | solution.py:34
  40.6 5.5 %collective-permute-start.12 = (f32[1,7,128]{2,1,0:T(8,128)S(1)}, f32[1,7,128]{2,1,0:T(8,128)S(1)}, u32[]{:S(2)}, u32[]{:S(2)}) collective-permute-start(f32[1,7,128]{2,1,0:T(8,128)S(1)} %get-tuple-element.72), channel_id=1, source_target_pairs={{0,8},{8,0},{16,24},{24,16},{32,40},{40,32},{48,56},{56,48},{1,9},... | collective-permute-start | bytes 10760 | tf_op jit(solution)/shard_map/ppermute | solution.py:314

commit v6 on v5

--- a/solution.py
+++ b/solution.py
@@ -122,15 +122,24 @@
         before, here = here, after
 
 
-def smooth_kernel(leads, places, rows, total_rows, members, cycle_days, count, date_ref, days_ref, *refs):
-    sums, (out_hbm, done, sem) = refs[:count], refs[-3:]
+def smooth_kernel(
+    leads, places, rows, total_rows, members, cycle_days, count, extra, date_ref, days_ref, *refs
+):
+    sums, (done, sem) = refs[:count], refs[-2:]
+    if extra:
+        forecast, kept, given = refs[count : count + 3]
+        out_hbm, anomalies, weeks, weeks_sem = refs[-6:-2]
+        weeks[:, 0, :] = forecast[...] - (kept[...] + given[...])
+        copies = [pltpu.make_async_copy(weeks, anomalies, weeks_sem)]
+        copies[0].start()
+    else:
+        out_hbm, copies = refs[-3], []
 
     def tile(row, lead):
         which, place = places[row]
         start = (place * leads + lead) * TILE
         return sums[which][start : start + TILE, :]
 
-    copies = []
     for slot, row in enumerate(rows):
         weights, inverse = neighbour_weights(days_ref, date_ref[0] * total_rows + row, cycle_days)
         inverse = inverse * (1.0 / members)
@@ -150,18 +159,28 @@
         copy.wait()
 
 
-def smooth_rows(date, days, arrays, rows, total_rows, leads, members, cycle_days, cost, into=None):
+def smooth_rows(
+    date, days, arrays, rows, total_rows, leads, members, cycle_days, cost, extra=(), into=None
+):
     places = {row: (i, j) for i, (_, held) in enumerate(arrays) for j, row in enumerate(held)}
     sums = [array for array, _ in arrays]
-    operands = [date, days, *sums] + ([] if into is None else [into])
+    operands = [date, days, *sums, *extra] + ([] if into is None else [into])
+    shapes = [jax.ShapeDtypeStruct((total_rows, leads * TILE, LANES), jnp.float32)]
+    if extra:
+        shapes.append(jax.ShapeDtypeStruct((WEEKS, 1, LANES), jnp.float32))
     return pl.pallas_call(
         functools.partial(
-            smooth_kernel, leads, places, rows, total_rows, members, cycle_days, len(sums)
+            smooth_kernel, leads, places, rows, total_rows, members, cycle_days, len(sums), bool(extra)
         ),
-        in_specs=[SMEM, SMEM] + [VMEM] * len(sums) + ([] if into is None else [HBM]),
-        out_specs=HBM,
-        out_shape=jax.ShapeDtypeStruct((total_rows, leads * TILE, LANES), jnp.float32),
-        scratch_shapes=[
+        in_specs=[SMEM, SMEM]
+        + [VMEM] * (len(sums) + len(extra))
+        + ([] if into is None else [HBM]),
+        out_specs=[HBM] * len(shapes),
+        out_shape=shapes,
+        scratch_shapes=(
+            [pltpu.VMEM((WEEKS, 1, LANES), jnp.float32), pltpu.SemaphoreType.DMA] if extra else []
+        )
+        + [
             pltpu.VMEM((len(rows), leads * TILE, LANES), jnp.float32),
             pltpu.SemaphoreType.DMA((len(rows),)),
         ],
@@ -169,21 +188,6 @@
         cost_estimate=estimate(cost),
         compiler_params=pltpu.CompilerParams(vmem_limit_bytes=8 * MIB),
     )(*operands)
-
-
-def anomaly_kernel(forecast, kept, given, out):
-    out[:, 0, :] = forecast[...] - (kept[...] + given[...])
-
-
-def weekly_anomalies(forecast, kept, given):
-    return pl.pallas_call(
-        anomaly_kernel,
-        in_specs=[VMEM] * 3,
-        out_specs=VMEM,
-        out_shape=jax.ShapeDtypeStruct((WEEKS, 1, LANES), jnp.float32),
-        cost_estimate=estimate(1),
-        compiler_params=pltpu.CompilerParams(vmem_limit_bytes=MIB),
-    )(forecast, kept, given)
 
 
 def count_weeks(leads, bins_ref, counts):
@@ -394,13 +398,14 @@
 
     low = local_sum(own[1], others[0], 0, arrived_0, 0, 2)
     high = local_sum(own[1], others[0], 2, arrived_0, 2, 2)
-    weeks, low, high = lax.optimization_barrier((weeks, low, high))
+    bins, low, high = lax.optimization_barrier((horizon_sevenfold_bin, low, high))
+    forecast = forecast_weeks(bins, prediction_runs[:, 0], leads)
+    weeks, forecast = lax.optimization_barrier((weeks, forecast))
     kept, given = weeks_over_dates(weeks, numbers)
     below = date_shift(high, 1)
     above = date_shift(low, -1)
     middle = local_sum(own[3], others[1], 0, arrived_1, 0, len(second))
 
-    forecast = forecast_weeks(horizon_sevenfold_bin, prediction_runs[:, 0], leads)
 
     arrays = [
         (below, [-2, -1]),
@@ -418,9 +423,11 @@
         members=members,
         cycle_days=cycle_days,
     )
-    smoothed = smooth(arrays[1:-1], list(range(2, rows - 2)), cost=10 * MIB)
-    smoothed = smooth(arrays, [0, 1, rows - 2, rows - 1], cost=1, into=smoothed)
-    return smoothed.reshape(rows, 1, leads, cells), weekly_anomalies(forecast, kept, given)
+    [smoothed] = smooth(arrays[1:-1], list(range(2, rows - 2)), cost=10 * MIB)
+    smoothed, anomalies = smooth(
+        arrays, [0, 1, rows - 2, rows - 1], cost=1, extra=(forecast, kept, given), into=smoothed
+    )
+    return smoothed.reshape(rows, 1, leads, cells), anomalies
 
 
 def solution(mesh):

time: 50.7 us -> 49 us (0.966)
  starting transfers between devices: 20.4 us -> 22.9 us
  waiting for transfers between devices: 14 us -> 12 us
  Pallas kernels: 13.5 us -> 11.6 us
    ppermute x3, waiting for transfers between devices: 7.9 us -> 6 us  [chip_swap(): return lax.ppermute(block, 'ens', [(0, 2), (1, 3), (2, 0), (3, 1)])]
    ppermute x3, waiting for transfers between devices: 4.87 us -> 3.26 us  [weeks_over_dates(): got = lax.ppermute(give, 'date', [(i, i ^ step) for i in range(slots)])]
    ppermute x2, waiting for transfers between devices: 0.01 us -> 1.46 us  [date_shift(): lax.ppermute(block, 'date', [(i, (i + step) % count) for i in range(count)])]
    ppermute x3, starting transfers between devices: 8.09 us -> 9.36 us  [weeks_over_dates(): got = lax.ppermute(give, 'date', [(i, i ^ step) for i in range(slots)])]
    pallas_call x1, Pallas kernels: 2.16 us -> 0.88 us  [weekly_shares(): pl.pallas_call(functools.partial(weekly_kernel, kinds, leads, rows, membe...]
    ppermute x2, starting transfers between devices: 4.2 us -> 5.44 us  [date_shift(): lax.ppermute(block, 'date', [(i, (i + step) % count) for i in range(count)])]
    pallas_call x1 -> x0, Pallas kernels: 0.59 us -> none  [weekly_anomalies(): pl.pallas_call(anomaly_kernel, in_specs=[VMEM] * 3, out_specs=VMEM, out_s...]
  transfers between devices with their start and end apart: 13 -> 13, of which waited for: 5 -> 5; matrix products, arithmetic and copies ran while one was open for 2% -> 2% of each run, Pallas kernels for 21% -> 17%
where the time goes in v6:
time: 49 us; the launch traced here: 49.1 us
  starting transfers between devices  22.9 us (47%)
  waiting for transfers between devices  12 us (24%)
  Pallas kernels  11.6 us (24%)
  between operations  1.49 us (3%)
  other arithmetic  1.04 us (2%)
    ppermute x3, starting transfers between devices, weeks_over_dates(): got = lax.ppermute(give, 'date', [(i, i ^ step) for i in range(slots)])  9.36 us
    ppermute x3, starting transfers between devices, chip_swap(): return lax.ppermute(block, 'ens', [(0, 2), (1, 3), (2, 0), (3, 1)])  6.75 us
    pallas_call x3, Pallas kernels, split_kinds(): pl.pallas_call(functools.partial(split_kernel, kinds, leads, rows, wanted...  6.12 us
    ppermute x3, waiting for transfers between devices, chip_swap(): return lax.ppermute(block, 'ens', [(0, 2), (1, 3), (2, 0), (3, 1)])  6 us
    ppermute x2, starting transfers between devices, date_shift(): lax.ppermute(block, 'date', [(i, (i + step) % count) for i in range(count)])  5.44 us
    pallas_call x2, Pallas kernels, smooth_rows(): pl.pallas_call(functools.partial(smooth_kernel, leads, places, rows, tota...  3.78 us
    ppermute x3, waiting for transfers between devices, weeks_over_dates(): got = lax.ppermute(give, 'date', [(i, i ^ step) for i in range(slots)])  3.26 us
    ppermute x2, waiting for transfers between devices, date_shift(): lax.ppermute(block, 'date', [(i, (i + step) % count) for i in range(count)])  1.46 us
  transfers between devices with their start and end apart: 13, of which 5 were waited for; matrix products, arithmetic and copies ran while one was open for 2% of the time, Pallas kernels for 17%

profile of v6, /device:TPU:8, one launch (start us, length us, event | category | flops | bytes accessed | tf_op | source)
XLA Modules:
  0.0 49.1 jit_solution(14802801338453059028)
XLA Ops:
  0.6 1.5 %shard_map.68 = (bf16[1472,128]{1,0:T(8,128)(2,1)S(1)}, bf16[1472,128]{1,0:T(8,128)(2,1)S(1)}) custom-call(s32[1]{0:T(128)} %bitcast.3.ens_ref, bf16[19136,128]{1,0:T(8,128)(2,1)} %bitcast.24), custom_call_target="tpu_custom_call" | custom-call | flops 1 | bytes 1507328 | tf_op jit(solution)/shard_map/pallas_call | solution.py:84
  2.1 0.1 collective-permute-start
  2.2 0.0 copy-start.1
  2.2 0.0 copy-start.2
  2.2 2.1 %shard_map.69 = (bf16[3312,128]{1,0:T(8,128)(2,1)S(1)}, bf16[3312,128]{1,0:T(8,128)(2,1)S(1)}) custom-call(s32[1]{0:T(128)} %bitcast.3.ens_ref, bf16[19136,128]{1,0:T(8,128)(2,1)} %bitcast.25), custom_call_target="tpu_custom_call" | custom-call | flops 1 | bytes 3391488 | tf_op jit(solution)/shard_map/pallas_call | solution.py:84
  4.3 0.6 %collective-permute-start.5 = (bf16[3312,128]{1,0:T(8,128)(2,1)S(1)}, bf16[3312,128]{1,0:T(8,128)(2,1)S(1)}, u32[]{:S(2)}, u32[]{:S(2)}) collective-permute-start(bf16[3312,128]{1,0:T(8,128)(2,1)S(1)} %get-tuple-element.60), channel_id=1, source_target_pairs={{0,64},{64,0},{128,192},{192,128},{1,65},{65,1},{129,193},{193,129... | collective-permute-start | bytes 2543624 | tf_op jit(solution)/shard_map/ppermute | solution.py:25
  5.6 0.0 copy-done.1
  5.6 0.0 copy-done.2
  5.6 0.9 %shard_map.70 = (f32[16,7,128]{2,1,0:T(8,128)S(1)}, f32[16,7,128]{2,1,0:T(8,128)S(1)}) custom-call(s32[1]{0:T(128)} %bitcast.3.ens_ref, s32[1]{0:T(128)} %bitcast.4.date_ref, s32[104]{0:T(128)S(1)} %copy-done.1, s32[1]{0:T(128)S(6)} %copy.13.position_ref, s32[46]{0:T(128)S(1)} %copy-done.2, bf16[19136,128]{1,0:T(8,128)(2,1)} %bitcast.26), custom_call_target="tpu_custom_call" | custom-call | flops 1 | bytes 1 | tf_op jit(solution)/shard_map/pallas_call | solution.py:257
  6.5 0.0 collective-permute-done
  6.5 0.2 multiply_convert_fusion.1
  6.6 0.1 collective-permute-start.8
  6.8 1.2 %collective-permute-done.8 = f32[16,7,128]{2,1,0:T(8,128)S(1)} collective-permute-done((f32[16,7,128]{2,1,0:T(8,128)S(1)}, f32[16,7,128]{2,1,0:T(8,128)S(1)}, u32[]{:S(2)}, u32[]{:S(2)}) %collective-permute-start.8) | collective-permute-done | bytes 57376 | tf_op jit(solution)/shard_map/ppermute | solution.py:25
  8.0 3.1 %collective-permute-start.9 = (f32[8,7,128]{2,1,0:T(8,128)S(1)}, f32[8,7,128]{2,1,0:T(8,128)S(1)}, u32[]{:S(2)}, u32[]{:S(2)}) collective-permute-start(f32[8,7,128]{2,1,0:T(8,128)S(1)} %slice.37), channel_id=1, source_target_pairs={{0,128},{64,192},{128,0},{192,64},{1,129},{65,193},{129,1},{193,65... | collective-permute-start | bytes 86024 | tf_op jit(solution)/shard_map/ppermute | solution.py:29
  11.1 0.5 collective-permute-start.2
  11.6 2.6 %shard_map.71 = (bf16[1472,128]{1,0:T(8,128)(2,1)S(1)}, bf16[1472,128]{1,0:T(8,128)(2,1)S(1)}, bf16[3312,128]{1,0:T(8,128)(2,1)S(1)}, bf16[3312,128]{1,0:T(8,128)(2,1)S(1)}) custom-call(s32[1]{0:T(128)} %bitcast.3.ens_ref, bf16[19136,128]{1,0:T(8,128)(2,1)} %bitcast.27), custom_call_target="tpu_custom_call" | custom-call | flops 1 | bytes 4898816 | tf_op jit(solution)/shard_map/pallas_call | solution.py:84
  14.2 0.1 collective-permute-start.1
  14.3 0.5 %collective-permute-start.4 = (bf16[3312,128]{1,0:T(8,128)(2,1)S(1)}, bf16[3312,128]{1,0:T(8,128)(2,1)S(1)}, u32[]{:S(2)}, u32[]{:S(2)}) collective-permute-start(bf16[3312,128]{1,0:T(8,128)(2,1)S(1)} %get-tuple-element.58), channel_id=1, source_target_pairs={{0,64},{64,0},{128,192},{192,128},{1,65},{65,1},{129,193},{193,129... | collective-permute-start | bytes 2543624 | tf_op jit(solution)/shard_map/ppermute | solution.py:25
  14.8 0.0 collective-permute-done.9
  14.8 0.0 copy-start
  14.8 0.0 collective-permute-done.5
  14.8 0.3 multiply_convert_fusion
  15.2 3.1 %collective-permute-start.6 = (f16[3312,128]{1,0:T(8,128)(2,1)S(1)}, f16[3312,128]{1,0:T(8,128)(2,1)S(1)}, u32[]{:S(2)}, u32[]{:S(2)}) collective-permute-start(f16[3312,128]{1,0:T(8,128)(2,1)S(1)} %multiply_convert_fusion), channel_id=1, source_target_pairs={{0,128},{64,192},{128,0},{192,64},{1,129},{65,193},{129,1},{193,65... | collective-permute-start | bytes 2543624 | tf_op jit(solution)/shard_map/ppermute | solution.py:29
  18.3 6.0 %collective-permute-done.2 = f16[1472,128]{1,0:T(8,128)(2,1)S(1)} collective-permute-done((f16[1472,128]{1,0:T(8,128)(2,1)S(1)}, f16[1472,128]{1,0:T(8,128)(2,1)S(1)}, u32[]{:S(2)}, u32[]{:S(2)}) %collective-permute-start.2) | collective-permute-done | bytes 376864 | tf_op jit(solution)/shard_map/ppermute | solution.py:29
  24.3 0.0 collective-permute-done.1
  24.3 0.2 multiply_add_fusion.1
  24.5 0.0 copy-done
  24.5 0.8 %shard_map.72.refs_5_ = f32[7,128]{1,0:T(8,128)S(1)} custom-call(s32[46]{0:T(128)S(1)} %copy-done.2, bf16[11,46,128]{2,1,0:T(8,128)(2,1)S(1)} %bitcast.22), custom_call_target="tpu_custom_call" | custom-call | flops 1 | bytes 1 | tf_op jit(solution)/shard_map/pallas_call | solution.py:290
  25.4 8.6 %collective-permute-start.10 = (f32[4,7,128]{2,1,0:T(8,128)S(1)}, f32[4,7,128]{2,1,0:T(8,128)S(1)}, u32[]{:S(2)}, u32[]{:S(2)}) collective-permute-start(f32[4,7,128]{2,1,0:T(8,128)S(1)} %dynamic-slice_bitcast_fusion), channel_id=1, source_target_pairs={{0,32},{8,40},{16,48},{24,56},{32,0},{40,8},{48,16},{56,24},{1,33}... | collective-permute-start | bytes 43016 | tf_op jit(solution)/shard_map/ppermute | solution.py:318
  33.9 1.7 %collective-permute-done.10 = f32[4,7,128]{2,1,0:T(8,128)S(1)} collective-permute-done((f32[4,7,128]{2,1,0:T(8,128)S(1)}, f32[4,7,128]{2,1,0:T(8,128)S(1)}, u32[]{:S(2)}, u32[]{:S(2)}) %collective-permute-start.10) | collective-permute-done | bytes 14368 | tf_op jit(solution)/shard_map/ppermute | solution.py:318
  35.7 0.7 %collective-permute-start.11 = (f32[2,7,128]{2,1,0:T(8,128)S(1)}, f32[2,7,128]{2,1,0:T(8,128)S(1)}, u32[]{:S(2)}, u32[]{:S(2)}) collective-permute-start(f32[2,7,128]{2,1,0:T(8,128)S(1)} %dynamic-slice_bitcast_fusion.1), channel_id=1, source_target_pairs={{0,16},{8,24},{16,0},{24,8},{32,48},{40,56},{48,32},{56,40},{1,17}... | collective-permute-start | bytes 21512 | tf_op jit(solution)/shard_map/ppermute | solution.py:318
  36.4 1.9 %collective-permute-start.3 = (f32[736,128]{1,0:T(8,128)S(1)}, f32[736,128]{1,0:T(8,128)S(1)}, u32[]{:S(2)}, u32[]{:S(2)}) collective-permute-start(f32[736,128]{1,0:T(8,128)S(1)} %get-tuple-element.55.refs_2_.refs_3_), channel_id=1, source_target_pairs={{0,8},{8,16},{16,24},{24,32},{32,40},{40,48},{48,56},{56,0},{1,9},... | collective-permute-start | bytes 1130504 | tf_op jit(solution)/shard_map/ppermute | solution.py:34
  38.3 3.5 %collective-permute-start.7 = (f32[736,128]{1,0:T(8,128)S(1)}, f32[736,128]{1,0:T(8,128)S(1)}, u32[]{:S(2)}, u32[]{:S(2)}) collective-permute-start(f32[736,128]{1,0:T(8,128)S(1)} %get-tuple-element.56.refs_0_.refs_1_), channel_id=1, source_target_pairs={{0,56},{8,0},{16,8},{24,16},{32,24},{40,32},{48,40},{56,48},{1,57}... | collective-permute-start | bytes 1130504 | tf_op jit(solution)/shard_map/ppermute | solution.py:34
  41.8 0.0 collective-permute-done.11
  41.8 0.1 collective-permute-start.12
  41.9 0.0 collective-permute-done.4
  41.9 0.0 collective-permute-done.6
  42.0 0.3 multiply_add_fusion.refs_1_.refs_2_
  42.3 2.1 %shard_map.73.refs_8_ = f32[13,368,128]{2,1,0:T(8,128)} custom-call(s32[1]{0:T(128)} %bitcast.4.date_ref, s32[104]{0:T(128)S(1)} %copy-done.1, f32[736,128]{1,0:T(8,128)S(1)} %get-tuple-element.56.refs_0_.refs_1_, f32[3312,128]{1,0:T(8,128)S(1)} %multiply_add_fusion.refs_1_.refs_2_, f32[736,128]{1,0:T(8,128)S(1)} %get-tuple-element.55.refs_2_.refs_3_), custom_call_target="tpu_custom_call" | custom-call | flops 1 | bytes 10485760 | tf_op jit(solution)/shard_map/pallas_call | solution.py:171
  44.4 1.5 %collective-permute-done.12 = f32[1,7,128]{2,1,0:T(8,128)S(1)} collective-permute-done((f32[1,7,128]{2,1,0:T(8,128)S(1)}, f32[1,7,128]{2,1,0:T(8,128)S(1)}, u32[]{:S(2)}, u32[]{:S(2)}) %collective-permute-start.12) | collective-permute-done | bytes 3616 | tf_op jit(solution)/shard_map/ppermute | solution.py:318
  45.9 1.5 %collective-permute-done.3.refs_0_ = f32[736,128]{1,0:T(8,128)S(1)} collective-permute-done((f32[736,128]{1,0:T(8,128)S(1)}, f32[736,128]{1,0:T(8,128)S(1)}, u32[]{:S(2)}, u32[]{:S(2)}) %collective-permute-start.3) | collective-permute-done | bytes 376864 | tf_op jit(solution)/shard_map/ppermute | solution.py:34
  47.4 0.0 collective-permute-done.7.refs_4_
  47.4 1.7 %shard_map.74 = (f32[13,368,128]{2,1,0:T(8,128)}, f32[7,1,128]{2,1,0:T(1,128)}) custom-call(s32[1]{0:T(128)} %bitcast.4.date_ref, s32[104]{0:T(128)S(1)} %copy-done.1, f32[736,128]{1,0:T(8,128)S(1)} %collective-permute-done.3.refs_0_, f32[736,128]{1,0:T(8,128)S(1)} %get-tuple-element.56.refs_0_.refs_1_, ...), custom_call_target="tpu_custom_call", output_to_operand_aliasing={{0}: (10, {})} | custom-call | flops 1 | bytes 1 | tf_op jit(solution)/shard_map/pallas_call | solution.py:171
  (8 shorter events, 0.0 us)
Async XLA Ops:
  2.1 4.4 %collective-permute-start = (bf16[1472,128]{1,0:T(8,128)(2,1)S(1)}, bf16[1472,128]{1,0:T(8,128)(2,1)S(1)}, u32[]{:S(2)}, u32[]{:S(2)}) collective-permute-start(bf16[1472,128]{1,0:T(8,128)(2,1)S(1)} %get-tuple-element.48), channel_id=1, source_target_pairs={{0,64},{64,0},{128,192},{192,128},{1,65},{65,1},{129,193},{193,129... | collective-permute-start | bytes 1130504 | tf_op jit(solution)/shard_map/ppermute | solution.py:25
  2.2 3.4 %copy-start.1 = (s32[104]{0:T(128)S(1)}, s32[104]{0:T(128)}, u32[]{:S(2)}) copy-start(s32[104]{0:T(128)} %days_ref.5) | copy-start | bytes 1252
  2.2 3.3 %copy-start.2 = (s32[46]{0:T(128)S(1)}, s32[46]{0:T(128)}, u32[]{:S(2)}) copy-start(s32[46]{0:T(128)} %bins_ref.2) | copy-start | bytes 556
  4.3 10.5 %collective-permute-start.5 = (bf16[3312,128]{1,0:T(8,128)(2,1)S(1)}, bf16[3312,128]{1,0:T(8,128)(2,1)S(1)}, u32[]{:S(2)}, u32[]{:S(2)}) collective-permute-start(bf16[3312,128]{1,0:T(8,128)(2,1)S(1)} %get-tuple-element.60), channel_id=1, source_target_pairs={{0,64},{64,0},{128,192},{192,128},{1,65},{65,1},{129,193},{193,129... | collective-permute-start | bytes 2543624 | tf_op jit(solution)/shard_map/ppermute | solution.py:25
  6.6 1.3 %collective-permute-start.8 = (f32[16,7,128]{2,1,0:T(8,128)S(1)}, f32[16,7,128]{2,1,0:T(8,128)S(1)}, u32[]{:S(2)}, u32[]{:S(2)}) collective-permute-start(f32[16,7,128]{2,1,0:T(8,128)S(1)} %get-tuple-element.62), channel_id=1, source_target_pairs={{0,64},{64,0},{128,192},{192,128},{1,65},{65,1},{129,193},{193,129... | collective-permute-start | bytes 172040 | tf_op jit(solution)/shard_map/ppermute | solution.py:25
  8.0 6.8 %collective-permute-start.9 = (f32[8,7,128]{2,1,0:T(8,128)S(1)}, f32[8,7,128]{2,1,0:T(8,128)S(1)}, u32[]{:S(2)}, u32[]{:S(2)}) collective-permute-start(f32[8,7,128]{2,1,0:T(8,128)S(1)} %slice.37), channel_id=1, source_target_pairs={{0,128},{64,192},{128,0},{192,64},{1,129},{65,193},{129,1},{193,65... | collective-permute-start | bytes 86024 | tf_op jit(solution)/shard_map/ppermute | solution.py:29
  11.1 13.2 %collective-permute-start.2 = (f16[1472,128]{1,0:T(8,128)(2,1)S(1)}, f16[1472,128]{1,0:T(8,128)(2,1)S(1)}, u32[]{:S(2)}, u32[]{:S(2)}) collective-permute-start(f16[1472,128]{1,0:T(8,128)(2,1)S(1)} %multiply_convert_fusion.1), channel_id=1, source_target_pairs={{0,128},{64,192},{128,0},{192,64},{1,129},{65,193},{129,1},{193,65... | collective-permute-start | bytes 1130504 | tf_op jit(solution)/shard_map/ppermute | solution.py:29
  14.2 10.1 %collective-permute-start.1 = (bf16[1472,128]{1,0:T(8,128)(2,1)S(1)}, bf16[1472,128]{1,0:T(8,128)(2,1)S(1)}, u32[]{:S(2)}, u32[]{:S(2)}) collective-permute-start(bf16[1472,128]{1,0:T(8,128)(2,1)S(1)} %get-tuple-element.54), channel_id=1, source_target_pairs={{0,64},{64,0},{128,192},{192,128},{1,65},{65,1},{129,193},{193,129... | collective-permute-start | bytes 1130504 | tf_op jit(solution)/shard_map/ppermute | solution.py:25
  14.3 27.6 %collective-permute-start.4 = (bf16[3312,128]{1,0:T(8,128)(2,1)S(1)}, bf16[3312,128]{1,0:T(8,128)(2,1)S(1)}, u32[]{:S(2)}, u32[]{:S(2)}) collective-permute-start(bf16[3312,128]{1,0:T(8,128)(2,1)S(1)} %get-tuple-element.58), channel_id=1, source_target_pairs={{0,64},{64,0},{128,192},{192,128},{1,65},{65,1},{129,193},{193,129... | collective-permute-start | bytes 2543624 | tf_op jit(solution)/shard_map/ppermute | solution.py:25
  14.8 9.7 %copy-start = (bf16[11,1,46,128]{3,2,1,0:T(8,128)(2,1)S(1)}, bf16[11,1,46,128]{3,2,1,0:T(8,128)(2,1)}, u32[]{:S(2)}) copy-start(bf16[11,1,46,128]{3,2,1,0:T(8,128)(2,1)} %param.9) | copy-start | bytes 388612
  15.2 26.8 %collective-permute-start.6 = (f16[3312,128]{1,0:T(8,128)(2,1)S(1)}, f16[3312,128]{1,0:T(8,128)(2,1)S(1)}, u32[]{:S(2)}, u32[]{:S(2)}) collective-permute-start(f16[3312,128]{1,0:T(8,128)(2,1)S(1)} %multiply_convert_fusion), channel_id=1, source_target_pairs={{0,128},{64,192},{128,0},{192,64},{1,129},{65,193},{129,1},{193,65... | collective-permute-start | bytes 2543624 | tf_op jit(solution)/shard_map/ppermute | solution.py:29
  25.4 10.3 %collective-permute-start.10 = (f32[4,7,128]{2,1,0:T(8,128)S(1)}, f32[4,7,128]{2,1,0:T(8,128)S(1)}, u32[]{:S(2)}, u32[]{:S(2)}) collective-permute-start(f32[4,7,128]{2,1,0:T(8,128)S(1)} %dynamic-slice_bitcast_fusion), channel_id=1, source_target_pairs={{0,32},{8,40},{16,48},{24,56},{32,0},{40,8},{48,16},{56,24},{1,33}... | collective-permute-start | bytes 43016 | tf_op jit(solution)/shard_map/ppermute | solution.py:318
  35.7 6.2 %collective-permute-start.11 = (f32[2,7,128]{2,1,0:T(8,128)S(1)}, f32[2,7,128]{2,1,0:T(8,128)S(1)}, u32[]{:S(2)}, u32[]{:S(2)}) collective-permute-start(f32[2,7,128]{2,1,0:T(8,128)S(1)} %dynamic-slice_bitcast_fusion.1), channel_id=1, source_target_pairs={{0,16},{8,24},{16,0},{24,8},{32,48},{40,56},{48,32},{56,40},{1,17}... | collective-permute-start | bytes 21512 | tf_op jit(solution)/shard_map/ppermute | solution.py:318
  36.4 11.0 %collective-permute-start.3 = (f32[736,128]{1,0:T(8,128)S(1)}, f32[736,128]{1,0:T(8,128)S(1)}, u32[]{:S(2)}, u32[]{:S(2)}) collective-permute-start(f32[736,128]{1,0:T(8,128)S(1)} %get-tuple-element.55.refs_2_.refs_3_), channel_id=1, source_target_pairs={{0,8},{8,16},{16,24},{24,32},{32,40},{40,48},{48,56},{56,0},{1,9},... | collective-permute-start | bytes 1130504 | tf_op jit(solution)/shard_map/ppermute | solution.py:34
  38.3 9.1 %collective-permute-start.7 = (f32[736,128]{1,0:T(8,128)S(1)}, f32[736,128]{1,0:T(8,128)S(1)}, u32[]{:S(2)}, u32[]{:S(2)}) collective-permute-start(f32[736,128]{1,0:T(8,128)S(1)} %get-tuple-element.56.refs_0_.refs_1_), channel_id=1, source_target_pairs={{0,56},{8,0},{16,8},{24,16},{32,24},{40,32},{48,40},{56,48},{1,57}... | collective-permute-start | bytes 1130504 | tf_op jit(solution)/shard_map/ppermute | solution.py:34
  41.8 4.1 %collective-permute-start.12 = (f32[1,7,128]{2,1,0:T(8,128)S(1)}, f32[1,7,128]{2,1,0:T(8,128)S(1)}, u32[]{:S(2)}, u32[]{:S(2)}) collective-permute-start(f32[1,7,128]{2,1,0:T(8,128)S(1)} %get-tuple-element.80), channel_id=1, source_target_pairs={{0,8},{8,0},{16,24},{24,16},{32,40},{40,32},{48,56},{56,48},{1,9},... | collective-permute-start | bytes 10760 | tf_op jit(solution)/shard_map/ppermute | solution.py:318

commit v7 on v6

--- a/solution.py
+++ b/solution.py
@@ -346,18 +346,17 @@
     second = list(range(2, rows - 2))
     split = functools.partial(split_kinds, kinds=kinds, leads=leads)
 
-    def for_x(flat, members):
-        return split(flat, ens, rows=members, wanted=[(members, True, True), (members, True, False)])
-
     def pair_sum(mine, other):
         return ((mine.astype(jnp.float32) + other.astype(jnp.float32)) * SCALE).astype(jnp.float16)
 
-    theirs_0, mine_0 = for_x(flat, first)
-    got_0 = core_swap(theirs_0)
-    flat, mine_0 = lax.optimization_barrier((flat, mine_0))
-    theirs_1, mine_1 = for_x(flat, second)
-    got_1 = core_swap(theirs_1)
-    flat, mine_1 = lax.optimization_barrier((flat, mine_1))
+    theirs_0, mine_0, theirs_1, mine_1 = split(
+        flat,
+        ens,
+        rows=first + second,
+        wanted=[(part, True, other) for part in (first, second) for other in (True, False)],
+    )
+    got_0, got_1 = core_swap(theirs_0), core_swap(theirs_1)
+    flat, mine_0, mine_1 = lax.optimization_barrier((flat, mine_0, mine_1))
     weeks_give, weeks_keep = weekly_shares(
         ens,
         date,

time: 49 us -> 47.5 us (0.969)
  Pallas kernels: 11.6 us -> 10.7 us
  starting transfers between devices: 22.9 us -> 22.4 us
    ppermute x2, starting transfers between devices: 5.44 us -> 3.24 us  [date_shift(): lax.ppermute(block, 'date', [(i, (i + step) % count) for i in range(count)])]
    ppermute x3, starting transfers between devices: 9.36 us -> 11.1 us  [weeks_over_dates(): got = lax.ppermute(give, 'date', [(i, i ^ step) for i in range(slots)])]
    pallas_call x3 -> x2, Pallas kernels: 6.12 us -> 5.14 us  [split_kinds(): pl.pallas_call(functools.partial(split_kernel, kinds, leads, rows, wanted...]
    ppermute x2, waiting for transfers between devices: 1.46 us -> 0.9 us  [date_shift(): lax.ppermute(block, 'date', [(i, (i + step) % count) for i in range(count)])]
    ppermute x3, waiting for transfers between devices: 3.26 us -> 3.81 us  [weeks_over_dates(): got = lax.ppermute(give, 'date', [(i, i ^ step) for i in range(slots)])]
  transfers between devices with their start and end apart: 13 -> 13, of which waited for: 5 -> 5; matrix products, arithmetic and copies ran while one was open for 2% -> 2% of each run, Pallas kernels for 17% -> 13%
where the time goes in v7:
time: 47.5 us
  starting transfers between devices  22.4 us (47%)
  waiting for transfers between devices  11.9 us (25%)
  Pallas kernels  10.7 us (23%)
  between operations  1.48 us (3%)
  other arithmetic  1.04 us (2%)
    ppermute x3, starting transfers between devices, weeks_over_dates(): got = lax.ppermute(give, 'date', [(i, i ^ step) for i in range(slots)])  11.1 us
    ppermute x3, starting transfers between devices, chip_swap(): return lax.ppermute(block, 'ens', [(0, 2), (1, 3), (2, 0), (3, 1)])  6.75 us
    ppermute x3, waiting for transfers between devices, chip_swap(): return lax.ppermute(block, 'ens', [(0, 2), (1, 3), (2, 0), (3, 1)])  6 us
    pallas_call x2, Pallas kernels, split_kinds(): pl.pallas_call(functools.partial(split_kernel, kinds, leads, rows, wanted...  5.14 us
    ppermute x3, waiting for transfers between devices, weeks_over_dates(): got = lax.ppermute(give, 'date', [(i, i ^ step) for i in range(slots)])  3.81 us
    pallas_call x2, Pallas kernels, smooth_rows(): pl.pallas_call(functools.partial(smooth_kernel, leads, places, rows, tota...  3.78 us
    ppermute x2, starting transfers between devices, date_shift(): lax.ppermute(block, 'date', [(i, (i + step) % count) for i in range(count)])  3.24 us
    ppermute x5, starting transfers between devices, core_swap(): return lax.ppermute(block, 'ens', [(0, 1), (1, 0), (2, 3), (3, 2)])  1.37 us
  transfers between devices with their start and end apart: 13, of which 5 were waited for; matrix products, arithmetic and copies ran while one was open for 2% of the time, Pallas kernels for 13%

profile of v7, /device:TPU:8, one launch (start us, length us, event | category | flops | bytes accessed | tf_op | source)
XLA Modules:
  0.0 47.5 jit_solution(17861248462148335374)
XLA Ops:
  0.6 0.0 copy-start.1
  0.7 0.0 copy-start.2
  0.7 2.6 %shard_map.68 = (bf16[1472,128]{1,0:T(8,128)(2,1)S(1)}, bf16[1472,128]{1,0:T(8,128)(2,1)S(1)}, bf16[3312,128]{1,0:T(8,128)(2,1)S(1)}, bf16[3312,128]{1,0:T(8,128)(2,1)S(1)}) custom-call(s32[1]{0:T(128)} %bitcast.3.ens_ref, bf16[19136,128]{1,0:T(8,128)(2,1)} %bitcast.24), custom_call_target="tpu_custom_call" | custom-call | flops 1 | bytes 4898816 | tf_op jit(solution)/shard_map/pallas_call | solution.py:84
  3.2 0.1 collective-permute-start
  3.3 0.5 %collective-permute-start.5 = (bf16[3312,128]{1,0:T(8,128)(2,1)S(1)}, bf16[3312,128]{1,0:T(8,128)(2,1)S(1)}, u32[]{:S(2)}, u32[]{:S(2)}) collective-permute-start(bf16[3312,128]{1,0:T(8,128)(2,1)S(1)} %get-tuple-element.58), channel_id=1, source_target_pairs={{0,64},{64,0},{128,192},{192,128},{1,65},{65,1},{129,193},{193,129... | collective-permute-start | bytes 2543624 | tf_op jit(solution)/shard_map/ppermute | solution.py:25
  4.5 0.0 copy-done.1
  4.5 0.0 copy-done.2
  4.5 0.9 %shard_map.69 = (f32[16,7,128]{2,1,0:T(8,128)S(1)}, f32[16,7,128]{2,1,0:T(8,128)S(1)}) custom-call(s32[1]{0:T(128)} %bitcast.3.ens_ref, s32[1]{0:T(128)} %bitcast.4.date_ref, s32[104]{0:T(128)S(1)} %copy-done.1, s32[1]{0:T(128)S(6)} %copy.13.position_ref, s32[46]{0:T(128)S(1)} %copy-done.2, bf16[19136,128]{1,0:T(8,128)(2,1)} %bitcast.25), custom_call_target="tpu_custom_call" | custom-call | flops 1 | bytes 1 | tf_op jit(solution)/shard_map/pallas_call | solution.py:257
  5.4 0.0 collective-permute-done
  5.4 0.2 multiply_convert_fusion.1
  5.6 0.2 collective-permute-start.8
  5.8 1.2 %collective-permute-done.8 = f32[16,7,128]{2,1,0:T(8,128)S(1)} collective-permute-done((f32[16,7,128]{2,1,0:T(8,128)S(1)}, f32[16,7,128]{2,1,0:T(8,128)S(1)}, u32[]{:S(2)}, u32[]{:S(2)}) %collective-permute-start.8) | collective-permute-done | bytes 57376 | tf_op jit(solution)/shard_map/ppermute | solution.py:25
  6.9 3.1 %collective-permute-start.9 = (f32[8,7,128]{2,1,0:T(8,128)S(1)}, f32[8,7,128]{2,1,0:T(8,128)S(1)}, u32[]{:S(2)}, u32[]{:S(2)}) collective-permute-start(f32[8,7,128]{2,1,0:T(8,128)S(1)} %slice.37), channel_id=1, source_target_pairs={{0,128},{64,192},{128,0},{192,64},{1,129},{65,193},{129,1},{193,65... | collective-permute-start | bytes 86024 | tf_op jit(solution)/shard_map/ppermute | solution.py:29
  10.1 0.5 %collective-permute-start.2 = (f16[1472,128]{1,0:T(8,128)(2,1)S(1)}, f16[1472,128]{1,0:T(8,128)(2,1)S(1)}, u32[]{:S(2)}, u32[]{:S(2)}) collective-permute-start(f16[1472,128]{1,0:T(8,128)(2,1)S(1)} %multiply_convert_fusion.1), channel_id=1, source_target_pairs={{0,128},{64,192},{128,0},{192,64},{1,129},{65,193},{129,1},{193,65... | collective-permute-start | bytes 1130504 | tf_op jit(solution)/shard_map/ppermute | solution.py:29
  10.6 2.6 %shard_map.70 = (bf16[1472,128]{1,0:T(8,128)(2,1)S(1)}, bf16[1472,128]{1,0:T(8,128)(2,1)S(1)}, bf16[3312,128]{1,0:T(8,128)(2,1)S(1)}, bf16[3312,128]{1,0:T(8,128)(2,1)S(1)}) custom-call(s32[1]{0:T(128)} %bitcast.3.ens_ref, bf16[19136,128]{1,0:T(8,128)(2,1)} %bitcast.26), custom_call_target="tpu_custom_call" | custom-call | flops 1 | bytes 4898816 | tf_op jit(solution)/shard_map/pallas_call | solution.py:84
  13.1 0.1 collective-permute-start.1
  13.2 0.5 %collective-permute-start.4 = (bf16[3312,128]{1,0:T(8,128)(2,1)S(1)}, bf16[3312,128]{1,0:T(8,128)(2,1)S(1)}, u32[]{:S(2)}, u32[]{:S(2)}) collective-permute-start(bf16[3312,128]{1,0:T(8,128)(2,1)S(1)} %get-tuple-element.56), channel_id=1, source_target_pairs={{0,64},{64,0},{128,192},{192,128},{1,65},{65,1},{129,193},{193,129... | collective-permute-start | bytes 2543624 | tf_op jit(solution)/shard_map/ppermute | solution.py:25
  13.7 0.0 collective-permute-done.9
  13.7 0.0 copy-start
  13.8 0.0 collective-permute-done.5
  13.8 0.3 multiply_convert_fusion
  14.1 3.1 %collective-permute-start.6 = (f16[3312,128]{1,0:T(8,128)(2,1)S(1)}, f16[3312,128]{1,0:T(8,128)(2,1)S(1)}, u32[]{:S(2)}, u32[]{:S(2)}) collective-permute-start(f16[3312,128]{1,0:T(8,128)(2,1)S(1)} %multiply_convert_fusion), channel_id=1, source_target_pairs={{0,128},{64,192},{128,0},{192,64},{1,129},{65,193},{129,1},{193,65... | collective-permute-start | bytes 2543624 | tf_op jit(solution)/shard_map/ppermute | solution.py:29
  17.2 6.0 %collective-permute-done.2 = f16[1472,128]{1,0:T(8,128)(2,1)S(1)} collective-permute-done((f16[1472,128]{1,0:T(8,128)(2,1)S(1)}, f16[1472,128]{1,0:T(8,128)(2,1)S(1)}, u32[]{:S(2)}, u32[]{:S(2)}) %collective-permute-start.2) | collective-permute-done | bytes 376864 | tf_op jit(solution)/shard_map/ppermute | solution.py:29
  23.2 0.0 collective-permute-done.1
  23.2 0.2 multiply_add_fusion.1
  23.4 0.0 copy-done
  23.4 0.8 %shard_map.71.refs_5_ = f32[7,128]{1,0:T(8,128)S(1)} custom-call(s32[46]{0:T(128)S(1)} %copy-done.2, bf16[11,46,128]{2,1,0:T(8,128)(2,1)S(1)} %bitcast.22), custom_call_target="tpu_custom_call" | custom-call | flops 1 | bytes 1 | tf_op jit(solution)/shard_map/pallas_call | solution.py:290
  24.3 7.3 %collective-permute-start.10 = (f32[4,7,128]{2,1,0:T(8,128)S(1)}, f32[4,7,128]{2,1,0:T(8,128)S(1)}, u32[]{:S(2)}, u32[]{:S(2)}) collective-permute-start(f32[4,7,128]{2,1,0:T(8,128)S(1)} %dynamic-slice_bitcast_fusion), channel_id=1, source_target_pairs={{0,32},{8,40},{16,48},{24,56},{32,0},{40,8},{48,16},{56,24},{1,33}... | collective-permute-start | bytes 43016 | tf_op jit(solution)/shard_map/ppermute | solution.py:318
  31.6 1.7 %collective-permute-done.10 = f32[4,7,128]{2,1,0:T(8,128)S(1)} collective-permute-done((f32[4,7,128]{2,1,0:T(8,128)S(1)}, f32[4,7,128]{2,1,0:T(8,128)S(1)}, u32[]{:S(2)}, u32[]{:S(2)}) %collective-permute-start.10) | collective-permute-done | bytes 14368 | tf_op jit(solution)/shard_map/ppermute | solution.py:318
  33.3 3.7 %collective-permute-start.11 = (f32[2,7,128]{2,1,0:T(8,128)S(1)}, f32[2,7,128]{2,1,0:T(8,128)S(1)}, u32[]{:S(2)}, u32[]{:S(2)}) collective-permute-start(f32[2,7,128]{2,1,0:T(8,128)S(1)} %dynamic-slice_bitcast_fusion.1), channel_id=1, source_target_pairs={{0,16},{8,24},{16,0},{24,8},{32,48},{40,56},{48,32},{56,40},{1,17}... | collective-permute-start | bytes 21512 | tf_op jit(solution)/shard_map/ppermute | solution.py:318
  37.0 0.3 collective-permute-start.3
  37.3 3.0 %collective-permute-start.7 = (f32[736,128]{1,0:T(8,128)S(1)}, f32[736,128]{1,0:T(8,128)S(1)}, u32[]{:S(2)}, u32[]{:S(2)}) collective-permute-start(f32[736,128]{1,0:T(8,128)S(1)} %get-tuple-element.54.refs_0_.refs_1_), channel_id=1, source_target_pairs={{0,56},{8,0},{16,8},{24,16},{32,24},{40,32},{48,40},{56,48},{1,57}... | collective-permute-start | bytes 1130504 | tf_op jit(solution)/shard_map/ppermute | solution.py:34
  40.3 0.0 collective-permute-done.11
  40.3 0.1 collective-permute-start.12
  40.4 0.0 collective-permute-done.4
  40.4 0.0 collective-permute-done.6
  40.4 0.3 multiply_add_fusion.refs_1_.refs_2_
  40.7 2.1 %shard_map.72.refs_8_ = f32[13,368,128]{2,1,0:T(8,128)} custom-call(s32[1]{0:T(128)} %bitcast.4.date_ref, s32[104]{0:T(128)S(1)} %copy-done.1, f32[736,128]{1,0:T(8,128)S(1)} %get-tuple-element.54.refs_0_.refs_1_, f32[3312,128]{1,0:T(8,128)S(1)} %multiply_add_fusion.refs_1_.refs_2_, f32[736,128]{1,0:T(8,128)S(1)} %get-tuple-element.53.refs_2_.refs_3_), custom_call_target="tpu_custom_call" | custom-call | flops 1 | bytes 10485760 | tf_op jit(solution)/shard_map/pallas_call | solution.py:171
  42.9 2.1 %collective-permute-done.12 = f32[1,7,128]{2,1,0:T(8,128)S(1)} collective-permute-done((f32[1,7,128]{2,1,0:T(8,128)S(1)}, f32[1,7,128]{2,1,0:T(8,128)S(1)}, u32[]{:S(2)}, u32[]{:S(2)}) %collective-permute-start.12) | collective-permute-done | bytes 3616 | tf_op jit(solution)/shard_map/ppermute | solution.py:318
  45.0 0.9 %collective-permute-done.3.refs_0_ = f32[736,128]{1,0:T(8,128)S(1)} collective-permute-done((f32[736,128]{1,0:T(8,128)S(1)}, f32[736,128]{1,0:T(8,128)S(1)}, u32[]{:S(2)}, u32[]{:S(2)}) %collective-permute-start.3) | collective-permute-done | bytes 376864 | tf_op jit(solution)/shard_map/ppermute | solution.py:34
  45.8 0.0 collective-permute-done.7.refs_4_
  45.9 1.7 %shard_map.73 = (f32[13,368,128]{2,1,0:T(8,128)}, f32[7,1,128]{2,1,0:T(1,128)}) custom-call(s32[1]{0:T(128)} %bitcast.4.date_ref, s32[104]{0:T(128)S(1)} %copy-done.1, f32[736,128]{1,0:T(8,128)S(1)} %collective-permute-done.3.refs_0_, f32[736,128]{1,0:T(8,128)S(1)} %get-tuple-element.54.refs_0_.refs_1_, ...), custom_call_target="tpu_custom_call", output_to_operand_aliasing={{0}: (10, {})} | custom-call | flops 1 | bytes 1 | tf_op jit(solution)/shard_map/pallas_call | solution.py:171
  (8 shorter events, 0.0 us)
Async XLA Ops:
  0.6 3.9 %copy-start.1 = (s32[104]{0:T(128)S(1)}, s32[104]{0:T(128)}, u32[]{:S(2)}) copy-start(s32[104]{0:T(128)} %days_ref.5) | copy-start | bytes 1252
  0.7 3.9 %copy-start.2 = (s32[46]{0:T(128)S(1)}, s32[46]{0:T(128)}, u32[]{:S(2)}) copy-start(s32[46]{0:T(128)} %bins_ref.2) | copy-start | bytes 556
  3.2 2.2 %collective-permute-start = (bf16[1472,128]{1,0:T(8,128)(2,1)S(1)}, bf16[1472,128]{1,0:T(8,128)(2,1)S(1)}, u32[]{:S(2)}, u32[]{:S(2)}) collective-permute-start(bf16[1472,128]{1,0:T(8,128)(2,1)S(1)} %get-tuple-element.46), channel_id=1, source_target_pairs={{0,64},{64,0},{128,192},{192,128},{1,65},{65,1},{129,193},{193,129... | collective-permute-start | bytes 1130504 | tf_op jit(solution)/shard_map/ppermute | solution.py:25
  3.3 10.4 %collective-permute-start.5 = (bf16[3312,128]{1,0:T(8,128)(2,1)S(1)}, bf16[3312,128]{1,0:T(8,128)(2,1)S(1)}, u32[]{:S(2)}, u32[]{:S(2)}) collective-permute-start(bf16[3312,128]{1,0:T(8,128)(2,1)S(1)} %get-tuple-element.58), channel_id=1, source_target_pairs={{0,64},{64,0},{128,192},{192,128},{1,65},{65,1},{129,193},{193,129... | collective-permute-start | bytes 2543624 | tf_op jit(solution)/shard_map/ppermute | solution.py:25
  5.6 1.3 %collective-permute-start.8 = (f32[16,7,128]{2,1,0:T(8,128)S(1)}, f32[16,7,128]{2,1,0:T(8,128)S(1)}, u32[]{:S(2)}, u32[]{:S(2)}) collective-permute-start(f32[16,7,128]{2,1,0:T(8,128)S(1)} %get-tuple-element.60), channel_id=1, source_target_pairs={{0,64},{64,0},{128,192},{192,128},{1,65},{65,1},{129,193},{193,129... | collective-permute-start | bytes 172040 | tf_op jit(solution)/shard_map/ppermute | solution.py:25
  6.9 6.8 %collective-permute-start.9 = (f32[8,7,128]{2,1,0:T(8,128)S(1)}, f32[8,7,128]{2,1,0:T(8,128)S(1)}, u32[]{:S(2)}, u32[]{:S(2)}) collective-permute-start(f32[8,7,128]{2,1,0:T(8,128)S(1)} %slice.37), channel_id=1, source_target_pairs={{0,128},{64,192},{128,0},{192,64},{1,129},{65,193},{129,1},{193,65... | collective-permute-start | bytes 86024 | tf_op jit(solution)/shard_map/ppermute | solution.py:29
  10.1 13.2 %collective-permute-start.2 = (f16[1472,128]{1,0:T(8,128)(2,1)S(1)}, f16[1472,128]{1,0:T(8,128)(2,1)S(1)}, u32[]{:S(2)}, u32[]{:S(2)}) collective-permute-start(f16[1472,128]{1,0:T(8,128)(2,1)S(1)} %multiply_convert_fusion.1), channel_id=1, source_target_pairs={{0,128},{64,192},{128,0},{192,64},{1,129},{65,193},{129,1},{193,65... | collective-permute-start | bytes 1130504 | tf_op jit(solution)/shard_map/ppermute | solution.py:29
  13.1 10.1 %collective-permute-start.1 = (bf16[1472,128]{1,0:T(8,128)(2,1)S(1)}, bf16[1472,128]{1,0:T(8,128)(2,1)S(1)}, u32[]{:S(2)}, u32[]{:S(2)}) collective-permute-start(bf16[1472,128]{1,0:T(8,128)(2,1)S(1)} %get-tuple-element.52), channel_id=1, source_target_pairs={{0,64},{64,0},{128,192},{192,128},{1,65},{65,1},{129,193},{193,129... | collective-permute-start | bytes 1130504 | tf_op jit(solution)/shard_map/ppermute | solution.py:25
  13.2 27.2 %collective-permute-start.4 = (bf16[3312,128]{1,0:T(8,128)(2,1)S(1)}, bf16[3312,128]{1,0:T(8,128)(2,1)S(1)}, u32[]{:S(2)}, u32[]{:S(2)}) collective-permute-start(bf16[3312,128]{1,0:T(8,128)(2,1)S(1)} %get-tuple-element.56), channel_id=1, source_target_pairs={{0,64},{64,0},{128,192},{192,128},{1,65},{65,1},{129,193},{193,129... | collective-permute-start | bytes 2543624 | tf_op jit(solution)/shard_map/ppermute | solution.py:25
  13.7 9.7 %copy-start = (bf16[11,1,46,128]{3,2,1,0:T(8,128)(2,1)S(1)}, bf16[11,1,46,128]{3,2,1,0:T(8,128)(2,1)}, u32[]{:S(2)}) copy-start(bf16[11,1,46,128]{3,2,1,0:T(8,128)(2,1)} %param.9) | copy-start | bytes 388612
  14.1 26.3 %collective-permute-start.6 = (f16[3312,128]{1,0:T(8,128)(2,1)S(1)}, f16[3312,128]{1,0:T(8,128)(2,1)S(1)}, u32[]{:S(2)}, u32[]{:S(2)}) collective-permute-start(f16[3312,128]{1,0:T(8,128)(2,1)S(1)} %multiply_convert_fusion), channel_id=1, source_target_pairs={{0,128},{64,192},{128,0},{192,64},{1,129},{65,193},{129,1},{193,65... | collective-permute-start | bytes 2543624 | tf_op jit(solution)/shard_map/ppermute | solution.py:29
  24.3 9.0 %collective-permute-start.10 = (f32[4,7,128]{2,1,0:T(8,128)S(1)}, f32[4,7,128]{2,1,0:T(8,128)S(1)}, u32[]{:S(2)}, u32[]{:S(2)}) collective-permute-start(f32[4,7,128]{2,1,0:T(8,128)S(1)} %dynamic-slice_bitcast_fusion), channel_id=1, source_target_pairs={{0,32},{8,40},{16,48},{24,56},{32,0},{40,8},{48,16},{56,24},{1,33}... | collective-permute-start | bytes 43016 | tf_op jit(solution)/shard_map/ppermute | solution.py:318
  33.3 7.0 %collective-permute-start.11 = (f32[2,7,128]{2,1,0:T(8,128)S(1)}, f32[2,7,128]{2,1,0:T(8,128)S(1)}, u32[]{:S(2)}, u32[]{:S(2)}) collective-permute-start(f32[2,7,128]{2,1,0:T(8,128)S(1)} %dynamic-slice_bitcast_fusion.1), channel_id=1, source_target_pairs={{0,16},{8,24},{16,0},{24,8},{32,48},{40,56},{48,32},{56,40},{1,17}... | collective-permute-start | bytes 21512 | tf_op jit(solution)/shard_map/ppermute | solution.py:318
  37.0 8.8 %collective-permute-start.3 = (f32[736,128]{1,0:T(8,128)S(1)}, f32[736,128]{1,0:T(8,128)S(1)}, u32[]{:S(2)}, u32[]{:S(2)}) collective-permute-start(f32[736,128]{1,0:T(8,128)S(1)} %get-tuple-element.53.refs_2_.refs_3_), channel_id=1, source_target_pairs={{0,8},{8,16},{16,24},{24,32},{32,40},{40,48},{48,56},{56,0},{1,9},... | collective-permute-start | bytes 1130504 | tf_op jit(solution)/shard_map/ppermute | solution.py:34
  37.3 8.5 %collective-permute-start.7 = (f32[736,128]{1,0:T(8,128)S(1)}, f32[736,128]{1,0:T(8,128)S(1)}, u32[]{:S(2)}, u32[]{:S(2)}) collective-permute-start(f32[736,128]{1,0:T(8,128)S(1)} %get-tuple-element.54.refs_0_.refs_1_), channel_id=1, source_target_pairs={{0,56},{8,0},{16,8},{24,16},{32,24},{40,32},{48,40},{56,48},{1,57}... | collective-permute-start | bytes 1130504 | tf_op jit(solution)/shard_map/ppermute | solution.py:34
  40.3 4.7 %collective-permute-start.12 = (f32[1,7,128]{2,1,0:T(8,128)S(1)}, f32[1,7,128]{2,1,0:T(8,128)S(1)}, u32[]{:S(2)}, u32[]{:S(2)}) collective-permute-start(f32[1,7,128]{2,1,0:T(8,128)S(1)} %get-tuple-element.78), channel_id=1, source_target_pairs={{0,8},{8,0},{16,24},{24,16},{32,40},{40,32},{48,56},{56,48},{1,9},... | collective-permute-start | bytes 10760 | tf_op jit(solution)/shard_map/ppermute | solution.py:318

commit v8 on v7

--- a/solution.py
+++ b/solution.py
@@ -370,7 +370,6 @@
         members,
         cycle_days,
     )
-    mine_0, weeks_keep = lax.optimization_barrier((mine_0, weeks_keep))
     packed_0 = pair_sum(mine_0, got_0)
     packed_0, weeks_give = lax.optimization_barrier((packed_0, weeks_give))
     weeks_got = core_swap(weeks_give)

time: 47.5 us -> 47.3 us (level); the launches traced: 47.5 us -> 46.6 us
  waiting for transfers between devices: 11.9 us -> 11.1 us
    ppermute x3, starting transfers between devices: 11.1 us -> 10.2 us  [weeks_over_dates(): got = lax.ppermute(give, 'date', [(i, i ^ step) for i in range(slots)])]
    ppermute x2, waiting for transfers between devices: 0.9 us -> 0.01 us  [date_shift(): lax.ppermute(block, 'date', [(i, (i + step) % count) for i in range(count)])]
    ppermute x2, starting transfers between devices: 3.24 us -> 4.05 us  [date_shift(): lax.ppermute(block, 'date', [(i, (i + step) % count) for i in range(count)])]
  transfers between devices with their start and end apart: 13 -> 13, of which waited for: 5 -> 4; matrix products, arithmetic and copies ran while one was open for 2% -> 2% of each run, Pallas kernels for 13% -> 14%
where the time goes in v8:
time: 47.3 us; the launch traced here: 46.6 us
  starting transfers between devices  22.3 us (47%)
  waiting for transfers between devices  11.1 us (23%)
  Pallas kernels  10.7 us (23%)
  between operations  1.45 us (3%)
  other arithmetic  1.03 us (2%)
    ppermute x3, starting transfers between devices, weeks_over_dates(): got = lax.ppermute(give, 'date', [(i, i ^ step) for i in range(slots)])  10.2 us
    ppermute x3, starting transfers between devices, chip_swap(): return lax.ppermute(block, 'ens', [(0, 2), (1, 3), (2, 0), (3, 1)])  6.75 us
    ppermute x3, waiting for transfers between devices, chip_swap(): return lax.ppermute(block, 'ens', [(0, 2), (1, 3), (2, 0), (3, 1)])  6.02 us
    pallas_call x2, Pallas kernels, split_kinds(): pl.pallas_call(functools.partial(split_kernel, kinds, leads, rows, wanted...  5.14 us
    ppermute x2, starting transfers between devices, date_shift(): lax.ppermute(block, 'date', [(i, (i + step) % count) for i in range(count)])  4.05 us
    ppermute x3, waiting for transfers between devices, weeks_over_dates(): got = lax.ppermute(give, 'date', [(i, i ^ step) for i in range(slots)])  3.95 us
    pallas_call x2, Pallas kernels, smooth_rows(): pl.pallas_call(functools.partial(smooth_kernel, leads, places, rows, tota...  3.79 us
    ppermute x5, starting transfers between devices, core_swap(): return lax.ppermute(block, 'ens', [(0, 1), (1, 0), (2, 3), (3, 2)])  1.37 us
  transfers between devices with their start and end apart: 13, of which 4 were waited for; matrix products, arithmetic and copies ran while one was open for 2% of the time, Pallas kernels for 14%

profile of v8, /device:TPU:8, one launch (start us, length us, event | category | flops | bytes accessed | tf_op | source)
XLA Modules:
  0.0 46.6 jit_solution(17861248462148335374)
XLA Ops:
  0.6 0.0 copy-start.1
  0.7 0.0 copy-start.2
  0.7 2.6 %shard_map.68 = (bf16[1472,128]{1,0:T(8,128)(2,1)S(1)}, bf16[1472,128]{1,0:T(8,128)(2,1)S(1)}, bf16[3312,128]{1,0:T(8,128)(2,1)S(1)}, bf16[3312,128]{1,0:T(8,128)(2,1)S(1)}) custom-call(s32[1]{0:T(128)} %bitcast.3.ens_ref, bf16[19136,128]{1,0:T(8,128)(2,1)} %bitcast.24), custom_call_target="tpu_custom_call" | custom-call | flops 1 | bytes 4898816 | tf_op jit(solution)/shard_map/pallas_call | solution.py:84
  3.2 0.1 collective-permute-start
  3.3 0.5 %collective-permute-start.5 = (bf16[3312,128]{1,0:T(8,128)(2,1)S(1)}, bf16[3312,128]{1,0:T(8,128)(2,1)S(1)}, u32[]{:S(2)}, u32[]{:S(2)}) collective-permute-start(bf16[3312,128]{1,0:T(8,128)(2,1)S(1)} %get-tuple-element.54), channel_id=1, source_target_pairs={{0,64},{64,0},{128,192},{192,128},{1,65},{65,1},{129,193},{193,129... | collective-permute-start | bytes 2543624 | tf_op jit(solution)/shard_map/ppermute | solution.py:25
  4.5 0.0 copy-done.1
  4.5 0.0 copy-done.2
  4.5 0.9 %shard_map.69 = (f32[16,7,128]{2,1,0:T(8,128)S(1)}, f32[16,7,128]{2,1,0:T(8,128)S(1)}) custom-call(s32[1]{0:T(128)} %bitcast.3.ens_ref, s32[1]{0:T(128)} %bitcast.4.date_ref, s32[104]{0:T(128)S(1)} %copy-done.1, s32[1]{0:T(128)S(6)} %copy.13.position_ref, s32[46]{0:T(128)S(1)} %copy-done.2, bf16[19136,128]{1,0:T(8,128)(2,1)} %bitcast.25), custom_call_target="tpu_custom_call" | custom-call | flops 1 | bytes 1 | tf_op jit(solution)/shard_map/pallas_call | solution.py:257
  5.4 0.0 collective-permute-done
  5.4 0.2 multiply_convert_fusion.1
  5.6 0.2 collective-permute-start.8
  5.8 1.2 %collective-permute-done.8 = f32[16,7,128]{2,1,0:T(8,128)S(1)} collective-permute-done((f32[16,7,128]{2,1,0:T(8,128)S(1)}, f32[16,7,128]{2,1,0:T(8,128)S(1)}, u32[]{:S(2)}, u32[]{:S(2)}) %collective-permute-start.8) | collective-permute-done | bytes 57376 | tf_op jit(solution)/shard_map/ppermute | solution.py:25
  6.9 3.1 %collective-permute-start.9 = (f32[8,7,128]{2,1,0:T(8,128)S(1)}, f32[8,7,128]{2,1,0:T(8,128)S(1)}, u32[]{:S(2)}, u32[]{:S(2)}) collective-permute-start(f32[8,7,128]{2,1,0:T(8,128)S(1)} %slice.37), channel_id=1, source_target_pairs={{0,128},{64,192},{128,0},{192,64},{1,129},{65,193},{129,1},{193,65... | collective-permute-start | bytes 86024 | tf_op jit(solution)/shard_map/ppermute | solution.py:29
  10.1 0.5 %collective-permute-start.2 = (f16[1472,128]{1,0:T(8,128)(2,1)S(1)}, f16[1472,128]{1,0:T(8,128)(2,1)S(1)}, u32[]{:S(2)}, u32[]{:S(2)}) collective-permute-start(f16[1472,128]{1,0:T(8,128)(2,1)S(1)} %multiply_convert_fusion.1), channel_id=1, source_target_pairs={{0,128},{64,192},{128,0},{192,64},{1,129},{65,193},{129,1},{193,65... | collective-permute-start | bytes 1130504 | tf_op jit(solution)/shard_map/ppermute | solution.py:29
  10.6 2.6 %shard_map.70 = (bf16[1472,128]{1,0:T(8,128)(2,1)S(1)}, bf16[1472,128]{1,0:T(8,128)(2,1)S(1)}, bf16[3312,128]{1,0:T(8,128)(2,1)S(1)}, bf16[3312,128]{1,0:T(8,128)(2,1)S(1)}) custom-call(s32[1]{0:T(128)} %bitcast.3.ens_ref, bf16[19136,128]{1,0:T(8,128)(2,1)} %bitcast.26), custom_call_target="tpu_custom_call" | custom-call | flops 1 | bytes 4898816 | tf_op jit(solution)/shard_map/pallas_call | solution.py:84
  13.1 0.1 collective-permute-start.1
  13.2 0.5 %collective-permute-start.4 = (bf16[3312,128]{1,0:T(8,128)(2,1)S(1)}, bf16[3312,128]{1,0:T(8,128)(2,1)S(1)}, u32[]{:S(2)}, u32[]{:S(2)}) collective-permute-start(bf16[3312,128]{1,0:T(8,128)(2,1)S(1)} %get-tuple-element.52), channel_id=1, source_target_pairs={{0,64},{64,0},{128,192},{192,128},{1,65},{65,1},{129,193},{193,129... | collective-permute-start | bytes 2543624 | tf_op jit(solution)/shard_map/ppermute | solution.py:25
  13.7 0.0 collective-permute-done.9
  13.7 0.0 copy-start
  13.8 0.0 collective-permute-done.5
  13.8 0.3 multiply_convert_fusion
  14.1 3.1 %collective-permute-start.6 = (f16[3312,128]{1,0:T(8,128)(2,1)S(1)}, f16[3312,128]{1,0:T(8,128)(2,1)S(1)}, u32[]{:S(2)}, u32[]{:S(2)}) collective-permute-start(f16[3312,128]{1,0:T(8,128)(2,1)S(1)} %multiply_convert_fusion), channel_id=1, source_target_pairs={{0,128},{64,192},{128,0},{192,64},{1,129},{65,193},{129,1},{193,65... | collective-permute-start | bytes 2543624 | tf_op jit(solution)/shard_map/ppermute | solution.py:29
  17.2 6.0 %collective-permute-done.2 = f16[1472,128]{1,0:T(8,128)(2,1)S(1)} collective-permute-done((f16[1472,128]{1,0:T(8,128)(2,1)S(1)}, f16[1472,128]{1,0:T(8,128)(2,1)S(1)}, u32[]{:S(2)}, u32[]{:S(2)}) %collective-permute-start.2) | collective-permute-done | bytes 376864 | tf_op jit(solution)/shard_map/ppermute | solution.py:29
  23.2 0.0 collective-permute-done.1
  23.2 0.2 multiply_add_fusion.1
  23.4 0.0 copy-done
  23.4 0.8 %shard_map.71.refs_5_ = f32[7,128]{1,0:T(8,128)S(1)} custom-call(s32[46]{0:T(128)S(1)} %copy-done.2, bf16[11,46,128]{2,1,0:T(8,128)(2,1)S(1)} %bitcast.22), custom_call_target="tpu_custom_call" | custom-call | flops 1 | bytes 1 | tf_op jit(solution)/shard_map/pallas_call | solution.py:290
  24.3 7.3 %collective-permute-start.10 = (f32[4,7,128]{2,1,0:T(8,128)S(1)}, f32[4,7,128]{2,1,0:T(8,128)S(1)}, u32[]{:S(2)}, u32[]{:S(2)}) collective-permute-start(f32[4,7,128]{2,1,0:T(8,128)S(1)} %dynamic-slice_bitcast_fusion), channel_id=1, source_target_pairs={{0,32},{8,40},{16,48},{24,56},{32,0},{40,8},{48,16},{56,24},{1,33}... | collective-permute-start | bytes 43016 | tf_op jit(solution)/shard_map/ppermute | solution.py:318
  31.6 1.7 %collective-permute-done.10 = f32[4,7,128]{2,1,0:T(8,128)S(1)} collective-permute-done((f32[4,7,128]{2,1,0:T(8,128)S(1)}, f32[4,7,128]{2,1,0:T(8,128)S(1)}, u32[]{:S(2)}, u32[]{:S(2)}) %collective-permute-start.10) | collective-permute-done | bytes 14368 | tf_op jit(solution)/shard_map/ppermute | solution.py:318
  33.3 2.0 %collective-permute-start.11 = (f32[2,7,128]{2,1,0:T(8,128)S(1)}, f32[2,7,128]{2,1,0:T(8,128)S(1)}, u32[]{:S(2)}, u32[]{:S(2)}) collective-permute-start(f32[2,7,128]{2,1,0:T(8,128)S(1)} %dynamic-slice_bitcast_fusion.1), channel_id=1, source_target_pairs={{0,16},{8,24},{16,0},{24,8},{32,48},{40,56},{48,32},{56,40},{1,17}... | collective-permute-start | bytes 21512 | tf_op jit(solution)/shard_map/ppermute | solution.py:318
  35.3 2.0 %collective-permute-start.3 = (f32[736,128]{1,0:T(8,128)S(1)}, f32[736,128]{1,0:T(8,128)S(1)}, u32[]{:S(2)}, u32[]{:S(2)}) collective-permute-start(f32[736,128]{1,0:T(8,128)S(1)} %get-tuple-element.49.refs_2_.refs_3_), channel_id=1, source_target_pairs={{0,8},{8,16},{16,24},{24,32},{32,40},{40,48},{48,56},{56,0},{1,9},... | collective-permute-start | bytes 1130504 | tf_op jit(solution)/shard_map/ppermute | solution.py:34
  37.3 2.1 %collective-permute-start.7 = (f32[736,128]{1,0:T(8,128)S(1)}, f32[736,128]{1,0:T(8,128)S(1)}, u32[]{:S(2)}, u32[]{:S(2)}) collective-permute-start(f32[736,128]{1,0:T(8,128)S(1)} %get-tuple-element.50.refs_0_.refs_1_), channel_id=1, source_target_pairs={{0,56},{8,0},{16,8},{24,16},{32,24},{40,32},{48,40},{56,48},{1,57}... | collective-permute-start | bytes 1130504 | tf_op jit(solution)/shard_map/ppermute | solution.py:34
  39.4 0.0 collective-permute-done.11
  39.4 0.9 %collective-permute-start.12 = (f32[1,7,128]{2,1,0:T(8,128)S(1)}, f32[1,7,128]{2,1,0:T(8,128)S(1)}, u32[]{:S(2)}, u32[]{:S(2)}) collective-permute-start(f32[1,7,128]{2,1,0:T(8,128)S(1)} %get-tuple-element.74), channel_id=1, source_target_pairs={{0,8},{8,0},{16,24},{24,16},{32,40},{40,32},{48,56},{56,48},{1,9},... | collective-permute-start | bytes 10760 | tf_op jit(solution)/shard_map/ppermute | solution.py:318
  40.3 0.0 collective-permute-done.4
  40.3 0.0 collective-permute-done.6
  40.3 0.3 multiply_add_fusion.refs_1_.refs_2_
  40.6 2.1 %shard_map.72.refs_8_ = f32[13,368,128]{2,1,0:T(8,128)} custom-call(s32[1]{0:T(128)} %bitcast.4.date_ref, s32[104]{0:T(128)S(1)} %copy-done.1, f32[736,128]{1,0:T(8,128)S(1)} %get-tuple-element.50.refs_0_.refs_1_, f32[3312,128]{1,0:T(8,128)S(1)} %multiply_add_fusion.refs_1_.refs_2_, f32[736,128]{1,0:T(8,128)S(1)} %get-tuple-element.49.refs_2_.refs_3_), custom_call_target="tpu_custom_call" | custom-call | flops 1 | bytes 10485760 | tf_op jit(solution)/shard_map/pallas_call | solution.py:171
  42.7 2.2 %collective-permute-done.12 = f32[1,7,128]{2,1,0:T(8,128)S(1)} collective-permute-done((f32[1,7,128]{2,1,0:T(8,128)S(1)}, f32[1,7,128]{2,1,0:T(8,128)S(1)}, u32[]{:S(2)}, u32[]{:S(2)}) %collective-permute-start.12) | collective-permute-done | bytes 3616 | tf_op jit(solution)/shard_map/ppermute | solution.py:318
  45.0 0.0 collective-permute-done.3.refs_0_
  45.0 0.0 collective-permute-done.7.refs_4_
  45.0 1.7 %shard_map.73 = (f32[13,368,128]{2,1,0:T(8,128)}, f32[7,1,128]{2,1,0:T(1,128)}) custom-call(s32[1]{0:T(128)} %bitcast.4.date_ref, s32[104]{0:T(128)S(1)} %copy-done.1, f32[736,128]{1,0:T(8,128)S(1)} %collective-permute-done.3.refs_0_, f32[736,128]{1,0:T(8,128)S(1)} %get-tuple-element.50.refs_0_.refs_1_, ...), custom_call_target="tpu_custom_call", output_to_operand_aliasing={{0}: (10, {})} | custom-call | flops 1 | bytes 1 | tf_op jit(solution)/shard_map/pallas_call | solution.py:171
  (8 shorter events, 0.0 us)
Async XLA Ops:
  0.6 3.9 %copy-start.1 = (s32[104]{0:T(128)S(1)}, s32[104]{0:T(128)}, u32[]{:S(2)}) copy-start(s32[104]{0:T(128)} %days_ref.5) | copy-start | bytes 1252
  0.7 3.9 %copy-start.2 = (s32[46]{0:T(128)S(1)}, s32[46]{0:T(128)}, u32[]{:S(2)}) copy-start(s32[46]{0:T(128)} %bins_ref.2) | copy-start | bytes 556
  3.2 2.2 %collective-permute-start = (bf16[1472,128]{1,0:T(8,128)(2,1)S(1)}, bf16[1472,128]{1,0:T(8,128)(2,1)S(1)}, u32[]{:S(2)}, u32[]{:S(2)}) collective-permute-start(bf16[1472,128]{1,0:T(8,128)(2,1)S(1)} %get-tuple-element.42), channel_id=1, source_target_pairs={{0,64},{64,0},{128,192},{192,128},{1,65},{65,1},{129,193},{193,129... | collective-permute-start | bytes 1130504 | tf_op jit(solution)/shard_map/ppermute | solution.py:25
  3.3 10.4 %collective-permute-start.5 = (bf16[3312,128]{1,0:T(8,128)(2,1)S(1)}, bf16[3312,128]{1,0:T(8,128)(2,1)S(1)}, u32[]{:S(2)}, u32[]{:S(2)}) collective-permute-start(bf16[3312,128]{1,0:T(8,128)(2,1)S(1)} %get-tuple-element.54), channel_id=1, source_target_pairs={{0,64},{64,0},{128,192},{192,128},{1,65},{65,1},{129,193},{193,129... | collective-permute-start | bytes 2543624 | tf_op jit(solution)/shard_map/ppermute | solution.py:25
  5.6 1.3 %collective-permute-start.8 = (f32[16,7,128]{2,1,0:T(8,128)S(1)}, f32[16,7,128]{2,1,0:T(8,128)S(1)}, u32[]{:S(2)}, u32[]{:S(2)}) collective-permute-start(f32[16,7,128]{2,1,0:T(8,128)S(1)} %get-tuple-element.56), channel_id=1, source_target_pairs={{0,64},{64,0},{128,192},{192,128},{1,65},{65,1},{129,193},{193,129... | collective-permute-start | bytes 172040 | tf_op jit(solution)/shard_map/ppermute | solution.py:25
  6.9 6.8 %collective-permute-start.9 = (f32[8,7,128]{2,1,0:T(8,128)S(1)}, f32[8,7,128]{2,1,0:T(8,128)S(1)}, u32[]{:S(2)}, u32[]{:S(2)}) collective-permute-start(f32[8,7,128]{2,1,0:T(8,128)S(1)} %slice.37), channel_id=1, source_target_pairs={{0,128},{64,192},{128,0},{192,64},{1,129},{65,193},{129,1},{193,65... | collective-permute-start | bytes 86024 | tf_op jit(solution)/shard_map/ppermute | solution.py:29
  10.1 13.2 %collective-permute-start.2 = (f16[1472,128]{1,0:T(8,128)(2,1)S(1)}, f16[1472,128]{1,0:T(8,128)(2,1)S(1)}, u32[]{:S(2)}, u32[]{:S(2)}) collective-permute-start(f16[1472,128]{1,0:T(8,128)(2,1)S(1)} %multiply_convert_fusion.1), channel_id=1, source_target_pairs={{0,128},{64,192},{128,0},{192,64},{1,129},{65,193},{129,1},{193,65... | collective-permute-start | bytes 1130504 | tf_op jit(solution)/shard_map/ppermute | solution.py:29
  13.1 10.1 %collective-permute-start.1 = (bf16[1472,128]{1,0:T(8,128)(2,1)S(1)}, bf16[1472,128]{1,0:T(8,128)(2,1)S(1)}, u32[]{:S(2)}, u32[]{:S(2)}) collective-permute-start(bf16[1472,128]{1,0:T(8,128)(2,1)S(1)} %get-tuple-element.48), channel_id=1, source_target_pairs={{0,64},{64,0},{128,192},{192,128},{1,65},{65,1},{129,193},{193,129... | collective-permute-start | bytes 1130504 | tf_op jit(solution)/shard_map/ppermute | solution.py:25
  13.2 27.0 %collective-permute-start.4 = (bf16[3312,128]{1,0:T(8,128)(2,1)S(1)}, bf16[3312,128]{1,0:T(8,128)(2,1)S(1)}, u32[]{:S(2)}, u32[]{:S(2)}) collective-permute-start(bf16[3312,128]{1,0:T(8,128)(2,1)S(1)} %get-tuple-element.52), channel_id=1, source_target_pairs={{0,64},{64,0},{128,192},{192,128},{1,65},{65,1},{129,193},{193,129... | collective-permute-start | bytes 2543624 | tf_op jit(solution)/shard_map/ppermute | solution.py:25
  13.7 9.7 %copy-start = (bf16[11,1,46,128]{3,2,1,0:T(8,128)(2,1)S(1)}, bf16[11,1,46,128]{3,2,1,0:T(8,128)(2,1)}, u32[]{:S(2)}) copy-start(bf16[11,1,46,128]{3,2,1,0:T(8,128)(2,1)} %param.9) | copy-start | bytes 388612
  14.1 26.2 %collective-permute-start.6 = (f16[3312,128]{1,0:T(8,128)(2,1)S(1)}, f16[3312,128]{1,0:T(8,128)(2,1)S(1)}, u32[]{:S(2)}, u32[]{:S(2)}) collective-permute-start(f16[3312,128]{1,0:T(8,128)(2,1)S(1)} %multiply_convert_fusion), channel_id=1, source_target_pairs={{0,128},{64,192},{128,0},{192,64},{1,129},{65,193},{129,1},{193,65... | collective-permute-start | bytes 2543624 | tf_op jit(solution)/shard_map/ppermute | solution.py:29
  24.3 9.0 %collective-permute-start.10 = (f32[4,7,128]{2,1,0:T(8,128)S(1)}, f32[4,7,128]{2,1,0:T(8,128)S(1)}, u32[]{:S(2)}, u32[]{:S(2)}) collective-permute-start(f32[4,7,128]{2,1,0:T(8,128)S(1)} %dynamic-slice_bitcast_fusion), channel_id=1, source_target_pairs={{0,32},{8,40},{16,48},{24,56},{32,0},{40,8},{48,16},{56,24},{1,33}... | collective-permute-start | bytes 43016 | tf_op jit(solution)/shard_map/ppermute | solution.py:318
  33.3 6.1 %collective-permute-start.11 = (f32[2,7,128]{2,1,0:T(8,128)S(1)}, f32[2,7,128]{2,1,0:T(8,128)S(1)}, u32[]{:S(2)}, u32[]{:S(2)}) collective-permute-start(f32[2,7,128]{2,1,0:T(8,128)S(1)} %dynamic-slice_bitcast_fusion.1), channel_id=1, source_target_pairs={{0,16},{8,24},{16,0},{24,8},{32,48},{40,56},{48,32},{56,40},{1,17}... | collective-permute-start | bytes 21512 | tf_op jit(solution)/shard_map/ppermute | solution.py:318
  35.3 9.6 %collective-permute-start.3 = (f32[736,128]{1,0:T(8,128)S(1)}, f32[736,128]{1,0:T(8,128)S(1)}, u32[]{:S(2)}, u32[]{:S(2)}) collective-permute-start(f32[736,128]{1,0:T(8,128)S(1)} %get-tuple-element.49.refs_2_.refs_3_), channel_id=1, source_target_pairs={{0,8},{8,16},{16,24},{24,32},{32,40},{40,48},{48,56},{56,0},{1,9},... | collective-permute-start | bytes 1130504 | tf_op jit(solution)/shard_map/ppermute | solution.py:34
  37.3 7.7 %collective-permute-start.7 = (f32[736,128]{1,0:T(8,128)S(1)}, f32[736,128]{1,0:T(8,128)S(1)}, u32[]{:S(2)}, u32[]{:S(2)}) collective-permute-start(f32[736,128]{1,0:T(8,128)S(1)} %get-tuple-element.50.refs_0_.refs_1_), channel_id=1, source_target_pairs={{0,56},{8,0},{16,8},{24,16},{32,24},{40,32},{48,40},{56,48},{1,57}... | collective-permute-start | bytes 1130504 | tf_op jit(solution)/shard_map/ppermute | solution.py:34
  39.4 5.6 %collective-permute-start.12 = (f32[1,7,128]{2,1,0:T(8,128)S(1)}, f32[1,7,128]{2,1,0:T(8,128)S(1)}, u32[]{:S(2)}, u32[]{:S(2)}) collective-permute-start(f32[1,7,128]{2,1,0:T(8,128)S(1)} %get-tuple-element.74), channel_id=1, source_target_pairs={{0,8},{8,0},{16,24},{24,16},{32,40},{40,32},{48,56},{56,48},{1,9},... | collective-permute-start | bytes 10760 | tf_op jit(solution)/shard_map/ppermute | solution.py:318
